TPU v7x, 128 devices: a whole 4x4x4 slice. The times are simulated.
128 devices in a mesh: rep: 4 (over x_lo, core), fsdp: 32 (over z, x_hi, y).
Axes of the slice: x: 4 (x_hi: 2, x_lo: 2; x = x_hi * 2 + x_lo), y: 4, z: 4, core: 2. Of those that a mesh axis runs over, the one named last changes fastest.
Arguments:
- inputs: bfloat16 [4, 4096, 1792], P('rep', 'fsdp'), may hold values from -6 to 6
- cotangent: bfloat16 [4, 4096, 1792], P('rep', 'fsdp'), may hold values from -18 to 18
- up_weight: bfloat16 [4, 14336, 1792], P('rep', 'fsdp'), may hold values from -6 to 6
- down_weight: bfloat16 [4, 14336, 1792], P('rep', 'fsdp'), may hold values from -6 to 6
- momentum_up: bfloat16 [4, 14336, 1792], P('rep', 'fsdp'), may hold values from -4.1875 to 4.1875
- momentum_down: bfloat16 [4, 14336, 1792], P('rep', 'fsdp'), may hold values from -4.1875 to 4.1875
- variance_up: bfloat16 [4, 14336, 1792], P('rep', 'fsdp'), may hold values from 0.25 to 4
- variance_down: bfloat16 [4, 14336, 1792], P('rep', 'fsdp'), may hold values from 0.25 to 4
- step_index: int32 [1], replicated, may hold values from 1 to 16
Outputs:
- mixed_up: bfloat16 [4, 14336, 1792], P('rep', 'fsdp')
- mixed_down: bfloat16 [4, 14336, 1792], P('rep', 'fsdp')
- moment_up: bfloat16 [4, 14336, 1792], P('rep', 'fsdp')
- moment_down: bfloat16 [4, 14336, 1792], P('rep', 'fsdp')
- squares_up: bfloat16 [4, 14336, 1792], P('rep', 'fsdp')
- squares_down: bfloat16 [4, 14336, 1792], P('rep', 'fsdp')
All inputs are finite; a program needn't handle non-finite values.
Results may differ from a plain program's by a relative error of at most 0.0052.
Values may be sent and summed in bfloat16 or wider, within the bound.
No kernel may reach another device: no remote copies, remote signals or barrier semaphores. Data moves between devices by JAX's collectives and lax.ppermute only.
A program may use at most 128 MiB of HBM per device.

v0:
```python
import functools
import math

import jax
import jax.numpy as jnp
from jax import lax
from jax.experimental import pallas as pl
from jax.experimental.pallas import tpu as pltpu
from jax.sharding import PartitionSpec as P

D = 1792
FF = 14336

beta_one = 0.9
beta_two = 0.95
learn_rate = 0.05
adam_eps = 1e-08
norm_eps = 1e-06
root_coef = math.sqrt(2.0 / math.pi)
up_scale = 1.0 / math.sqrt(D)
down_scale = 1.0 / math.sqrt(FF)

ROWS = 128
HELD = 448
SHARED = 2 * HELD
TOKENS = 2048
CHUNKS = ((0, 128),) + tuple((256 * k, 256) for k in range(1, 7)) + ((128, 128),)
MIXING = 7
EARLY = 1536
NZ, NX, NY = 4, 2, 4


def moved(block, place):
    route = []
    for z in range(NZ):
        for x in range(NX):
            for y in range(NY):
                a, b, c = place(z, x, y)
                route.append(((z * NX + x) * NY + y, (a % NZ * NX + b) * NY + c))
    return lax.ppermute(block, "fsdp", route)


def z_up(z, x, y):
    return z + 1, x, y


def z_down(z, x, y):
    return z - 1, x, y


def z_over(z, x, y):
    return z + 2, x, y


def x_other(z, x, y):
    return z, 1 - x, y


def y_same_half(z, x, y):
    return z, x, 3 - y


def diagonal(z, x, y):
    return z, 1 - x, 3 - y


def y_sharing(z, x, y):
    return z, x, y ^ 1


def gelu_pair(pre):
    square = pre * pre
    tangent = jnp.tanh(pre * (root_coef + (root_coef * 0.044715) * square))
    half = 0.5 * tangent + 0.5
    value = pre * half
    slope = half + pre * (0.5 - 0.5 * tangent * tangent) * (
        root_coef + (3.0 * 0.044715 * root_coef) * square
    )
    return (value, slope)


def normalize(rows):
    wide = rows.astype(jnp.float32)
    factor = lax.rsqrt(jnp.mean(wide * wide, axis=-1, keepdims=True) + norm_eps)
    return (wide * factor).astype(jnp.bfloat16)


contract_last = (((1,), (1,)), ((), ()))
ANY = pl.BlockSpec(memory_space=pl.ANY)
INSIDE = pl.BlockSpec(memory_space=pltpu.VMEM)


def vmem(mebibytes):
    return pltpu.CompilerParams(vmem_limit_bytes=mebibytes * 1024 * 1024)


def cost(flops, moved_bytes):
    return pl.CostEstimate(flops=2 * flops, bytes_accessed=moved_bytes, transcendentals=0)


def prepare_kernel(inputs, cotangent, a_ref, b_ref, held, sem):
    half = ROWS // 2
    loads = [
        pltpu.make_async_copy(inputs, held, sem.at[0]),
        pltpu.make_async_copy(cotangent.at[pl.ds(0, half)], a_ref.at[1], sem.at[1]),
        pltpu.make_async_copy(cotangent.at[pl.ds(half, half)], b_ref.at[1], sem.at[2]),
    ]
    for load in loads:
        load.start()
    loads[0].wait()
    a_ref[0] = normalize(held[:half])
    b_ref[0] = normalize(held[half:])
    for load in loads[1:]:
        load.wait()


def prepare(inputs, cotangent):
    half = jax.ShapeDtypeStruct((2, ROWS // 2, D), jnp.bfloat16)
    return pl.pallas_call(
        prepare_kernel,
        out_shape=[half, half],
        in_specs=[ANY] * 2,
        out_specs=[INSIDE] * 2,
        scratch_shapes=[pltpu.VMEM((ROWS, D), jnp.bfloat16), pltpu.SemaphoreType.DMA((3,))],
        compiler_params=vmem(16),
        cost_estimate=cost(0, 8 * ROWS * D),
    )(inputs, cotangent)


def stack_kernel(up, down, out, held, load_sem, store_sem):
    parts = 2
    rows = HELD // parts
    loads, stores = [], []
    for which, ref in enumerate((up, down)):
        for part in range(parts):
            k, at = which * parts + part, pl.ds(part * rows, rows)
            place = held.at[which, at]
            loads.append(pltpu.make_async_copy(ref.at[at], place, load_sem.at[k]))
            stores.append(pltpu.make_async_copy(place, out.at[which, at], store_sem.at[k]))
    for load in loads:
        load.start()
    for load, store in zip(loads, stores):
        load.wait()
        store.start()
    for store in stores:
        store.wait()


def stack_weights(up, down):
    shape = (2, HELD, D)
    return pl.pallas_call(
        stack_kernel,
        out_shape=jax.ShapeDtypeStruct(shape, jnp.bfloat16),
        in_specs=[ANY] * 2,
        out_specs=ANY,
        scratch_shapes=[pltpu.VMEM(shape, jnp.bfloat16)] + [pltpu.SemaphoreType.DMA((4,))] * 2,
        compiler_params=vmem(16),
        cost_estimate=cost(0, 8 * HELD * D),
    )(up, down)


def join_kernel(count, *refs):
    first = 0
    for ref in refs[:count]:
        rows = ref.shape[1]
        refs[-1][:, first : first + rows] = ref[...]
        first += rows


def join(pieces, after):
    rows = sum(p.shape[1] for p in pieces)
    return pl.pallas_call(
        functools.partial(join_kernel, len(pieces)),
        out_shape=jax.ShapeDtypeStruct((2, rows, D), jnp.bfloat16),
        in_specs=[INSIDE] * len(pieces) + [ANY] * len(after),
        out_specs=INSIDE,
        compiler_params=vmem(16),
        cost_estimate=cost(0, 8 * rows * D),
    )(*pieces, *after)


def cut_kernel(firsts, count_in, *refs):
    sem = refs[-1]
    loads = []
    for k, first in enumerate(firsts):
        out = refs[count_in + k]
        source = refs[k].at[:, pl.ds(first, out.shape[1])]
        loads.append(pltpu.make_async_copy(source, out, sem.at[k]))
        loads[-1].start()
    for load in loads:
        load.wait()


def cut(blocks, firsts, rows, after):
    out = jax.ShapeDtypeStruct((2, rows, D), jnp.bfloat16)
    operands = list(blocks) + list(after)
    return pl.pallas_call(
        functools.partial(cut_kernel, firsts, len(operands)),
        out_shape=[out] * len(blocks),
        in_specs=[ANY] * len(operands),
        out_specs=[INSIDE] * len(blocks),
        scratch_shapes=[pltpu.SemaphoreType.DMA((len(blocks),))],
        compiler_params=vmem(16),
        cost_estimate=cost(0, 8 * rows * D * len(blocks)),
    )(*operands)


def hidden_kernel(jobs, sizes, pieces, skipped, kept, tile, both, *refs):
    arrays = refs[: len(pieces)]
    blocks = refs[len(pieces) : len(pieces) + len(sizes)]
    refs = refs[len(pieces) + len(sizes) + skipped :]
    weights, tokens, pair, weight_sem, token_sem, out_sem, keep_sem = refs[-7:]
    top, total = weights.shape[1], tokens.shape[1]
    loads = []
    for k, (ref, (which, first, rows)) in enumerate(zip(arrays, pieces)):
        target = weights.at[:, pl.ds(first, rows)]
        if which is not None:
            target = weights.at[which, pl.ds(first, rows)]
        loads.append(pltpu.make_async_copy(ref, target, weight_sem.at[k]))
    first = 0
    for k, (ref, count) in enumerate(zip(blocks, sizes)):
        loads.append(pltpu.make_async_copy(ref, tokens.at[:, pl.ds(first, count)], token_sem.at[k]))
        first += count
    for load in loads:
        load.start()
    for load in loads:
        load.wait()
    stores = []
    if kept is not None:
        source = tokens.at[:, pl.ds(0, kept[1])]
        target = refs[2].at[:, pl.ds(kept[0], kept[1])]
        stores.append(pltpu.make_async_copy(source, target, keep_sem.at[0]))
        stores[-1].start()

    def step(i, carry):
        blocks = top // HELD
        here = i < blocks * both
        row = jnp.where(here, i % blocks, blocks - 1) * HELD
        token = jnp.where(here, i // blocks, i - (blocks - 1) * both) * tile
        rows = pl.ds(pl.multiple_of(row, HELD), HELD)
        at = pl.ds(pl.multiple_of(token, tile), tile)
        pre = up_scale * lax.dot_general(
            weights[0, rows], tokens[0, at], contract_last, preferred_element_type=jnp.float32
        )
        back = down_scale * lax.dot_general(
            weights[1, rows], tokens[1, at], contract_last, preferred_element_type=jnp.float32
        )
        value, slope = gelu_pair(pre)
        pair[0, rows, at] = (back * slope).astype(jnp.bfloat16)
        pair[1, rows, at] = value.astype(jnp.bfloat16)
        return carry

    lax.fori_loop(0, top // HELD * both + (total // tile - both), step, 0)
    for k, (shared, token, count, place) in enumerate(jobs):
        stores.append(
            pltpu.make_async_copy(
                pair.at[:, pl.ds(shared * HELD, HELD), pl.ds(token, count)],
                refs[shared].at[:, :, pl.ds(place, count)],
                out_sem.at[k],
            )
        )
        stores[-1].start()
    for store in stores:
        store.wait()


def hidden_step(jobs, pieces, arrays, blocks, results, kept, both, after=()):
    sizes = tuple(b.shape[1] for b in blocks)
    total = sum(sizes)
    top = max(first + rows for _, first, rows in pieces)
    shapes = ((2, HELD, EARLY), (2, HELD, TOKENS), (2, TOKENS, D))
    out = [jax.ShapeDtypeStruct(shape, jnp.bfloat16) for shape in shapes]
    operands = [*arrays, *blocks]
    aliases = {len(operands) + k: k for k in range(len(results))}
    operands += [*results, *after]
    flops = sum(4 * HELD * count * D for _, _, count, _ in jobs)
    skipped = len(results) + len(after)
    return pl.pallas_call(
        functools.partial(hidden_kernel, jobs, sizes, pieces, skipped, kept, 512, both),
        out_shape=out,
        in_specs=[ANY] * len(operands),
        out_specs=[ANY] * 3,
        input_output_aliases=aliases,
        scratch_shapes=[
            pltpu.VMEM((2, top, D), jnp.bfloat16),
            pltpu.VMEM((2, total, D), jnp.bfloat16),
            pltpu.VMEM((2, top, total), jnp.bfloat16),
            pltpu.SemaphoreType.DMA((len(pieces),)),
            pltpu.SemaphoreType.DMA((len(blocks),)),
            pltpu.SemaphoreType.DMA((len(jobs),)),
            pltpu.SemaphoreType.DMA((1,)),
        ],
        compiler_params=vmem(36 if len(jobs) > 1 else 24),
        cost_estimate=cost(flops, 4 * (total + top) * D + 4 * top * total),
    )(*operands)


def last_own_kernel(up, down, tokens_in, *refs):
    pair, weights, tokens, sem = refs[-4:]
    loads = [
        pltpu.make_async_copy(up, weights.at[0], sem.at[0]),
        pltpu.make_async_copy(down, weights.at[1], sem.at[1]),
        pltpu.make_async_copy(tokens_in.at[:, pl.ds(EARLY, TOKENS - EARLY)], tokens, sem.at[2]),
    ]
    for load in loads:
        load.start()
    for load in loads:
        load.wait()
    tile = 256

    def step(i, carry):
        at = pl.ds(pl.multiple_of(i * tile, tile), tile)
        pre = up_scale * lax.dot_general(
            weights[0], tokens[0, at], contract_last, preferred_element_type=jnp.float32
        )
        back = down_scale * lax.dot_general(
            weights[1], tokens[1, at], contract_last, preferred_element_type=jnp.float32
        )
        value, slope = gelu_pair(pre)
        pair[0, :, at] = (back * slope).astype(jnp.bfloat16)
        pair[1, :, at] = value.astype(jnp.bfloat16)
        return carry

    lax.fori_loop(0, (TOKENS - EARLY) // tile, step, 0)


def last_own(up, down, tokens, after):
    out = jax.ShapeDtypeStruct((2, HELD, TOKENS - EARLY), jnp.bfloat16)
    return pl.pallas_call(
        last_own_kernel,
        out_shape=out,
        in_specs=[ANY] * (3 + len(after)),
        out_specs=INSIDE,
        scratch_shapes=[
            pltpu.VMEM((2, HELD, D), jnp.bfloat16),
            pltpu.VMEM((2, TOKENS - EARLY, D), jnp.bfloat16),
            pltpu.SemaphoreType.DMA((3,)),
        ],
        compiler_params=vmem(22),
        cost_estimate=cost(4 * HELD * (TOKENS - EARLY) * D, 4 * (HELD + TOKENS - EARLY) * D),
    )(up, down, tokens, *after)


def last_shared_kernel(*refs):
    weights_in, blocks = refs[0], refs[1:5]
    pair_in, tokens_in, pair_out, tokens_out, chunk = refs[5:10]
    weights, tokens, pair, columns, sem, out_sem = refs[10:]
    first, width = CHUNKS[0]
    rest = TOKENS - EARLY
    loads = [pltpu.make_async_copy(weights_in, weights, sem.at[0])]
    row = 0
    for k, ref in enumerate(blocks):
        rows = ref.shape[1]
        loads.append(pltpu.make_async_copy(ref, tokens.at[:, pl.ds(row, rows)], sem.at[1 + k]))
        row += rows
    early, late = pl.ds(0, EARLY), pl.ds(EARLY, rest)
    source = tokens_in.at[:, early, pl.ds(first, width)]
    more = [
        pltpu.make_async_copy(pair_in.at[:, :, early], pair.at[:, :, early], sem.at[5]),
        pltpu.make_async_copy(source, columns, sem.at[6]),
    ]
    for load in loads + more:
        load.start()
    for load in loads:
        load.wait()
    stores = [pltpu.make_async_copy(tokens, tokens_out.at[:, late], out_sem.at[0])]
    stores[0].start()
    tile = 256

    def step(i, carry):
        at = pl.ds(pl.multiple_of(i * tile, tile), tile)
        to = pl.ds(pl.multiple_of(EARLY + i * tile, tile), tile)
        pre = up_scale * lax.dot_general(
            weights[0], tokens[0, at], contract_last, preferred_element_type=jnp.float32
        )
        back = down_scale * lax.dot_general(
            weights[1], tokens[1, at], contract_last, preferred_element_type=jnp.float32
        )
        value, slope = gelu_pair(pre)
        pair[0, :, to] = (back * slope).astype(jnp.bfloat16)
        pair[1, :, to] = value.astype(jnp.bfloat16)
        return carry

    lax.fori_loop(0, rest // tile, step, 0)
    stores.append(pltpu.make_async_copy(pair.at[:, :, late], pair_out.at[:, :, late], out_sem.at[1]))
    stores[1].start()
    for load in more:
        load.wait()
    for which, scale in enumerate((up_scale, down_scale)):
        grad = jnp.dot(pair[which, :, :EARLY], columns[which], preferred_element_type=jnp.float32)
        grad += jnp.dot(
            pair[which, :, EARLY:],
            tokens[which, :, first : first + width],
            preferred_element_type=jnp.float32,
        )
        chunk[which] = (scale * grad).astype(jnp.bfloat16)
    for store in stores:
        store.wait()


def last_shared(weights, blocks, pair, tokens):
    width = CHUNKS[0][1]
    return pl.pallas_call(
        last_shared_kernel,
        out_shape=[
            jax.ShapeDtypeStruct((2, HELD, TOKENS), jnp.bfloat16),
            jax.ShapeDtypeStruct((2, TOKENS, D), jnp.bfloat16),
            jax.ShapeDtypeStruct((2, HELD, width), jnp.bfloat16),
        ],
        in_specs=[ANY] * 7,
        out_specs=[ANY] * 2 + [INSIDE],
        input_output_aliases={5: 0, 6: 1},
        scratch_shapes=[
            pltpu.VMEM((2, HELD, D), jnp.bfloat16),
            pltpu.VMEM((2, TOKENS - EARLY, D), jnp.bfloat16),
            pltpu.VMEM((2, HELD, TOKENS), jnp.bfloat16),
            pltpu.VMEM((2, EARLY, width), jnp.bfloat16),
            pltpu.SemaphoreType.DMA((7,)),
            pltpu.SemaphoreType.DMA((2,)),
        ],
        compiler_params=vmem(22),
        cost_estimate=cost(
            4 * HELD * ((TOKENS - EARLY) * D + TOKENS * width), 4 * (HELD + TOKENS - EARLY) * D
        ),
    )(weights, *blocks, pair, tokens)


def column_spec(c):
    first, width = CHUNKS[c]
    return pl.BlockSpec((HELD, width), lambda j: (0, first // width))


def token_spec(c):
    first, width = CHUNKS[c]
    return pl.BlockSpec((2, TOKENS, width), lambda j: (0, 0, first // width))


def pair_spec(c):
    return pl.BlockSpec((2, HELD, CHUNKS[c][1]), lambda j: (0, 0, 0))


def rows_spec(tokens):
    return pl.BlockSpec((2, HELD, tokens), lambda j: (0, 0, 0))


def theirs_kernel(pair, tokens, *refs):
    def step(which, carry):
        scale = jnp.where(which == 0, up_scale, down_scale)
        grad = jnp.dot(pair[which], tokens[which], preferred_element_type=jnp.float32)
        refs[-1][which] = (scale * grad).astype(jnp.bfloat16)
        return carry

    lax.fori_loop(0, 2, step, 0)


def theirs_chunk(c, pair, tokens, after):
    width = CHUNKS[c][1]
    return pl.pallas_call(
        theirs_kernel,
        out_shape=jax.ShapeDtypeStruct((2, HELD, width), jnp.bfloat16),
        grid=(1,),
        in_specs=[rows_spec(TOKENS), token_spec(c)] + [ANY] * len(after),
        out_specs=pair_spec(c),
        compiler_params=vmem(22),
        cost_estimate=cost(4 * HELD * TOKENS * width, 4 * TOKENS * (HELD + width)),
    )(pair, tokens, *after)


def adam_kernel(mixing, *refs):
    pair, pair_last, tokens, bias, arrived = refs[:5]
    state = refs[5:11]
    outs = refs[-8:-1]
    grads = refs[-1]

    def multiply(which, carry):
        scale = jnp.where(which == 0, up_scale, down_scale)
        early = jnp.dot(pair[which], tokens[which, :EARLY], preferred_element_type=jnp.float32)
        late = jnp.dot(pair_last[which], tokens[which, EARLY:], preferred_element_type=jnp.float32)
        grads[which] = scale * (early + late)
        return carry

    lax.fori_loop(0, 2, multiply, 0)
    tile = 32

    def step(i, carry):
        at = pl.ds(pl.multiple_of(i * tile, tile), tile)
        for which in (0, 1):
            weight, first, second = (ref[at] for ref in state[3 * which : 3 * which + 3])
            grad = grads[which, at] + arrived[which, at].astype(jnp.float32)
            first_new = beta_one * first.astype(jnp.float32) + (1.0 - beta_one) * grad
            second_new = beta_two * second.astype(jnp.float32) + (1.0 - beta_two) * grad * grad
            update = (learn_rate * bias[0]) * first_new / (jnp.sqrt(second_new * bias[1]) + adam_eps)
            outs[0][which, at] = (weight.astype(jnp.float32) - update).astype(jnp.bfloat16)
            outs[1 + 2 * which][at] = first_new.astype(jnp.bfloat16)
            outs[2 + 2 * which][at] = second_new.astype(jnp.bfloat16)
        return carry

    lax.fori_loop(0, HELD // tile, step, 0)
    if mixing:
        mix_kernel(refs[11], refs[12], *outs[-2:])


def mix_kernel(own, other, *refs):
    tile = 32

    def step(i, carry):
        at = pl.ds(pl.multiple_of(i * tile, tile), tile)
        for which in (0, 1):
            both = own[which, at].astype(jnp.float32) + other[which, at].astype(jnp.float32)
            refs[which - 2][at] = (both * 0.5).astype(jnp.bfloat16)
        return carry

    lax.fori_loop(0, HELD // tile, step, 0)


whole = jax.ShapeDtypeStruct((HELD, D), jnp.bfloat16)


def adam_chunk(c, sides, tokens, bias, arrived, state, mixed, results):
    width = CHUNKS[c][1]
    operands = [*sides, tokens, bias, arrived, *state, *mixed]
    aliases = {len(operands) + k: 1 + k for k in range(len(results))}
    before = max(c - 2, 0)
    mixing = [column_spec(before)] * 2 if mixed or not results else []
    early, last = rows_spec(EARLY), rows_spec(TOKENS - EARLY)
    smem = pl.BlockSpec(memory_space=pltpu.SMEM)
    return pl.pallas_call(
        functools.partial(adam_kernel, bool(mixed)),
        out_shape=[jax.ShapeDtypeStruct((2, HELD, width), jnp.bfloat16)] + [whole] * 6,
        grid=(1,),
        in_specs=[early, last, token_spec(c), smem, pair_spec(c)]
        + [column_spec(c)] * 6
        + [pair_spec(before)] * len(mixed)
        + [ANY] * len(results),
        out_specs=[pair_spec(c)] + [column_spec(c)] * 4 + (mixing or [ANY] * 2),
        input_output_aliases=aliases,
        scratch_shapes=[pltpu.VMEM((2, HELD, width), jnp.float32)],
        compiler_params=vmem(22),
        cost_estimate=cost(4 * HELD * TOKENS * width, 4 * TOKENS * (HELD + width) + 36 * HELD * width),
    )(*operands, *results)


def mix_chunk(c, own, other, results):
    return pl.pallas_call(
        mix_kernel,
        out_shape=[whole] * 2,
        grid=(1,),
        in_specs=[pair_spec(c)] * 2 + [ANY] * 2,
        out_specs=[column_spec(c)] * 2,
        input_output_aliases={2: 0, 3: 1},
        compiler_params=vmem(22),
        cost_estimate=cost(0, 12 * HELD * CHUNKS[c][1]),
    )(own, other, *results)


def on_device(
    inputs,
    cotangent,
    up_weight,
    down_weight,
    momentum_up,
    momentum_down,
    variance_up,
    variance_down,
    step_index,
):
    up, down = up_weight[0], down_weight[0]
    half = ROWS // 2

    weights_sent = moved(stack_weights(up, down), y_sharing)
    a, b = prepare(inputs[0], cotangent[0])
    a_x, a_y = moved(a, x_other), moved(a, y_same_half)
    b_up, b_down = moved(b, z_up), moved(b, z_down)
    quarter = half // 2
    a_far = [moved(a_x[:, :quarter], y_same_half), moved(a_y[:, quarter:], x_other)]
    b_far = [moved(b_up[:, :quarter], z_up), moved(b_down[:, quarter:], z_down)]
    a_all = join([a, a_x, a_y, *a_far], [])
    b_all = join([b, b_up, b_down, *b_far], [])

    a_up, a_down = moved(a_all, z_up), moved(a_all, z_down)
    b_x, b_y = moved(b_all, x_other), moved(b_all, y_same_half)
    held = ((0, 0, HELD), (1, 0, HELD))
    job = (0, 0, 512, 0)
    results = hidden_step((job,), held, [up, down], [a_all, b_all], (), (0, 512), 1)

    mid = 2 * half
    halves = cut([a_up, a_down, b_x, b_y], (0, mid, 0, mid), mid, [results[0]])
    last = [
        moved(halves[0], z_up),
        moved(halves[1], z_down),
        moved(halves[2], y_same_half),
        moved(halves[3], x_other),
    ]
    results = hidden_step(
        ((0, 0, 1024, 512), (1, 0, 1024, 512), (1, 1024, 512, 0)),
        held + ((None, HELD, HELD),),
        [up, down, weights_sent],
        [a_up, a_down, b_x, b_y, a_all, b_all],
        results,
        (512, 1024),
        2,
        halves[:1],
    )
    own_pair = results[0]
    pair, tokens, theirs = last_shared(weights_sent, last, *results[1:])

    count = step_index[0].astype(jnp.float32)
    bias_one = 1.0 - jnp.exp(count * math.log(beta_one))
    bias_two = 1.0 - jnp.exp(count * math.log(beta_two))
    bias = jnp.stack([1.0 / bias_one, 1.0 / bias_two])
    state = [up, momentum_up[0], variance_up[0], down, momentum_down[0], variance_down[0]]

    def finish(hop):
        route = [(g, (g + hop) % 4) for g in range(4)]
        news, updated, others = (), [], []
        second = theirs_chunk(1, pair, tokens, [])
        third = theirs_chunk(2, pair, tokens, [second])
        sent = [moved(t, y_sharing) for t in (theirs, second, third)]
        sides = [own_pair, last_own(up, down, tokens, [third])]
        for c in range(len(CHUNKS)):
            mixed = [updated[c - 2], others[c - 2]] if 2 <= c < MIXING else []
            out = adam_chunk(c, sides, tokens, bias, sent[c], state, mixed, news)
            updated.append(out[0])
            news = out[1:]
            others.append(lax.ppermute(out[0], "rep", route))
            if 3 <= c + 2 < len(CHUNKS):
                more = theirs_chunk(c + 2, pair, tokens, [out[0]])
                sent.append(moved(more, y_sharing))
        mixed = news[4:]
        for c in range(MIXING - 2, len(CHUNKS)):
            mixed = mix_chunk(c, updated[c], others[c], mixed)
        return mixed[0], mixed[1], news[0], news[2], news[1], news[3]

    outs = lax.cond(step_index[0] % 2 == 0, lambda: finish(1), lambda: finish(2))
    return tuple(o[None] for o in outs)


def solution(mesh):
    shard = P("rep", "fsdp", None)
    return jax.shard_map(
        on_device,
        mesh=mesh,
        in_specs=(shard,) * 8 + (P(),),
        out_specs=(shard,) * 6,
        check_vma=False,
    )
```

profile of v0, /device:TPU:0, one launch (start us, length us, event | category | flops | bytes accessed | tf_op | source)
XLA Modules:
  0.0 212.9 jit_solution(14046964274430033523)
XLA Ops:
  0.7 3.0 %shard_map.136 = bf16[2,448,1792]{2,1,0:T(8,128)(2,1)} custom-call(bf16[448,1792]{1,0:T(8,128)(2,1)} %bitcast.23, bf16[448,1792]{1,0:T(8,128)(2,1)} %bitcast.28), custom_call_target="tpu_custom_call" | custom-call | bytes 6422528 | tf_op jit(solution)/shard_map/pallas_call | solution.py:151
  6.5 3.1 %collective-permute-start.33 = (bf16[2,64,1792]{2,1,0:T(8,128)(2,1)S(1)}, bf16[2,64,1792]{2,1,0:T(8,128)(2,1)S(1)}, u32[]{:S(2)}, u32[]{:S(2)}) collective-permute-start(bf16[2,64,1792]{2,1,0:T(8,128)(2,1)S(1)} %get-tuple-element.217.refs_0_), channel_id=1, source_target_pairs={{0,4},{1,5},{2,6},{3,7},{4,0},{5,1},{6,2},{7,3},{8,12},{9,13},{10,... | collective-permute-start | bytes 1376264 | tf_op jit(solution)/shard_map/ppermute | solution.py:40
  9.6 2.2 %collective-permute-start.34 = (bf16[2,64,1792]{2,1,0:T(8,128)(2,1)S(1)}, bf16[2,64,1792]{2,1,0:T(8,128)(2,1)S(1)}, u32[]{:S(2)}, u32[]{:S(2)}) collective-permute-start(bf16[2,64,1792]{2,1,0:T(8,128)(2,1)S(1)} %get-tuple-element.217.refs_0_), channel_id=1, source_target_pairs={{0,3},{1,2},{2,1},{3,0},{4,7},{5,6},{6,5},{7,4},{8,11},{9,10},{10,... | collective-permute-start | bytes 1376264 | tf_op jit(solution)/shard_map/ppermute | solution.py:40
  15.8 4.2 %collective-permute-done.33.refs_1_ = bf16[2,64,1792]{2,1,0:T(8,128)(2,1)S(1)} collective-permute-done((bf16[2,64,1792]{2,1,0:T(8,128)(2,1)S(1)}, bf16[2,64,1792]{2,1,0:T(8,128)(2,1)S(1)}, u32[]{:S(2)}, u32[]{:S(2)}) %collective-permute-start.33) | collective-permute-done | bytes 458784 | tf_op jit(solution)/shard_map/ppermute | solution.py:40
  20.0 2.3 %collective-permute-start.35 = (bf16[2,32,1792]{2,1,0:T(8,128)(2,1)S(1)}, bf16[2,32,1792]{2,1,0:T(8,128)(2,1)S(1)}, u32[]{:S(2)}, u32[]{:S(2)}) collective-permute-start(bf16[2,32,1792]{2,1,0:T(8,128)(2,1)S(1)} %slice.16), channel_id=1, source_target_pairs={{0,3},{1,2},{2,1},{3,0},{4,7},{5,6},{6,5},{7,4},{8,11},{9,10},{10,... | collective-permute-start | bytes 688136 | tf_op jit(solution)/shard_map/ppermute | solution.py:40
  22.5 2.9 %collective-permute-start.36 = (bf16[2,32,1792]{2,1,0:T(8,128)(2,1)S(1)}, bf16[2,32,1792]{2,1,0:T(8,128)(2,1)S(1)}, u32[]{:S(2)}, u32[]{:S(2)}) collective-permute-start(bf16[2,32,1792]{2,1,0:T(8,128)(2,1)S(1)} %slice.17), channel_id=1, source_target_pairs={{0,4},{1,5},{2,6},{3,7},{4,0},{5,1},{6,2},{7,3},{8,12},{9,13},{10,... | collective-permute-start | bytes 688136 | tf_op jit(solution)/shard_map/ppermute | solution.py:40
  27.5 2.2 %collective-permute-start.42 = (bf16[2,32,1792]{2,1,0:T(8,128)(2,1)S(1)}, bf16[2,32,1792]{2,1,0:T(8,128)(2,1)S(1)}, u32[]{:S(2)}, u32[]{:S(2)}) collective-permute-start(bf16[2,32,1792]{2,1,0:T(8,128)(2,1)S(1)} %slice.19), channel_id=1, source_target_pairs={{0,24},{1,25},{2,26},{3,27},{4,28},{5,29},{6,30},{7,31},{8,0},{9,1... | collective-permute-start | bytes 688136 | tf_op jit(solution)/shard_map/ppermute | solution.py:40
  36.9 2.9 %collective-permute-start.43 = (bf16[2,256,1792]{2,1,0:T(8,128)(2,1)}, bf16[2,256,1792]{2,1,0:T(8,128)(2,1)}, u32[]{:S(2)}, u32[]{:S(2)}) collective-permute-start(bf16[2,256,1792]{2,1,0:T(8,128)(2,1)} %shard_map.139.refs_3_.refs_8_), channel_id=1, source_target_pairs={{0,4},{1,5},{2,6},{3,7},{4,0},{5,1},{6,2},{7,3},{8,12},{9,13},{10,... | collective-permute-start | bytes 5505032 | tf_op jit(solution)/shard_map/ppermute | solution.py:40
  41.8 5.2 %shard_map.140 = (bf16[2,448,1536]{2,1,0:T(8,128)(2,1)S(1)}, bf16[2,448,2048]{2,1,0:T(8,128)(2,1)S(1)}, bf16[2,2048,1792]{2,1,0:T(8,128)(2,1)}) custom-call(bf16[448,1792]{1,0:T(8,128)(2,1)} %bitcast.24, bf16[448,1792]{1,0:T(8,128)(2,1)} %bitcast.29, bf16[2,256,1792]{2,1,0:T(8,128)(2,1)} %shard_map.138.refs_2_.refs_7_, ...), custom_call_target="tpu_custom_call" | custom-call | flops 3288334336 | bytes 7798784 | tf_op jit(solution)/shard_map/pallas_call | solution.py:278
  46.9 26.2 %collective-permute-done.37.refs_0_.refs_3_ = bf16[2,256,1792]{2,1,0:T(8,128)(2,1)} collective-permute-done((bf16[2,256,1792]{2,1,0:T(8,128)(2,1)}, bf16[2,256,1792]{2,1,0:T(8,128)(2,1)}, u32[]{:S(2)}, u32[]{:S(2)}) %collective-permute-start.37) | collective-permute-done | bytes 1835040 | tf_op jit(solution)/shard_map/ppermute | solution.py:40
  73.2 4.4 %collective-permute-done.43.refs_2_.refs_5_ = bf16[2,256,1792]{2,1,0:T(8,128)(2,1)} collective-permute-done((bf16[2,256,1792]{2,1,0:T(8,128)(2,1)}, bf16[2,256,1792]{2,1,0:T(8,128)(2,1)}, u32[]{:S(2)}, u32[]{:S(2)}) %collective-permute-start.43) | collective-permute-done | bytes 1835040 | tf_op jit(solution)/shard_map/ppermute | solution.py:40
  77.6 2.6 %collective-permute-done.44.refs_3_.refs_6_ = bf16[2,256,1792]{2,1,0:T(8,128)(2,1)} collective-permute-done((bf16[2,256,1792]{2,1,0:T(8,128)(2,1)}, bf16[2,256,1792]{2,1,0:T(8,128)(2,1)}, u32[]{:S(2)}, u32[]{:S(2)}) %collective-permute-start.44) | collective-permute-done | bytes 1835040 | tf_op jit(solution)/shard_map/ppermute | solution.py:40
  82.3 3.2 %collective-permute-start.46 = (bf16[2,128,1792]{2,1,0:T(8,128)(2,1)S(1)}, bf16[2,128,1792]{2,1,0:T(8,128)(2,1)S(1)}, u32[]{:S(2)}, u32[]{:S(2)}) collective-permute-start(bf16[2,128,1792]{2,1,0:T(8,128)(2,1)S(1)} %get-tuple-element.221), channel_id=1, source_target_pairs={{0,24},{1,25},{2,26},{3,27},{4,28},{5,29},{6,30},{7,31},{8,0},{9,1... | collective-permute-start | bytes 2752520 | tf_op jit(solution)/shard_map/ppermute | solution.py:40
  88.1 16.0 %shard_map.142 = (bf16[2,448,1536]{2,1,0:T(8,128)(2,1)S(1)}, bf16[2,448,2048]{2,1,0:T(8,128)(2,1)S(1)}, bf16[2,2048,1792]{2,1,0:T(8,128)(2,1)}) custom-call(bf16[448,1792]{1,0:T(8,128)(2,1)} %bitcast.25, bf16[448,1792]{1,0:T(8,128)(2,1)} %bitcast.30, ...), custom_call_target="tpu_custom_call", output_to_operand_aliasing={{0}: (9, {}), {1}: (10, {}), {2}: (11, {})} | custom-call | flops 16441671680 | bytes 22937600 | tf_op jit(solution)/shard_map/pallas_call | solution.py:278
  105.6 5.9 %shard_map.143 = (bf16[2,448,2048]{2,1,0:T(8,128)(2,1)S(1)}, bf16[2,2048,1792]{2,1,0:T(8,128)(2,1)}, bf16[2,448,128]{2,1,0:T(8,128)(2,1)S(1)}) custom-call(bf16[2,448,1792]{2,1,0:T(8,128)(2,1)S(1)} %collective-permute-done.32.refs_2_.refs_0_, ...), custom_call_target="tpu_custom_call", output_to_operand_aliasing={{0}: (5, {}), {1}: (6, {})} | custom-call | flops 4227858432 | bytes 6881280 | tf_op jit(solution)/shard_map/pallas_call | solution.py:403
  111.6 100.2 %conditional.1 = (bf16[448,1792]{1,0:T(8,128)(2,1)}, bf16[448,1792]{1,0:T(8,128)(2,1)}, bf16[448,1792]{1,0:T(8,128)(2,1)}, bf16[448,1792]{1,0:T(8,128)(2,1)}, bf...) conditional(s32[]{:T(128)} %convert_element_type.6, (bf16[2,448,2048]{2,1,0:T(8,128)(2,1)S(1)}, ...), branch_computations={%region_0.1_spmd, %region_1.2_spmd} | conditional | flops 28655484928 | bytes 206996112 | solution.py:634
  112.0 3.0 %branch_0_fun.19.refs_0_ = bf16[2,448,256]{2,1,0:T(8,128)(2,1)S(1)} custom-call(bf16[2,448,2048]{2,1,0:T(8,128)(2,1)S(1)} %get-tuple-element.48.pair, bf16[2,2048,1792]{2,1,0:T(8,128)(2,1)} %get-tuple-element.47.tokens.tokens_in.refs_2_), custom_call_target="tpu_custom_call" | custom-call | flops 1879048192 | bytes 5767168 | tf_op jit(solution)/shard_map/cond/branch_0_fun/pallas_call | solution.py:458
  121.3 3.0 %branch_0_fun.21.refs_1_ = bf16[2,448,512]{2,1,0:T(8,128)(2,1)S(1)} custom-call(bf16[448,1792]{1,0:T(8,128)(2,1)S(1)} %get-tuple-element.45.up.refs_5_, bf16[448,1792]{1,0:T(8,128)(2,1)S(1)} %get-tuple-element.46.down.refs_8_, bf16[2,2048,1792]{2,1,0:T(8,128)(2,1)S(1)} %copy-done.2, bf16[2,448,256]{2,1,0:T(8,128)(2,1)S(1)} %branch_0_fun.20.refs_0_), custom_call_target="tpu_custom_call" | custom-call | flops 3288334336 | bytes 6881280 | tf_op jit(solution)/shard_map/cond/branch_0_fun/pallas_call | solution.py:329
  124.4 3.4 %branch_0_fun.22 = (bf16[2,448,128]{2,1,0:T(8,128)(2,1)S(1)}, bf16[448,1792]{1,0:T(8,128)(2,1)}, bf16[448,1792]{1,0:T(8,128)(2,1)}, bf16[448,1792]{1,0:T(8,128)(...) custom-call(bf16[2,448,1536]{2,1,0:T(8,128)(2,1)S(1)} %get-tuple-element.44.refs_0_, ...), custom_call_target="tpu_custom_call" | custom-call | flops 939524096 | bytes 6782976 | tf_op jit(solution)/shard_map/cond/branch_0_fun/pallas_call | solution.py:527
  129.2 3.7 %branch_0_fun.23 = (bf16[2,448,256]{2,1,0:T(8,128)(2,1)S(1)}, bf16[448,1792]{1,0:T(8,128)(2,1)}, bf16[448,1792]{1,0:T(8,128)(2,1)}, bf16[448,1792]{1,0:T(8,128)(...) custom-call(bf16[2,448,1536]{2,1,0:T(8,128)(2,1)S(1)} %get-tuple-ele, ...), custom_call_target="tpu_custom_call", output_to_operand_aliasing={{1}: (11, {}), {2}: (12, {}), {3}: (13, {}), {4}: (14, {}),... | custom-call | flops 1879048192 | bytes 9895936 | tf_op jit(solution)/shard_map/cond/branch_0_fun/pallas_call | solution.py:527
  136.3 2.5 %collective-permute-done.4.refs_4_ = bf16[2,448,256]{2,1,0:T(8,128)(2,1)S(1)} collective-permute-done((bf16[2,448,256]{2,1,0:T(8,128)(2,1)S(1)}, bf16[2,448,256]{2,1,0:T(8,128)(2,1)S(1)}, u32[]{:S(2)}, u32[]{:S(2)}) %collective-permute-start.4) | collective-permute-done | bytes 458784 | tf_op jit(solution)/shard_map/cond/branch_0_fun/ppermute | solution.py:40
  138.8 3.9 %branch_0_fun.25 = (bf16[2,448,256]{2,1,0:T(8,128)(2,1)S(1)}, bf16[448,1792]{1,0:T(8,128)(2,1)}, bf16[448,1792]{1,0:T(8,128)(2,1)}, bf16[448,1792]{1,0:T(8,128)(...) custom-call(bf16[2,448,1536]{2,1,0:T(8,128)(2,1)S(1)} %get-tuple-ele, ...), custom_call_target="tpu_custom_call", output_to_operand_aliasing={{1}: (13, {}), {2}: (14, {}), {3}: (15, {}), {4}: (16, {}),... | custom-call | flops 1879048192 | bytes 9895936 | tf_op jit(solution)/shard_map/cond/branch_0_fun/pallas_call | solution.py:527
  145.8 2.8 %collective-permute-done.2.refs_4_ = bf16[2,448,256]{2,1,0:T(8,128)(2,1)S(1)} collective-permute-done((bf16[2,448,256]{2,1,0:T(8,128)(2,1)S(1)}, bf16[2,448,256]{2,1,0:T(8,128)(2,1)S(1)}, u32[]{:S(2)}, u32[]{:S(2)}) %collective-permute-start.2) | collective-permute-done | bytes 458784 | tf_op jit(solution)/shard_map/cond/branch_0_fun/ppermute | solution.py:40
  149.2 4.1 %branch_0_fun.26 = (bf16[2,448,256]{2,1,0:T(8,128)(2,1)S(1)}, bf16[448,1792]{1,0:T(8,128)(2,1)}, bf16[448,1792]{1,0:T(8,128)(2,1)}, bf16[448,1792]{1,0:T(8,128)(...) custom-call(bf16[2,448,1536]{2,1,0:T(8,128)(2,1)S(1)} %get-tuple-ele, ...), custom_call_target="tpu_custom_call", output_to_operand_aliasing={{1}: (13, {}), {2}: (14, {}), {3}: (15, {}), {4}: (16, {}),... | custom-call | flops 1879048192 | bytes 9895936 | tf_op jit(solution)/shard_map/cond/branch_0_fun/pallas_call | solution.py:527
  156.0 2.4 %collective-permute-done.8.refs_4_ = bf16[2,448,256]{2,1,0:T(8,128)(2,1)S(1)} collective-permute-done((bf16[2,448,256]{2,1,0:T(8,128)(2,1)S(1)}, bf16[2,448,256]{2,1,0:T(8,128)(2,1)S(1)}, u32[]{:S(2)}, u32[]{:S(2)}) %collective-permute-start.8) | collective-permute-done | bytes 458784 | tf_op jit(solution)/shard_map/cond/branch_0_fun/ppermute | solution.py:40
  158.7 4.1 %branch_0_fun.29 = (bf16[2,448,256]{2,1,0:T(8,128)(2,1)S(1)}, bf16[448,1792]{1,0:T(8,128)(2,1)}, bf16[448,1792]{1,0:T(8,128)(2,1)}, bf16[448,1792]{1,0:T(8,128)(...) custom-call(bf16[2,448,1536]{2,1,0:T(8,128)(2,1)S(1)} %get-tuple-ele, ...), custom_call_target="tpu_custom_call", output_to_operand_aliasing={{1}: (13, {}), {2}: (14, {}), {3}: (15, {}), {4}: (16, {}),... | custom-call | flops 1879048192 | bytes 9895936 | tf_op jit(solution)/shard_map/cond/branch_0_fun/pallas_call | solution.py:527
  165.6 2.6 %collective-permute-done.6.refs_4_ = bf16[2,448,256]{2,1,0:T(8,128)(2,1)S(1)} collective-permute-done((bf16[2,448,256]{2,1,0:T(8,128)(2,1)S(1)}, bf16[2,448,256]{2,1,0:T(8,128)(2,1)S(1)}, u32[]{:S(2)}, u32[]{:S(2)}) %collective-permute-start.6) | collective-permute-done | bytes 458784 | tf_op jit(solution)/shard_map/cond/branch_0_fun/ppermute | solution.py:40
  168.3 4.1 %branch_0_fun.30 = (bf16[2,448,256]{2,1,0:T(8,128)(2,1)S(1)}, bf16[448,1792]{1,0:T(8,128)(2,1)}, bf16[448,1792]{1,0:T(8,128)(2,1)}, bf16[448,1792]{1,0:T(8,128)(...) custom-call(bf16[2,448,1536]{2,1,0:T(8,128)(2,1)S(1)} %get-tuple-ele, ...), custom_call_target="tpu_custom_call", output_to_operand_aliasing={{1}: (13, {}), {2}: (14, {}), {3}: (15, {}), {4}: (16, {}),... | custom-call | flops 1879048192 | bytes 9895936 | tf_op jit(solution)/shard_map/cond/branch_0_fun/pallas_call | solution.py:527
  176.0 3.1 %collective-permute-done.12.refs_12_ = bf16[2,448,256]{2,1,0:T(8,128)(2,1)S(1)} collective-permute-done((bf16[2,448,256]{2,1,0:T(8,128)(2,1)S(1)}, bf16[2,448,256]{2,1,0:T(8,128)(2,1)S(1)}, u32[]{:S(2)}, u32[]{:S(2)}) %collective-permute-start.12) | collective-permute-done | bytes 458784 | tf_op jit(solution)/shard_map/cond/branch_0_fun/ppermute | solution.py:625
  179.1 4.1 %branch_0_fun.33 = (bf16[2,448,256]{2,1,0:T(8,128)(2,1)S(1)}, bf16[448,1792]{1,0:T(8,128)(2,1)}, bf16[448,1792]{1,0:T(8,128)(2,1)}, bf16[448,1792]{1,0:T(8,128)(...) custom-call(bf16[2,448,1536]{2,1,0:T(8,128)(2,1)S(1)} %get-tuple-ele, ...), custom_call_target="tpu_custom_call", output_to_operand_aliasing={{1}: (13, {}), {2}: (14, {}), {3}: (15, {}), {4}: (16, {}),... | custom-call | flops 1879048192 | bytes 9895936 | tf_op jit(solution)/shard_map/cond/branch_0_fun/pallas_call | solution.py:527
  183.2 3.3 %branch_0_fun.34 = (bf16[2,448,128]{2,1,0:T(8,128)(2,1)S(1)}, bf16[448,1792]{1,0:T(8,128)(2,1)}, bf16[448,1792]{1,0:T(8,128)(2,1)}, bf16[448,1792]{1,0:T(8,128)(...) custom-call(bf16[2,448,1536]{2,1,0:T(8,128)(2,1)S(1)} %get-tuple-ele, ...), custom_call_target="tpu_custom_call", output_to_operand_aliasing={{1}: (11, {}), {2}: (12, {}), {3}: (13, {}), {4}: (14, {}),... | custom-call | flops 939524096 | bytes 6782976 | tf_op jit(solution)/shard_map/cond/branch_0_fun/pallas_call | solution.py:527
  189.9 5.7 %collective-permute-done.14.other = bf16[2,448,256]{2,1,0:T(8,128)(2,1)S(1)} collective-permute-done((bf16[2,448,256]{2,1,0:T(8,128)(2,1)S(1)}, bf16[2,448,256]{2,1,0:T(8,128)(2,1)S(1)}, u32[]{:S(2)}, u32[]{:S(2)}) %collective-permute-start.14) | collective-permute-done | bytes 458784 | tf_op jit(solution)/shard_map/cond/branch_0_fun/ppermute | solution.py:625
  (85 shorter events, 54.9 us)
Async XLA Ops:
  3.6 84.5 %collective-permute-start.32 = (bf16[2,448,1792]{2,1,0:T(8,128)(2,1)}, bf16[2,448,1792]{2,1,0:T(8,128)(2,1)S(1)}, u32[]{:S(2)}, u32[]{:S(2)}) collective-permute-start(bf16[2,448,1792]{2,1,0:T(8,128)(2,1)} %shard_map.136), channel_id=1, source_target_pairs={{0,1},{1,0},{2,3},{3,2},{4,5},{5,4},{6,7},{7,6},{8,9},{9,8},{10,11... | collective-permute-start | bytes 9633800 | tf_op jit(solution)/shard_map/ppermute | solution.py:40
  6.5 13.6 %collective-permute-start.33 = (bf16[2,64,1792]{2,1,0:T(8,128)(2,1)S(1)}, bf16[2,64,1792]{2,1,0:T(8,128)(2,1)S(1)}, u32[]{:S(2)}, u32[]{:S(2)}) collective-permute-start(bf16[2,64,1792]{2,1,0:T(8,128)(2,1)S(1)} %get-tuple-element.217.refs_0_), channel_id=1, source_target_pairs={{0,4},{1,5},{2,6},{3,7},{4,0},{5,1},{6,2},{7,3},{8,12},{9,13},{10,... | collective-permute-start | bytes 1376264 | tf_op jit(solution)/shard_map/ppermute | solution.py:40
  9.6 12.9 %collective-permute-start.34 = (bf16[2,64,1792]{2,1,0:T(8,128)(2,1)S(1)}, bf16[2,64,1792]{2,1,0:T(8,128)(2,1)S(1)}, u32[]{:S(2)}, u32[]{:S(2)}) collective-permute-start(bf16[2,64,1792]{2,1,0:T(8,128)(2,1)S(1)} %get-tuple-element.217.refs_0_), channel_id=1, source_target_pairs={{0,3},{1,2},{2,1},{3,0},{4,7},{5,6},{6,5},{7,4},{8,11},{9,10},{10,... | collective-permute-start | bytes 1376264 | tf_op jit(solution)/shard_map/ppermute | solution.py:40
  11.7 13.7 %collective-permute-start.39 = (bf16[2,64,1792]{2,1,0:T(8,128)(2,1)S(1)}, bf16[2,64,1792]{2,1,0:T(8,128)(2,1)S(1)}, u32[]{:S(2)}, u32[]{:S(2)}) collective-permute-start(bf16[2,64,1792]{2,1,0:T(8,128)(2,1)S(1)} %get-tuple-element.218.refs_0_), channel_id=1, source_target_pairs={{0,8},{1,9},{2,10},{3,11},{4,12},{5,13},{6,14},{7,15},{8,16},{9,17... | collective-permute-start | bytes 1376264 | tf_op jit(solution)/shard_map/ppermute | solution.py:40
  13.7 13.8 %collective-permute-start.40 = (bf16[2,64,1792]{2,1,0:T(8,128)(2,1)S(1)}, bf16[2,64,1792]{2,1,0:T(8,128)(2,1)S(1)}, u32[]{:S(2)}, u32[]{:S(2)}) collective-permute-start(bf16[2,64,1792]{2,1,0:T(8,128)(2,1)S(1)} %get-tuple-element.218.refs_0_), channel_id=1, source_target_pairs={{0,24},{1,25},{2,26},{3,27},{4,28},{5,29},{6,30},{7,31},{8,0},{9,1... | collective-permute-start | bytes 1376264 | tf_op jit(solution)/shard_map/ppermute | solution.py:40
  20.0 9.6 %collective-permute-start.35 = (bf16[2,32,1792]{2,1,0:T(8,128)(2,1)S(1)}, bf16[2,32,1792]{2,1,0:T(8,128)(2,1)S(1)}, u32[]{:S(2)}, u32[]{:S(2)}) collective-permute-start(bf16[2,32,1792]{2,1,0:T(8,128)(2,1)S(1)} %slice.16), channel_id=1, source_target_pairs={{0,3},{1,2},{2,1},{3,0},{4,7},{5,6},{6,5},{7,4},{8,11},{9,10},{10,... | collective-permute-start | bytes 688136 | tf_op jit(solution)/shard_map/ppermute | solution.py:40
  25.5 10.0 %collective-permute-start.41 = (bf16[2,32,1792]{2,1,0:T(8,128)(2,1)S(1)}, bf16[2,32,1792]{2,1,0:T(8,128)(2,1)S(1)}, u32[]{:S(2)}, u32[]{:S(2)}) collective-permute-start(bf16[2,32,1792]{2,1,0:T(8,128)(2,1)S(1)} %slice.18), channel_id=1, source_target_pairs={{0,8},{1,9},{2,10},{3,11},{4,12},{5,13},{6,14},{7,15},{8,16},{9,17... | collective-permute-start | bytes 688136 | tf_op jit(solution)/shard_map/ppermute | solution.py:40
  27.5 8.0 %collective-permute-start.42 = (bf16[2,32,1792]{2,1,0:T(8,128)(2,1)S(1)}, bf16[2,32,1792]{2,1,0:T(8,128)(2,1)S(1)}, u32[]{:S(2)}, u32[]{:S(2)}) collective-permute-start(bf16[2,32,1792]{2,1,0:T(8,128)(2,1)S(1)} %slice.19), channel_id=1, source_target_pairs={{0,24},{1,25},{2,26},{3,27},{4,28},{5,29},{6,30},{7,31},{8,0},{9,1... | collective-permute-start | bytes 688136 | tf_op jit(solution)/shard_map/ppermute | solution.py:40
  31.4 41.7 %collective-permute-start.37 = (bf16[2,256,1792]{2,1,0:T(8,128)(2,1)}, bf16[2,256,1792]{2,1,0:T(8,128)(2,1)}, u32[]{:S(2)}, u32[]{:S(2)}) collective-permute-start(bf16[2,256,1792]{2,1,0:T(8,128)(2,1)} %shard_map.138.refs_2_.refs_7_), channel_id=1, source_target_pairs={{0,8},{1,9},{2,10},{3,11},{4,12},{5,13},{6,14},{7,15},{8,16},{9,17... | collective-permute-start | bytes 5505032 | tf_op jit(solution)/shard_map/ppermute | solution.py:40
  33.4 39.8 %collective-permute-start.38 = (bf16[2,256,1792]{2,1,0:T(8,128)(2,1)}, bf16[2,256,1792]{2,1,0:T(8,128)(2,1)}, u32[]{:S(2)}, u32[]{:S(2)}) collective-permute-start(bf16[2,256,1792]{2,1,0:T(8,128)(2,1)} %shard_map.138.refs_2_.refs_7_), channel_id=1, source_target_pairs={{0,24},{1,25},{2,26},{3,27},{4,28},{5,29},{6,30},{7,31},{8,0},{9,1... | collective-permute-start | bytes 5505032 | tf_op jit(solution)/shard_map/ppermute | solution.py:40
  36.9 40.7 %collective-permute-start.43 = (bf16[2,256,1792]{2,1,0:T(8,128)(2,1)}, bf16[2,256,1792]{2,1,0:T(8,128)(2,1)}, u32[]{:S(2)}, u32[]{:S(2)}) collective-permute-start(bf16[2,256,1792]{2,1,0:T(8,128)(2,1)} %shard_map.139.refs_3_.refs_8_), channel_id=1, source_target_pairs={{0,4},{1,5},{2,6},{3,7},{4,0},{5,1},{6,2},{7,3},{8,12},{9,13},{10,... | collective-permute-start | bytes 5505032 | tf_op jit(solution)/shard_map/ppermute | solution.py:40
  39.8 40.4 %collective-permute-start.44 = (bf16[2,256,1792]{2,1,0:T(8,128)(2,1)}, bf16[2,256,1792]{2,1,0:T(8,128)(2,1)}, u32[]{:S(2)}, u32[]{:S(2)}) collective-permute-start(bf16[2,256,1792]{2,1,0:T(8,128)(2,1)} %shard_map.139.refs_3_.refs_8_), channel_id=1, source_target_pairs={{0,3},{1,2},{2,1},{3,0},{4,7},{5,6},{6,5},{7,4},{8,11},{9,10},{10,... | collective-permute-start | bytes 5505032 | tf_op jit(solution)/shard_map/ppermute | solution.py:40
  82.2 21.9 %collective-permute-start.45 = (bf16[2,128,1792]{2,1,0:T(8,128)(2,1)S(1)}, bf16[2,128,1792]{2,1,0:T(8,128)(2,1)S(1)}, u32[]{:S(2)}, u32[]{:S(2)}) collective-permute-start(bf16[2,128,1792]{2,1,0:T(8,128)(2,1)S(1)} %get-tuple-element.220.refs_12_), channel_id=1, source_target_pairs={{0,8},{1,9},{2,10},{3,11},{4,12},{5,13},{6,14},{7,15},{8,16},{9,17... | collective-permute-start | bytes 2752520 | tf_op jit(solution)/shard_map/ppermute | solution.py:40
  82.3 21.8 %collective-permute-start.46 = (bf16[2,128,1792]{2,1,0:T(8,128)(2,1)S(1)}, bf16[2,128,1792]{2,1,0:T(8,128)(2,1)S(1)}, u32[]{:S(2)}, u32[]{:S(2)}) collective-permute-start(bf16[2,128,1792]{2,1,0:T(8,128)(2,1)S(1)} %get-tuple-element.221), channel_id=1, source_target_pairs={{0,24},{1,25},{2,26},{3,27},{4,28},{5,29},{6,30},{7,31},{8,0},{9,1... | collective-permute-start | bytes 2752520 | tf_op jit(solution)/shard_map/ppermute | solution.py:40
  85.6 18.9 %collective-permute-start.47 = (bf16[2,128,1792]{2,1,0:T(8,128)(2,1)S(1)}, bf16[2,128,1792]{2,1,0:T(8,128)(2,1)S(1)}, u32[]{:S(2)}, u32[]{:S(2)}) collective-permute-start(bf16[2,128,1792]{2,1,0:T(8,128)(2,1)S(1)} %get-tuple-element.222), channel_id=1, source_target_pairs={{0,3},{1,2},{2,1},{3,0},{4,7},{5,6},{6,5},{7,4},{8,11},{9,10},{10,... | collective-permute-start | bytes 2752520 | tf_op jit(solution)/shard_map/ppermute | solution.py:40
  86.6 18.9 %collective-permute-start.48 = (bf16[2,128,1792]{2,1,0:T(8,128)(2,1)S(1)}, bf16[2,128,1792]{2,1,0:T(8,128)(2,1)S(1)}, u32[]{:S(2)}, u32[]{:S(2)}) collective-permute-start(bf16[2,128,1792]{2,1,0:T(8,128)(2,1)S(1)} %get-tuple-element.223), channel_id=1, source_target_pairs={{0,4},{1,5},{2,6},{3,7},{4,0},{5,1},{6,2},{7,3},{8,12},{9,13},{10,... | collective-permute-start | bytes 2752520 | tf_op jit(solution)/shard_map/ppermute | solution.py:40
  111.6 12.7 %collective-permute-start.1 = (bf16[2,448,128]{2,1,0:T(8,128)(2,1)S(1)}, bf16[2,448,128]{2,1,0:T(8,128)(2,1)S(1)}, u32[]{:S(2)}, u32[]{:S(2)}) collective-permute-start(bf16[2,448,128]{2,1,0:T(8,128)(2,1)S(1)} %get-tuple-element.54), channel_id=1, source_target_pairs={{0,1},{1,0},{2,3},{3,2},{4,5},{5,4},{6,7},{7,6},{8,9},{9,8},{10,11... | collective-permute-start | bytes 688136 | tf_op jit(solution)/shard_map/cond/branch_0_fun/ppermute | solution.py:40
  115.0 14.1 %collective-permute-start = (bf16[2,448,256]{2,1,0:T(8,128)(2,1)S(1)}, bf16[2,448,256]{2,1,0:T(8,128)(2,1)S(1)}, u32[]{:S(2)}, u32[]{:S(2)}) collective-permute-start(bf16[2,448,256]{2,1,0:T(8,128)(2,1)S(1)} %branch_0_fun.19.refs_0_), channel_id=1, source_target_pairs={{0,1},{1,0},{2,3},{3,2},{4,5},{5,4},{6,7},{7,6},{8,9},{9,8},{10,11... | collective-permute-start | bytes 1376264 | tf_op jit(solution)/shard_map/cond/branch_0_fun/ppermute | solution.py:40
  119.2 19.5 %collective-permute-start.4 = (bf16[2,448,256]{2,1,0:T(8,128)(2,1)S(1)}, bf16[2,448,256]{2,1,0:T(8,128)(2,1)S(1)}, u32[]{:S(2)}, u32[]{:S(2)}) collective-permute-start(bf16[2,448,256]{2,1,0:T(8,128)(2,1)S(1)} %branch_0_fun.20.refs_0_), channel_id=1, source_target_pairs={{0,1},{1,0},{2,3},{3,2},{4,5},{5,4},{6,7},{7,6},{8,9},{9,8},{10,11... | collective-permute-start | bytes 1376264 | tf_op jit(solution)/shard_map/cond/branch_0_fun/ppermute | solution.py:40
  127.8 8.5 %collective-permute-start.5 = (bf16[2,448,128]{2,1,0:T(8,128)(2,1)S(1)}, bf16[2,448,128]{2,1,0:T(8,128)(2,1)S(1)}, u32[]{:S(2)}, u32[]{:S(2)}) collective-permute-start(bf16[2,448,128]{2,1,0:T(8,128)(2,1)S(1)} %get-tuple-element.62.refs_11_), channel_id=1, source_target_pairs={{0,64},{32,96},{64,0},{96,32},{1,65},{33,97},{65,1},{97,33},{2,66}... | collective-permute-start | bytes 688136 | tf_op jit(solution)/shard_map/cond/branch_0_fun/ppermute | solution.py:625
  134.3 14.3 %collective-permute-start.2 = (bf16[2,448,256]{2,1,0:T(8,128)(2,1)S(1)}, bf16[2,448,256]{2,1,0:T(8,128)(2,1)S(1)}, u32[]{:S(2)}, u32[]{:S(2)}) collective-permute-start(bf16[2,448,256]{2,1,0:T(8,128)(2,1)S(1)} %branch_0_fun.24), channel_id=1, source_target_pairs={{0,1},{1,0},{2,3},{3,2},{4,5},{5,4},{6,7},{7,6},{8,9},{9,8},{10,11... | collective-permute-start | bytes 1376264 | tf_op jit(solution)/shard_map/cond/branch_0_fun/ppermute | solution.py:40
  135.8 13.4 %collective-permute-start.3 = (bf16[2,448,256]{2,1,0:T(8,128)(2,1)S(1)}, bf16[2,448,256]{2,1,0:T(8,128)(2,1)S(1)}, u32[]{:S(2)}, u32[]{:S(2)}) collective-permute-start(bf16[2,448,256]{2,1,0:T(8,128)(2,1)S(1)} %get-tuple-element.61.refs_0_.refs_11_), channel_id=1, source_target_pairs={{0,64},{32,96},{64,0},{96,32},{1,65},{33,97},{65,1},{97,33},{2,66}... | collective-permute-start | bytes 1376264 | tf_op jit(solution)/shard_map/cond/branch_0_fun/ppermute | solution.py:625
  144.1 14.3 %collective-permute-start.8 = (bf16[2,448,256]{2,1,0:T(8,128)(2,1)S(1)}, bf16[2,448,256]{2,1,0:T(8,128)(2,1)S(1)}, u32[]{:S(2)}, u32[]{:S(2)}) collective-permute-start(bf16[2,448,256]{2,1,0:T(8,128)(2,1)S(1)} %branch_0_fun.28), channel_id=1, source_target_pairs={{0,1},{1,0},{2,3},{3,2},{4,5},{5,4},{6,7},{7,6},{8,9},{9,8},{10,11... | collective-permute-start | bytes 1376264 | tf_op jit(solution)/shard_map/cond/branch_0_fun/ppermute | solution.py:40
  145.8 12.9 %collective-permute-start.9 = (bf16[2,448,256]{2,1,0:T(8,128)(2,1)S(1)}, bf16[2,448,256]{2,1,0:T(8,128)(2,1)S(1)}, u32[]{:S(2)}, u32[]{:S(2)}) collective-permute-start(bf16[2,448,256]{2,1,0:T(8,128)(2,1)S(1)} %get-tuple-element.76.refs_0_.refs_11_), channel_id=1, source_target_pairs={{0,64},{32,96},{64,0},{96,32},{1,65},{33,97},{65,1},{97,33},{2,66}... | collective-permute-start | bytes 1376264 | tf_op jit(solution)/shard_map/cond/branch_0_fun/ppermute | solution.py:625
  153.2 15.1 %collective-permute-start.7 = (bf16[2,448,256]{2,1,0:T(8,128)(2,1)S(1)}, bf16[2,448,256]{2,1,0:T(8,128)(2,1)S(1)}, u32[]{:S(2)}, u32[]{:S(2)}) collective-permute-start(bf16[2,448,256]{2,1,0:T(8,128)(2,1)S(1)} %get-tuple-element.75.refs_0_.refs_11_), channel_id=1, source_target_pairs={{0,64},{32,96},{64,0},{96,32},{1,65},{33,97},{65,1},{97,33},{2,66}... | collective-permute-start | bytes 1376264 | tf_op jit(solution)/shard_map/cond/branch_0_fun/ppermute | solution.py:625
  154.7 13.6 %collective-permute-start.6 = (bf16[2,448,256]{2,1,0:T(8,128)(2,1)S(1)}, bf16[2,448,256]{2,1,0:T(8,128)(2,1)S(1)}, u32[]{:S(2)}, u32[]{:S(2)}) collective-permute-start(bf16[2,448,256]{2,1,0:T(8,128)(2,1)S(1)} %branch_0_fun.27), channel_id=1, source_target_pairs={{0,1},{1,0},{2,3},{3,2},{4,5},{5,4},{6,7},{7,6},{8,9},{9,8},{10,11... | collective-permute-start | bytes 1376264 | tf_op jit(solution)/shard_map/cond/branch_0_fun/ppermute | solution.py:40
  164.2 11.7 %collective-permute-start.11 = (bf16[2,448,256]{2,1,0:T(8,128)(2,1)S(1)}, bf16[2,448,256]{2,1,0:T(8,128)(2,1)S(1)}, u32[]{:S(2)}, u32[]{:S(2)}) collective-permute-start(bf16[2,448,256]{2,1,0:T(8,128)(2,1)S(1)} %branch_0_fun.32), channel_id=1, source_target_pairs={{0,1},{1,0},{2,3},{3,2},{4,5},{5,4},{6,7},{7,6},{8,9},{9,8},{10,11... | collective-permute-start | bytes 1376264 | tf_op jit(solution)/shard_map/cond/branch_0_fun/ppermute | solution.py:40
  165.6 13.5 %collective-permute-start.12 = (bf16[2,448,256]{2,1,0:T(8,128)(2,1)S(1)}, bf16[2,448,256]{2,1,0:T(8,128)(2,1)S(1)}, u32[]{:S(2)}, u32[]{:S(2)}) collective-permute-start(bf16[2,448,256]{2,1,0:T(8,128)(2,1)S(1)} %get-tuple-element.90.refs_0_.refs_11_), channel_id=1, source_target_pairs={{0,64},{32,96},{64,0},{96,32},{1,65},{33,97},{65,1},{97,33},{2,66}... | collective-permute-start | bytes 1376264 | tf_op jit(solution)/shard_map/cond/branch_0_fun/ppermute | solution.py:625
  172.4 16.5 %collective-permute-start.15 = (bf16[2,448,256]{2,1,0:T(8,128)(2,1)S(1)}, bf16[2,448,256]{2,1,0:T(8,128)(2,1)S(1)}, u32[]{:S(2)}, u32[]{:S(2)}) collective-permute-start(bf16[2,448,256]{2,1,0:T(8,128)(2,1)S(1)} %get-tuple-element.89.refs_0_.own), channel_id=1, source_target_pairs={{0,64},{32,96},{64,0},{96,32},{1,65},{33,97},{65,1},{97,33},{2,66}... | collective-permute-start | bytes 1376264 | tf_op jit(solution)/shard_map/cond/branch_0_fun/ppermute | solution.py:625
  174.2 9.0 %collective-permute-start.10 = (bf16[2,448,128]{2,1,0:T(8,128)(2,1)S(1)}, bf16[2,448,128]{2,1,0:T(8,128)(2,1)S(1)}, u32[]{:S(2)}, u32[]{:S(2)}) collective-permute-start(bf16[2,448,128]{2,1,0:T(8,128)(2,1)S(1)} %branch_0_fun.31), channel_id=1, source_target_pairs={{0,1},{1,0},{2,3},{3,2},{4,5},{5,4},{6,7},{7,6},{8,9},{9,8},{10,11... | collective-permute-start | bytes 688136 | tf_op jit(solution)/shard_map/cond/branch_0_fun/ppermute | solution.py:40
  183.2 12.4 %collective-permute-start.14 = (bf16[2,448,256]{2,1,0:T(8,128)(2,1)S(1)}, bf16[2,448,256]{2,1,0:T(8,128)(2,1)S(1)}, u32[]{:S(2)}, u32[]{:S(2)}) collective-permute-start(bf16[2,448,256]{2,1,0:T(8,128)(2,1)S(1)} %get-tuple-element.104.own), channel_id=1, source_target_pairs={{0,64},{32,96},{64,0},{96,32},{1,65},{33,97},{65,1},{97,33},{2,66}... | collective-permute-start | bytes 1376264 | tf_op jit(solution)/shard_map/cond/branch_0_fun/ppermute | solution.py:625
  186.5 11.6 %collective-permute-start.13 = (bf16[2,448,128]{2,1,0:T(8,128)(2,1)S(1)}, bf16[2,448,128]{2,1,0:T(8,128)(2,1)S(1)}, u32[]{:S(2)}, u32[]{:S(2)}) collective-permute-start(bf16[2,448,128]{2,1,0:T(8,128)(2,1)S(1)} %get-tuple-element.103.own), channel_id=1, source_target_pairs={{0,64},{32,96},{64,0},{96,32},{1,65},{33,97},{65,1},{97,33},{2,66}... | collective-permute-start | bytes 688136 | tf_op jit(solution)/shard_map/cond/branch_0_fun/ppermute | solution.py:625
  (10 other events, 58.9 us)
where the time goes:
time: 217 us; the launch traced here: 213 us
  Pallas kernels  84 us (39%)
  waiting for transfers between devices  63.5 us (29%)
  starting transfers between devices  48.7 us (22%)
  loops' own time  13 us (6%)
  between operations  2.76 us (1%)
    ppermute x25, waiting for transfers between devices, moved(): return lax.ppermute(block, 'fsdp', route)  51.2 us
    ppermute x25, starting transfers between devices, moved(): return lax.ppermute(block, 'fsdp', route)  46.4 us
    pallas_call x8, Pallas kernels, adam_chunk(): pl.pallas_call(functools.partial(adam_kernel, bool(mixed)), out_shape=[ja...  30.7 us
    pallas_call x2, Pallas kernels, hidden_step(): pl.pallas_call(functools.partial(hidden_kernel, jobs, sizes, pieces, skip...  21.2 us
    another operation x1, loops' own time, on_device(): lax.cond(step_index[0] % 2 == 0, lambda: finish(1), lambda: finish(2))  13 us
    ppermute x8, waiting for transfers between devices, finish(): others.append(lax.ppermute(out[0], 'rep', route))  12.2 us
    pallas_call x7, Pallas kernels, theirs_chunk(): pl.pallas_call(theirs_kernel, out_shape=jax.ShapeDtypeStruct((2, HELD, wi...  11.6 us
    pallas_call x1, Pallas kernels, last_shared(): pl.pallas_call(last_shared_kernel, out_shape=[jax.ShapeDtypeStruct((2, HE...  5.94 us
  transfers between devices with their start and end apart: 33, of which 21 were waited for; matrix products, arithmetic and copies ran while one was open for 0% of the time, Pallas kernels for 35%

commit v1 on v0

--- a/solution.py
+++ b/solution.py
@@ -24,8 +24,11 @@
 HELD = 448
 SHARED = 2 * HELD
 TOKENS = 2048
-CHUNKS = ((0, 128),) + tuple((256 * k, 256) for k in range(1, 7)) + ((128, 128),)
-MIXING = 7
+WIDTH = 256
+CHUNKS = D // WIDTH
+FIRST_OWN = 2
+OWN_LATER = ((1, 2, 2), (2, 4, 3))
+MIXING = CHUNKS
 EARLY = 1536
 NZ, NX, NY = 4, 2, 4
 
@@ -295,16 +298,21 @@
     )(*operands)
 
 
-def last_own_kernel(up, down, tokens_in, *refs):
-    pair, weights, tokens, sem = refs[-4:]
+def own_first_kernel(up, down, tokens_in, pair_in, *refs):
+    out, pair, weights, tokens, columns, early, grads, sem = refs[-8:]
+    width = FIRST_OWN * WIDTH
     loads = [
         pltpu.make_async_copy(up, weights.at[0], sem.at[0]),
         pltpu.make_async_copy(down, weights.at[1], sem.at[1]),
         pltpu.make_async_copy(tokens_in.at[:, pl.ds(EARLY, TOKENS - EARLY)], tokens, sem.at[2]),
+        pltpu.make_async_copy(
+            tokens_in.at[:, pl.ds(0, EARLY), pl.ds(0, width)], columns, sem.at[3]
+        ),
+        pltpu.make_async_copy(pair_in, early, sem.at[4]),
     ]
     for load in loads:
         load.start()
-    for load in loads:
+    for load in loads[:3]:
         load.wait()
     tile = 256
 
@@ -322,30 +330,83 @@
         return carry
 
     lax.fori_loop(0, (TOKENS - EARLY) // tile, step, 0)
-
-
-def last_own(up, down, tokens, after):
-    out = jax.ShapeDtypeStruct((2, HELD, TOKENS - EARLY), jnp.bfloat16)
-    return pl.pallas_call(
-        last_own_kernel,
-        out_shape=out,
-        in_specs=[ANY] * (3 + len(after)),
-        out_specs=INSIDE,
+    for load in loads[3:]:
+        load.wait()
+
+    def multiply(i, carry):
+        which, k = i % 2, i // 2
+        at = pl.ds(pl.multiple_of(k * WIDTH, WIDTH), WIDTH)
+        grads[...] = jnp.dot(
+            early[which], columns[which, :, at], preferred_element_type=jnp.float32
+        )
+        out[k, which] = grads[...] + jnp.dot(
+            pair[which], tokens[which, :, at], preferred_element_type=jnp.float32
+        )
+        return carry
+
+    lax.fori_loop(0, 2 * FIRST_OWN, multiply, 0)
+
+
+def own_first(up, down, tokens, pair, after):
+    rest = TOKENS - EARLY
+    return pl.pallas_call(
+        own_first_kernel,
+        out_shape=[
+            jax.ShapeDtypeStruct((FIRST_OWN, 2, HELD, WIDTH), jnp.float32),
+            jax.ShapeDtypeStruct((2, HELD, rest), jnp.bfloat16),
+        ],
+        in_specs=[ANY] * (4 + len(after)),
+        out_specs=[INSIDE] * 2,
         scratch_shapes=[
             pltpu.VMEM((2, HELD, D), jnp.bfloat16),
-            pltpu.VMEM((2, TOKENS - EARLY, D), jnp.bfloat16),
-            pltpu.SemaphoreType.DMA((3,)),
+            pltpu.VMEM((2, rest, D), jnp.bfloat16),
+            pltpu.VMEM((2, EARLY, FIRST_OWN * WIDTH), jnp.bfloat16),
+            pltpu.VMEM((2, HELD, EARLY), jnp.bfloat16),
+            pltpu.VMEM((HELD, WIDTH), jnp.float32),
+            pltpu.SemaphoreType.DMA((5,)),
         ],
+        compiler_params=vmem(24),
+        cost_estimate=cost(4 * HELD * (rest * D + TOKENS * FIRST_OWN * WIDTH), 4 * (HELD + rest) * D),
+    )(up, down, tokens, pair, *after)
+
+
+def own_rest_kernel(pair, pair_last, tokens, out, grads):
+    def multiply(which, carry):
+        grads[...] = jnp.dot(pair[which], tokens[which, :EARLY], preferred_element_type=jnp.float32)
+        out[0, which] = grads[...] + jnp.dot(
+            pair_last[which], tokens[which, EARLY:], preferred_element_type=jnp.float32
+        )
+        return carry
+
+    lax.fori_loop(0, 2, multiply, 0)
+
+
+def own_rest(first, count, pair, pair_last, tokens, after):
+    def kernel(*refs):
+        own_rest_kernel(*refs[:3], *refs[-2:])
+
+    return pl.pallas_call(
+        kernel,
+        out_shape=jax.ShapeDtypeStruct((count, 2, HELD, WIDTH), jnp.float32),
+        grid=(count,),
+        in_specs=[
+            rows_spec(EARLY),
+            rows_spec(TOKENS - EARLY),
+            pl.BlockSpec((2, TOKENS, WIDTH), lambda j: (0, 0, j + first)),
+        ]
+        + [ANY] * len(after),
+        out_specs=pl.BlockSpec((1, 2, HELD, WIDTH), lambda j: (j, 0, 0, 0)),
+        scratch_shapes=[pltpu.VMEM((HELD, WIDTH), jnp.float32)],
         compiler_params=vmem(22),
-        cost_estimate=cost(4 * HELD * (TOKENS - EARLY) * D, 4 * (HELD + TOKENS - EARLY) * D),
-    )(up, down, tokens, *after)
+        cost_estimate=cost(4 * HELD * TOKENS * count * WIDTH, 4 * TOKENS * (HELD + count * WIDTH)),
+    )(pair, pair_last, tokens, *after)
 
 
 def last_shared_kernel(*refs):
     weights_in, blocks = refs[0], refs[1:5]
     pair_in, tokens_in, pair_out, tokens_out, chunk = refs[5:10]
     weights, tokens, pair, columns, sem, out_sem = refs[10:]
-    first, width = CHUNKS[0]
+    first, width = 0, WIDTH
     rest = TOKENS - EARLY
     loads = [pltpu.make_async_copy(weights_in, weights, sem.at[0])]
     row = 0
@@ -399,7 +460,7 @@
 
 
 def last_shared(weights, blocks, pair, tokens):
-    width = CHUNKS[0][1]
+    width = WIDTH
     return pl.pallas_call(
         last_shared_kernel,
         out_shape=[
@@ -426,78 +487,86 @@
 
 
 def column_spec(c):
-    first, width = CHUNKS[c]
-    return pl.BlockSpec((HELD, width), lambda j: (0, first // width))
-
-
-def token_spec(c):
-    first, width = CHUNKS[c]
-    return pl.BlockSpec((2, TOKENS, width), lambda j: (0, 0, first // width))
-
-
-def pair_spec(c):
-    return pl.BlockSpec((2, HELD, CHUNKS[c][1]), lambda j: (0, 0, 0))
+    return pl.BlockSpec((HELD, WIDTH), lambda j: (0, c))
+
+
+pair_spec = pl.BlockSpec((2, HELD, WIDTH), lambda j: (0, 0, 0))
 
 
 def rows_spec(tokens):
     return pl.BlockSpec((2, HELD, tokens), lambda j: (0, 0, 0))
 
 
-def theirs_kernel(pair, tokens, *refs):
-    def step(which, carry):
+def theirs_kernel(count, skipped, pair, tokens, *refs):
+    outs = refs[skipped : skipped + count]
+    held, sem = refs[-2:]
+    j = pl.program_id(0)
+    slot = j % 2
+
+    @pl.when(j >= 2)
+    def _():
+        pltpu.make_async_copy(held.at[slot], outs[0], sem.at[slot]).wait()
+
+    def multiply(which, carry):
         scale = jnp.where(which == 0, up_scale, down_scale)
         grad = jnp.dot(pair[which], tokens[which], preferred_element_type=jnp.float32)
-        refs[-1][which] = (scale * grad).astype(jnp.bfloat16)
+        held[slot, which] = (scale * grad).astype(jnp.bfloat16)
         return carry
 
-    lax.fori_loop(0, 2, step, 0)
-
-
-def theirs_chunk(c, pair, tokens, after):
-    width = CHUNKS[c][1]
-    return pl.pallas_call(
-        theirs_kernel,
-        out_shape=jax.ShapeDtypeStruct((2, HELD, width), jnp.bfloat16),
-        grid=(1,),
-        in_specs=[rows_spec(TOKENS), token_spec(c)] + [ANY] * len(after),
-        out_specs=pair_spec(c),
+    lax.fori_loop(0, 2, multiply, 0)
+    for k, out in enumerate(outs):
+
+        @pl.when(j == k)
+        def _(out=out):
+            pltpu.make_async_copy(held.at[slot], out, sem.at[slot]).start()
+
+    @pl.when(j == count - 1)
+    def _():
+        for last in range(max(count - 2, 0), count):
+            pltpu.make_async_copy(held.at[last % 2], outs[last], sem.at[last % 2]).wait()
+
+
+def theirs_chunks(first, count, pair, tokens, after):
+    return pl.pallas_call(
+        functools.partial(theirs_kernel, count, len(after)),
+        out_shape=[jax.ShapeDtypeStruct((2, HELD, WIDTH), jnp.bfloat16)] * count,
+        grid=(count,),
+        in_specs=[rows_spec(TOKENS), pl.BlockSpec((2, TOKENS, WIDTH), lambda j: (0, 0, j + first))]
+        + [ANY] * len(after),
+        out_specs=[ANY] * count,
+        scratch_shapes=[
+            pltpu.VMEM((2, 2, HELD, WIDTH), jnp.bfloat16),
+            pltpu.SemaphoreType.DMA((2,)),
+        ],
         compiler_params=vmem(22),
-        cost_estimate=cost(4 * HELD * TOKENS * width, 4 * TOKENS * (HELD + width)),
+        cost_estimate=cost(4 * HELD * TOKENS * count * WIDTH, 4 * TOKENS * (HELD + count * WIDTH)),
     )(pair, tokens, *after)
 
 
 def adam_kernel(mixing, *refs):
-    pair, pair_last, tokens, bias, arrived = refs[:5]
-    state = refs[5:11]
-    outs = refs[-8:-1]
-    grads = refs[-1]
-
-    def multiply(which, carry):
-        scale = jnp.where(which == 0, up_scale, down_scale)
-        early = jnp.dot(pair[which], tokens[which, :EARLY], preferred_element_type=jnp.float32)
-        late = jnp.dot(pair_last[which], tokens[which, EARLY:], preferred_element_type=jnp.float32)
-        grads[which] = scale * (early + late)
-        return carry
-
-    lax.fori_loop(0, 2, multiply, 0)
+    own, bias, arrived = refs[:3]
+    state = refs[3:9]
+    outs = refs[-7 - mixing[1] :]
     tile = 32
 
     def step(i, carry):
         at = pl.ds(pl.multiple_of(i * tile, tile), tile)
         for which in (0, 1):
             weight, first, second = (ref[at] for ref in state[3 * which : 3 * which + 3])
-            grad = grads[which, at] + arrived[which, at].astype(jnp.float32)
+            scale = (up_scale, down_scale)[which]
+            grad = scale * own[0, which, at] + arrived[which, at].astype(jnp.float32)
             first_new = beta_one * first.astype(jnp.float32) + (1.0 - beta_one) * grad
             second_new = beta_two * second.astype(jnp.float32) + (1.0 - beta_two) * grad * grad
             update = (learn_rate * bias[0]) * first_new / (jnp.sqrt(second_new * bias[1]) + adam_eps)
             outs[0][which, at] = (weight.astype(jnp.float32) - update).astype(jnp.bfloat16)
             outs[1 + 2 * which][at] = first_new.astype(jnp.bfloat16)
             outs[2 + 2 * which][at] = second_new.astype(jnp.bfloat16)
+            if mixing[0]:
+                both = refs[9][which, at].astype(jnp.float32) + refs[10][which, at].astype(jnp.float32)
+                outs[5 + which][at] = (both * 0.5).astype(jnp.bfloat16)
         return carry
 
     lax.fori_loop(0, HELD // tile, step, 0)
-    if mixing:
-        mix_kernel(refs[11], refs[12], *outs[-2:])
 
 
 def mix_kernel(own, other, *refs):
@@ -516,28 +585,31 @@
 whole = jax.ShapeDtypeStruct((HELD, D), jnp.bfloat16)
 
 
-def adam_chunk(c, sides, tokens, bias, arrived, state, mixed, results):
-    width = CHUNKS[c][1]
-    operands = [*sides, tokens, bias, arrived, *state, *mixed]
+def adam_chunk(c, own, bias, arrived, state, mixed, results, passing):
+    operands = [own[0], bias, arrived, *state, *mixed]
     aliases = {len(operands) + k: 1 + k for k in range(len(results))}
+    operands += results
+    if passing:
+        aliases[len(operands)] = 7
+        operands += passing
     before = max(c - 2, 0)
-    mixing = [column_spec(before)] * 2 if mixed or not results else []
-    early, last = rows_spec(EARLY), rows_spec(TOKENS - EARLY)
+    mixing = [column_spec(before)] * 2 if mixed or not results else [ANY] * 2
+    block, place = (1, 2, HELD, WIDTH), own[1]
     smem = pl.BlockSpec(memory_space=pltpu.SMEM)
-    return pl.pallas_call(
-        functools.partial(adam_kernel, bool(mixed)),
-        out_shape=[jax.ShapeDtypeStruct((2, HELD, width), jnp.bfloat16)] + [whole] * 6,
+    pair = jax.ShapeDtypeStruct((2, HELD, WIDTH), jnp.bfloat16)
+    return pl.pallas_call(
+        functools.partial(adam_kernel, (bool(mixed), len(passing))),
+        out_shape=[pair] + [whole] * 6 + [pair] * len(passing),
         grid=(1,),
-        in_specs=[early, last, token_spec(c), smem, pair_spec(c)]
+        in_specs=[pl.BlockSpec(block, lambda j: (place, 0, 0, 0)), smem, pair_spec]
         + [column_spec(c)] * 6
-        + [pair_spec(before)] * len(mixed)
-        + [ANY] * len(results),
-        out_specs=[pair_spec(c)] + [column_spec(c)] * 4 + (mixing or [ANY] * 2),
+        + [pair_spec] * len(mixed)
+        + [ANY] * (len(results) + len(passing)),
+        out_specs=[pair_spec] + [column_spec(c)] * 4 + mixing + [ANY] * len(passing),
         input_output_aliases=aliases,
-        scratch_shapes=[pltpu.VMEM((2, HELD, width), jnp.float32)],
         compiler_params=vmem(22),
-        cost_estimate=cost(4 * HELD * TOKENS * width, 4 * TOKENS * (HELD + width) + 36 * HELD * width),
-    )(*operands, *results)
+        cost_estimate=cost(0, 60 * HELD * WIDTH),
+    )(*operands)
 
 
 def mix_chunk(c, own, other, results):
@@ -545,11 +617,11 @@
         mix_kernel,
         out_shape=[whole] * 2,
         grid=(1,),
-        in_specs=[pair_spec(c)] * 2 + [ANY] * 2,
+        in_specs=[pair_spec] * 2 + [ANY] * 2,
         out_specs=[column_spec(c)] * 2,
         input_output_aliases={2: 0, 3: 1},
         compiler_params=vmem(22),
-        cost_estimate=cost(0, 12 * HELD * CHUNKS[c][1]),
+        cost_estimate=cost(0, 12 * HELD * WIDTH),
     )(own, other, *results)
 
 
@@ -613,21 +685,28 @@
     def finish(hop):
         route = [(g, (g + hop) % 4) for g in range(4)]
         news, updated, others = (), [], []
-        second = theirs_chunk(1, pair, tokens, [])
-        third = theirs_chunk(2, pair, tokens, [second])
-        sent = [moved(t, y_sharing) for t in (theirs, second, third)]
-        sides = [own_pair, last_own(up, down, tokens, [third])]
-        for c in range(len(CHUNKS)):
+        sent = [moved(theirs, y_sharing)]
+        more = theirs_chunks(1, 2, pair, tokens, [])
+        sent.append(moved(more[0], y_sharing))
+        own, last_pair = own_first(up, down, tokens, own_pair, more[:1])
+        place = [(own, c) for c in range(FIRST_OWN)]
+        for c in range(CHUNKS):
             mixed = [updated[c - 2], others[c - 2]] if 2 <= c < MIXING else []
-            out = adam_chunk(c, sides, tokens, bias, sent[c], state, mixed, news)
+            passing = more[c + 1 : c + 2]
+            out = adam_chunk(c, place[c], bias, sent[c], state, mixed, news, passing)
             updated.append(out[0])
-            news = out[1:]
+            news = out[1:7]
             others.append(lax.ppermute(out[0], "rep", route))
-            if 3 <= c + 2 < len(CHUNKS):
-                more = theirs_chunk(c + 2, pair, tokens, [out[0]])
-                sent.append(moved(more, y_sharing))
+            if passing:
+                sent.append(moved(out[7], y_sharing))
+            if c == 0:
+                more += theirs_chunks(3, CHUNKS - 3, pair, tokens, [out[0]])
+            for after, first, count in OWN_LATER:
+                if c == after:
+                    own = own_rest(first, count, own_pair, last_pair, tokens, [out[0]])
+                    place += [(own, k) for k in range(count)]
         mixed = news[4:]
-        for c in range(MIXING - 2, len(CHUNKS)):
+        for c in range(MIXING - 2, CHUNKS):
             mixed = mix_chunk(c, updated[c], others[c], mixed)
         return mixed[0], mixed[1], news[0], news[2], news[1], news[3]
 

time: 217 us -> 196 us (0.903); the launches traced: 213 us -> 195 us
  loops' own time: 13 us -> 0.16 us
  starting transfers between devices: 48.7 us -> 41.9 us
  waiting for transfers between devices: 63.5 us -> 66.3 us
    another operation x1, loops' own time: 13 us -> 0.16 us  [on_device(): lax.cond(step_index[0] % 2 == 0, lambda: finish(1), lambda: finish(2))]
    ppermute x25 -> x24, waiting for transfers between devices: 51.2 us -> 59.4 us  [moved(): return lax.ppermute(block, 'fsdp', route)]
    ppermute x8 -> x7, waiting for transfers between devices: 12.2 us -> 6.94 us  [finish(): others.append(lax.ppermute(out[0], 'rep', route))]
    ppermute x25 -> x24, starting transfers between devices: 46.4 us -> 41.2 us  [moved(): return lax.ppermute(block, 'fsdp', route)]
    pallas_call x16 -> x12, Pallas kernels: 45.3 us -> 44.8 us  [the longest x7 18.4 us: adam_chunk(): pl.pallas_call(functools.partial(adam_kernel, (bool(mixed), len(passing))...]
  transfers between devices with their start and end apart: 33 -> 31, of which waited for: 21 -> 12; matrix products, arithmetic and copies ran while one was open for 0% -> 0% of each run, Pallas kernels for 35% -> 38%
where the time goes in v1:
time: 196 us; the launch traced here: 195 us
  Pallas kernels  84.1 us (43%)
  waiting for transfers between devices  66.3 us (34%)
  starting transfers between devices  41.9 us (21%)
    ppermute x24, waiting for transfers between devices, moved(): return lax.ppermute(block, 'fsdp', route)  59.4 us
    ppermute x24, starting transfers between devices, moved(): return lax.ppermute(block, 'fsdp', route)  41.2 us
    pallas_call x2, Pallas kernels, hidden_step(): pl.pallas_call(functools.partial(hidden_kernel, jobs, sizes, pieces, skip...  21.9 us
    pallas_call x7, Pallas kernels, adam_chunk(): pl.pallas_call(functools.partial(adam_kernel, (bool(mixed), len(passing))...  18.4 us
    pallas_call x2, Pallas kernels, theirs_chunks(): pl.pallas_call(functools.partial(theirs_kernel, count, len(after)), out_s...  13 us
    pallas_call x2, Pallas kernels, own_rest(): pl.pallas_call(kernel, out_shape=jax.ShapeDtypeStruct((count, 2, HELD, WI...  7.21 us
    ppermute x7, waiting for transfers between devices, finish(): others.append(lax.ppermute(out[0], 'rep', route))  6.94 us
    pallas_call x1, Pallas kernels, last_shared(): pl.pallas_call(last_shared_kernel, out_shape=[jax.ShapeDtypeStruct((2, HE...  6.4 us
  transfers between devices with their start and end apart: 31, of which 12 were waited for; matrix products, arithmetic and copies ran while one was open for 0% of the time, Pallas kernels for 38%

profile of v1, /device:TPU:0, one launch (start us, length us, event | category | flops | bytes accessed | tf_op | source)
XLA Modules:
  0.0 195.4 jit_solution(16694161179166753252)
XLA Ops:
  0.7 3.0 %shard_map.136 = bf16[2,448,1792]{2,1,0:T(8,128)(2,1)} custom-call(bf16[448,1792]{1,0:T(8,128)(2,1)} %bitcast.23, bf16[448,1792]{1,0:T(8,128)(2,1)} %bitcast.28), custom_call_target="tpu_custom_call" | custom-call | bytes 6422528 | tf_op jit(solution)/shard_map/pallas_call | solution.py:154
  6.5 3.1 %collective-permute-start.29 = (bf16[2,64,1792]{2,1,0:T(8,128)(2,1)S(1)}, bf16[2,64,1792]{2,1,0:T(8,128)(2,1)S(1)}, u32[]{:S(2)}, u32[]{:S(2)}) collective-permute-start(bf16[2,64,1792]{2,1,0:T(8,128)(2,1)S(1)} %get-tuple-element.225.refs_0_), channel_id=1, source_target_pairs={{0,4},{1,5},{2,6},{3,7},{4,0},{5,1},{6,2},{7,3},{8,12},{9,13},{10,... | collective-permute-start | bytes 1376264 | tf_op jit(solution)/shard_map/ppermute | solution.py:43
  15.8 4.2 %collective-permute-done.29.refs_1_ = bf16[2,64,1792]{2,1,0:T(8,128)(2,1)S(1)} collective-permute-done((bf16[2,64,1792]{2,1,0:T(8,128)(2,1)S(1)}, bf16[2,64,1792]{2,1,0:T(8,128)(2,1)S(1)}, u32[]{:S(2)}, u32[]{:S(2)}) %collective-permute-start.29) | collective-permute-done | bytes 458784 | tf_op jit(solution)/shard_map/ppermute | solution.py:43
  20.1 2.3 %collective-permute-start.31 = (bf16[2,32,1792]{2,1,0:T(8,128)(2,1)S(1)}, bf16[2,32,1792]{2,1,0:T(8,128)(2,1)S(1)}, u32[]{:S(2)}, u32[]{:S(2)}) collective-permute-start(bf16[2,32,1792]{2,1,0:T(8,128)(2,1)S(1)} %slice.16), channel_id=1, source_target_pairs={{0,3},{1,2},{2,1},{3,0},{4,7},{5,6},{6,5},{7,4},{8,11},{9,10},{10,... | collective-permute-start | bytes 688136 | tf_op jit(solution)/shard_map/ppermute | solution.py:43
  22.5 2.9 %collective-permute-start.32 = (bf16[2,32,1792]{2,1,0:T(8,128)(2,1)S(1)}, bf16[2,32,1792]{2,1,0:T(8,128)(2,1)S(1)}, u32[]{:S(2)}, u32[]{:S(2)}) collective-permute-start(bf16[2,32,1792]{2,1,0:T(8,128)(2,1)S(1)} %slice.17), channel_id=1, source_target_pairs={{0,4},{1,5},{2,6},{3,7},{4,0},{5,1},{6,2},{7,3},{8,12},{9,13},{10,... | collective-permute-start | bytes 688136 | tf_op jit(solution)/shard_map/ppermute | solution.py:43
  27.5 2.2 %collective-permute-start.38 = (bf16[2,32,1792]{2,1,0:T(8,128)(2,1)S(1)}, bf16[2,32,1792]{2,1,0:T(8,128)(2,1)S(1)}, u32[]{:S(2)}, u32[]{:S(2)}) collective-permute-start(bf16[2,32,1792]{2,1,0:T(8,128)(2,1)S(1)} %slice.19), channel_id=1, source_target_pairs={{0,24},{1,25},{2,26},{3,27},{4,28},{5,29},{6,30},{7,31},{8,0},{9,1... | collective-permute-start | bytes 688136 | tf_op jit(solution)/shard_map/ppermute | solution.py:43
  37.0 2.9 %collective-permute-start.39 = (bf16[2,256,1792]{2,1,0:T(8,128)(2,1)}, bf16[2,256,1792]{2,1,0:T(8,128)(2,1)}, u32[]{:S(2)}, u32[]{:S(2)}) collective-permute-start(bf16[2,256,1792]{2,1,0:T(8,128)(2,1)} %shard_map.139.refs_3_.refs_8_), channel_id=1, source_target_pairs={{0,4},{1,5},{2,6},{3,7},{4,0},{5,1},{6,2},{7,3},{8,12},{9,13},{10,... | collective-permute-start | bytes 5505032 | tf_op jit(solution)/shard_map/ppermute | solution.py:43
  41.8 5.2 %shard_map.140 = (bf16[2,448,1536]{2,1,0:T(8,128)(2,1)S(1)}, bf16[2,448,2048]{2,1,0:T(8,128)(2,1)}, bf16[2,2048,1792]{2,1,0:T(8,128)(2,1)}) custom-call(bf16[448,1792]{1,0:T(8,128)(2,1)} %bitcast.24, bf16[448,1792]{1,0:T(8,128)(2,1)} %bitcast.29, bf16[2,256,1792]{2,1,0:T(8,128)(2,1)} %shard_map.138.refs_2_.refs_7_, ...), custom_call_target="tpu_custom_call" | custom-call | flops 3288334336 | bytes 7798784 | tf_op jit(solution)/shard_map/pallas_call | solution.py:281
  47.0 26.2 %collective-permute-done.33.refs_0_.refs_3_ = bf16[2,256,1792]{2,1,0:T(8,128)(2,1)} collective-permute-done((bf16[2,256,1792]{2,1,0:T(8,128)(2,1)}, bf16[2,256,1792]{2,1,0:T(8,128)(2,1)}, u32[]{:S(2)}, u32[]{:S(2)}) %collective-permute-start.33) | collective-permute-done | bytes 1835040 | tf_op jit(solution)/shard_map/ppermute | solution.py:43
  73.2 4.4 %collective-permute-done.39.refs_2_.refs_5_ = bf16[2,256,1792]{2,1,0:T(8,128)(2,1)} collective-permute-done((bf16[2,256,1792]{2,1,0:T(8,128)(2,1)}, bf16[2,256,1792]{2,1,0:T(8,128)(2,1)}, u32[]{:S(2)}, u32[]{:S(2)}) %collective-permute-start.39) | collective-permute-done | bytes 1835040 | tf_op jit(solution)/shard_map/ppermute | solution.py:43
  77.7 2.6 %collective-permute-done.40.refs_3_.refs_6_ = bf16[2,256,1792]{2,1,0:T(8,128)(2,1)} collective-permute-done((bf16[2,256,1792]{2,1,0:T(8,128)(2,1)}, bf16[2,256,1792]{2,1,0:T(8,128)(2,1)}, u32[]{:S(2)}, u32[]{:S(2)}) %collective-permute-start.40) | collective-permute-done | bytes 1835040 | tf_op jit(solution)/shard_map/ppermute | solution.py:43
  80.3 2.2 %shard_map.141 = (bf16[2,128,1792]{2,1,0:T(8,128)(2,1)S(1)}, bf16[2,128,1792]{2,1,0:T(8,128)(2,1)S(1)}, bf16[2,128,1792]{2,1,0:T(8,128)(2,1)S(1)}, bf16[2,128,1792]{2,1,0:T(8,128)(2,1)S(1)}) custom-call(bf16[2,256,1792]{2,1,0:T(8,128)(2,1)} %collective-permute-done.33.refs_0_.refs_3_, bf16[2,256,1792]{2,1,0:T(8,128)(2,1)} %collective-permute-done.34.refs_1_.refs_4_, ...), custom_call_target="tpu_custom_call" | custom-call | bytes 7340032 | tf_op jit(solution)/shard_map/pallas_call | solution.py:200
  82.5 3.2 %collective-permute-start.42 = (bf16[2,128,1792]{2,1,0:T(8,128)(2,1)S(1)}, bf16[2,128,1792]{2,1,0:T(8,128)(2,1)S(1)}, u32[]{:S(2)}, u32[]{:S(2)}) collective-permute-start(bf16[2,128,1792]{2,1,0:T(8,128)(2,1)S(1)} %get-tuple-element.229), channel_id=1, source_target_pairs={{0,24},{1,25},{2,26},{3,27},{4,28},{5,29},{6,30},{7,31},{8,0},{9,1... | collective-permute-start | bytes 2752520 | tf_op jit(solution)/shard_map/ppermute | solution.py:43
  88.3 16.7 %shard_map.142 = (bf16[2,448,1536]{2,1,0:T(8,128)(2,1)S(1)}, bf16[2,448,2048]{2,1,0:T(8,128)(2,1)}, bf16[2,2048,1792]{2,1,0:T(8,128)(2,1)}) custom-call(bf16[448,1792]{1,0:T(8,128)(2,1)S(1)} %bitcast.25, bf16[448,1792]{1,0:T(8,128)(2,1)S(1)} %bitcast.30, ...), custom_call_target="tpu_custom_call", output_to_operand_aliasing={{0}: (9, {}), {1}: (10, {}), {2}: (11, {})} | custom-call | flops 16441671680 | bytes 22937600 | tf_op jit(solution)/shard_map/pallas_call | solution.py:281
  106.7 6.4 %shard_map.143 = (bf16[2,448,2048]{2,1,0:T(8,128)(2,1)}, bf16[2,2048,1792]{2,1,0:T(8,128)(2,1)}, bf16[2,448,256]{2,1,0:T(8,128)(2,1)S(1)}) custom-call(bf16[2,448,1792]{2,1,0:T(8,128)(2,1)S(1)} %collective-permute-done.28.refs_2_.refs_0_, bf16[2,128,1792]{2,1,0:T(8,128)(2,1)S(1)} %collective-permute-done.41.refs_1_, ...), custom_call_target="tpu_custom_call", output_to_operand_aliasing={{0}: (5, {}), {1}: (6, {})} | custom-call | flops 5167382528 | bytes 6881280 | tf_op jit(solution)/shard_map/pallas_call | solution.py:464
  113.3 82.1 %conditional.1 = (bf16[448,1792]{1,0:T(8,128)(2,1)}, bf16[448,1792]{1,0:T(8,128)(2,1)}, bf16[448,1792]{1,0:T(8,128)(2,1)}, bf16[448,1792]{1,0:T(8,128)(2,1)}, bf...) conditional(s32[]{:T(128)} %convert_element_type.6, (bf16[2,448,2048]{2,1,0:T(8,128)(2,1)}, ...), branch_computations={%region_0.1_spmd, %region_1.2_spmd} | conditional | flops 27715960832 | bytes 194642512 | solution.py:713
  113.5 6.0 %branch_1_fun.14 = (bf16[2,448,256]{2,1,0:T(8,128)(2,1)S(1)}, bf16[2,448,256]{2,1,0:T(8,128)(2,1)S(1)}) custom-call(bf16[2,448,2048]{2,1,0:T(8,128)(2,1)} %get-tuple-element.125.pair, bf16[2,2048,1792]{2,1,0:T(8,128)(2,1)} %get-tuple-element.124.tokens.tokens_in.refs_2_), custom_call_target="tpu_custom_call" | custom-call | flops 3758096384 | bytes 7864320 | tf_op jit(solution)/shard_map/cond/branch_1_fun/pallas_call | solution.py:530
  121.6 6.2 %branch_1_fun.15 = (f32[2,2,448,256]{3,2,1,0:T(8,128)S(1)}, bf16[2,448,512]{2,1,0:T(8,128)(2,1)S(1)}) custom-call(bf16[448,1792]{1,0:T(8,128)(2,1)S(1)} %get-tuple-element.122.up.refs_3_, bf16[448,1792]{1,0:T(8,128)(2,1)S(1)} %get-tuple-element.123.down.refs_6_, bf16[2,2048,1792]{2,1,0:T(8,128)(2,1)S(1)} %copy-done.3, ...), custom_call_target="tpu_custom_call" | custom-call | flops 7046430720 | bytes 6881280 | tf_op jit(solution)/shard_map/cond/branch_1_fun/pallas_call | solution.py:352
  127.8 2.6 %branch_1_fun.16 = (bf16[2,448,256]{2,1,0:T(8,128)(2,1)S(1)}, bf16[448,1792]{1,0:T(8,128)(2,1)}, bf16[448,1792]{1,0:T(8,128)(2,1)}, bf16[448,1792]{1,0:T(8,128)(...) custom-call(f32[2,2,448,256]{3,2,1,0:T(8,128)S(1)} %get-tuple-elemen, ...), custom_call_target="tpu_custom_call", output_to_operand_aliasing={{7}: (9, {})} | custom-call | bytes 6881280 | tf_op jit(solution)/shard_map/cond/branch_1_fun/pallas_call | solution.py:600
  131.8 6.9 %branch_1_fun.17 = (bf16[2,448,256]{2,1,0:T(8,128)(2,1)S(1)}, bf16[2,448,256]{2,1,0:T(8,128)(2,1)S(1)}, bf16[2,448,256]{2,1,0:T(8,128)(2,1)S(1)}, bf16[2,448,256]{2,1,0:T(8,128)(2,1)S(1)}) custom-call(bf16[2,448,2048]{2,1,0:T(8,128)(2,1)S(1)} %copy-done.13, bf16[2,2048,1792]{2,1,0:T(8,128)(2,1)S(1)} %copy-done.3, ...), custom_call_target="tpu_custom_call" | custom-call | flops 7516192768 | bytes 12058624 | tf_op jit(solution)/shard_map/cond/branch_1_fun/pallas_call | solution.py:530
  138.8 2.5 %branch_1_fun.18 = (bf16[2,448,256]{2,1,0:T(8,128)(2,1)S(1)}, bf16[448,1792]{1,0:T(8,128)(2,1)}, bf16[448,1792]{1,0:T(8,128)(2,1)}, bf16[448,1792]{1,0:T(8,128)(...) custom-call(f32[2,2,448,256]{3,2,1,0:T(8,128)S(1)} %get-tuple-elemen, ...), custom_call_target="tpu_custom_call", output_to_operand_aliasing={{1}: (9, {}), {2}: (10, {}), {3}: (11, {}), {4}: (12, {}), ... | custom-call | bytes 6881280 | tf_op jit(solution)/shard_map/cond/branch_1_fun/pallas_call | solution.py:600
  142.3 2.9 %branch_1_fun.19.refs_0_ = f32[2,2,448,256]{3,2,1,0:T(8,128)S(1)} custom-call(bf16[2,448,1536]{2,1,0:T(8,128)(2,1)S(1)} %get-tuple-element.121.pair_in.refs_0_, bf16[2,448,512]{2,1,0:T(8,128)(2,1)S(1)} %get-tuple-element.127.refs_1_, bf16[2,2048,1792]{2,1,0:T(8,128)(2,1)S(1)} %copy-done.3, bf16[2,448,256]{2,1,0:T(8,128)(2,1)S(1)} %get-tuple-element.144.refs_3_.refs_9_), custom_call_target="tpu_custom_call" | custom-call | flops 3758096384 | bytes 7864320 | tf_op jit(solution)/shard_map/cond/branch_1_fun/pallas_call | solution.py:388
  145.2 2.7 %branch_1_fun.20 = (bf16[2,448,256]{2,1,0:T(8,128)(2,1)S(1)}, bf16[448,1792]{1,0:T(8,128)(2,1)}, bf16[448,1792]{1,0:T(8,128)(2,1)}, bf16[448,1792]{1,0:T(8,128)(...) custom-call(f32[2,2,448,256]{3,2,1,0:T(8,128)S(1)} %branch_1_fun.19., ...), custom_call_target="tpu_custom_call", output_to_operand_aliasing={{1}: (11, {}), {2}: (12, {}), {3}: (13, {}), {4}: (14, {}),... | custom-call | bytes 6881280 | tf_op jit(solution)/shard_map/cond/branch_1_fun/pallas_call | solution.py:600
  149.6 5.0 %collective-permute-done.20.refs_2_ = bf16[2,448,256]{2,1,0:T(8,128)(2,1)S(1)} collective-permute-done((bf16[2,448,256]{2,1,0:T(8,128)(2,1)S(1)}, bf16[2,448,256]{2,1,0:T(8,128)(2,1)S(1)}, u32[]{:S(2)}, u32[]{:S(2)}) %collective-permute-start.20) | collective-permute-done | bytes 458784 | tf_op jit(solution)/shard_map/cond/branch_1_fun/ppermute | solution.py:43
  154.6 2.7 %branch_1_fun.22 = (bf16[2,448,256]{2,1,0:T(8,128)(2,1)S(1)}, bf16[448,1792]{1,0:T(8,128)(2,1)}, bf16[448,1792]{1,0:T(8,128)(2,1)}, bf16[448,1792]{1,0:T(8,128)(...) custom-call(f32[2,2,448,256]{3,2,1,0:T(8,128)S(1)} %branch_1_fun.19., ...), custom_call_target="tpu_custom_call", output_to_operand_aliasing={{1}: (11, {}), {2}: (12, {}), {3}: (13, {}), {4}: (14, {}),... | custom-call | bytes 6881280 | tf_op jit(solution)/shard_map/cond/branch_1_fun/pallas_call | solution.py:600
  158.0 4.3 %branch_1_fun.21.refs_0_ = f32[3,2,448,256]{3,2,1,0:T(8,128)S(1)} custom-call(bf16[2,448,1536]{2,1,0:T(8,128)(2,1)S(1)} %get-tuple-element.121.pair_in.refs_0_, bf16[2,448,512]{2,1,0:T(8,128)(2,1)S(1)} %get-tuple-element.127.refs_1_, bf16[2,2048,1792]{2,1,0:T(8,128)(2,1)S(1)} %copy-done.3, bf16[2,448,256]{2,1,0:T(8,128)(2,1)S(1)} %get-tuple-element.153.refs_3_.refs_9_), custom_call_target="tpu_custom_call" | custom-call | flops 5637144576 | bytes 9961472 | tf_op jit(solution)/shard_map/cond/branch_1_fun/pallas_call | solution.py:388
  164.5 2.7 %branch_1_fun.23 = (bf16[2,448,256]{2,1,0:T(8,128)(2,1)S(1)}, bf16[448,1792]{1,0:T(8,128)(2,1)}, bf16[448,1792]{1,0:T(8,128)(2,1)}, bf16[448,1792]{1,0:T(8,128)(...) custom-call(f32[3,2,448,256]{3,2,1,0:T(8,128)S(1)} %branch_1_fun.21., ...), custom_call_target="tpu_custom_call", output_to_operand_aliasing={{1}: (11, {}), {2}: (12, {}), {3}: (13, {}), {4}: (14, {}),... | custom-call | bytes 6881280 | tf_op jit(solution)/shard_map/cond/branch_1_fun/pallas_call | solution.py:600
  167.8 6.5 %collective-permute-done.24.refs_2_ = bf16[2,448,256]{2,1,0:T(8,128)(2,1)S(1)} collective-permute-done((bf16[2,448,256]{2,1,0:T(8,128)(2,1)S(1)}, bf16[2,448,256]{2,1,0:T(8,128)(2,1)S(1)}, u32[]{:S(2)}, u32[]{:S(2)}) %collective-permute-start.24) | collective-permute-done | bytes 458784 | tf_op jit(solution)/shard_map/cond/branch_1_fun/ppermute | solution.py:43
  174.3 2.7 %branch_1_fun.24 = (bf16[2,448,256]{2,1,0:T(8,128)(2,1)S(1)}, bf16[448,1792]{1,0:T(8,128)(2,1)}, bf16[448,1792]{1,0:T(8,128)(2,1)}, bf16[448,1792]{1,0:T(8,128)(...) custom-call(f32[3,2,448,256]{3,2,1,0:T(8,128)S(1)} %branch_1_fun.21., ...), custom_call_target="tpu_custom_call", output_to_operand_aliasing={{1}: (11, {}), {2}: (12, {}), {3}: (13, {}), {4}: (14, {}),... | custom-call | bytes 6881280 | tf_op jit(solution)/shard_map/cond/branch_1_fun/pallas_call | solution.py:600
  176.9 6.9 %collective-permute-done.22.refs_2_ = bf16[2,448,256]{2,1,0:T(8,128)(2,1)S(1)} collective-permute-done((bf16[2,448,256]{2,1,0:T(8,128)(2,1)S(1)}, bf16[2,448,256]{2,1,0:T(8,128)(2,1)S(1)}, u32[]{:S(2)}, u32[]{:S(2)}) %collective-permute-start.22) | collective-permute-done | bytes 458784 | tf_op jit(solution)/shard_map/cond/branch_1_fun/ppermute | solution.py:43
  183.9 2.7 %branch_1_fun.25 = (bf16[2,448,256]{2,1,0:T(8,128)(2,1)S(1)}, bf16[448,1792]{1,0:T(8,128)(2,1)}, bf16[448,1792]{1,0:T(8,128)(2,1)}, bf16[448,1792]{1,0:T(8,128)(...) custom-call(f32[3,2,448,256]{3,2,1,0:T(8,128)S(1)} %branch_1_fun.21., ...), custom_call_target="tpu_custom_call", output_to_operand_aliasing={{1}: (11, {}), {2}: (12, {}), {3}: (13, {}), {4}: (14, {}),... | custom-call | bytes 6881280 | tf_op jit(solution)/shard_map/cond/branch_1_fun/pallas_call | solution.py:600
  187.5 6.9 %collective-permute-done.26.other = bf16[2,448,256]{2,1,0:T(8,128)(2,1)S(1)} collective-permute-done((bf16[2,448,256]{2,1,0:T(8,128)(2,1)S(1)}, bf16[2,448,256]{2,1,0:T(8,128)(2,1)S(1)}, u32[]{:S(2)}, u32[]{:S(2)}) %collective-permute-start.26) | collective-permute-done | bytes 458784 | tf_op jit(solution)/shard_map/cond/branch_1_fun/ppermute | solution.py:699
  (82 shorter events, 35.9 us)
Async XLA Ops:
  3.7 84.6 %collective-permute-start.28 = (bf16[2,448,1792]{2,1,0:T(8,128)(2,1)}, bf16[2,448,1792]{2,1,0:T(8,128)(2,1)S(1)}, u32[]{:S(2)}, u32[]{:S(2)}) collective-permute-start(bf16[2,448,1792]{2,1,0:T(8,128)(2,1)} %shard_map.136), channel_id=1, source_target_pairs={{0,1},{1,0},{2,3},{3,2},{4,5},{5,4},{6,7},{7,6},{8,9},{9,8},{10,11... | collective-permute-start | bytes 9633800 | tf_op jit(solution)/shard_map/ppermute | solution.py:43
  6.5 13.6 %collective-permute-start.29 = (bf16[2,64,1792]{2,1,0:T(8,128)(2,1)S(1)}, bf16[2,64,1792]{2,1,0:T(8,128)(2,1)S(1)}, u32[]{:S(2)}, u32[]{:S(2)}) collective-permute-start(bf16[2,64,1792]{2,1,0:T(8,128)(2,1)S(1)} %get-tuple-element.225.refs_0_), channel_id=1, source_target_pairs={{0,4},{1,5},{2,6},{3,7},{4,0},{5,1},{6,2},{7,3},{8,12},{9,13},{10,... | collective-permute-start | bytes 1376264 | tf_op jit(solution)/shard_map/ppermute | solution.py:43
  9.6 12.9 %collective-permute-start.30 = (bf16[2,64,1792]{2,1,0:T(8,128)(2,1)S(1)}, bf16[2,64,1792]{2,1,0:T(8,128)(2,1)S(1)}, u32[]{:S(2)}, u32[]{:S(2)}) collective-permute-start(bf16[2,64,1792]{2,1,0:T(8,128)(2,1)S(1)} %get-tuple-element.225.refs_0_), channel_id=1, source_target_pairs={{0,3},{1,2},{2,1},{3,0},{4,7},{5,6},{6,5},{7,4},{8,11},{9,10},{10,... | collective-permute-start | bytes 1376264 | tf_op jit(solution)/shard_map/ppermute | solution.py:43
  11.8 13.7 %collective-permute-start.35 = (bf16[2,64,1792]{2,1,0:T(8,128)(2,1)S(1)}, bf16[2,64,1792]{2,1,0:T(8,128)(2,1)S(1)}, u32[]{:S(2)}, u32[]{:S(2)}) collective-permute-start(bf16[2,64,1792]{2,1,0:T(8,128)(2,1)S(1)} %get-tuple-element.226.refs_0_), channel_id=1, source_target_pairs={{0,8},{1,9},{2,10},{3,11},{4,12},{5,13},{6,14},{7,15},{8,16},{9,17... | collective-permute-start | bytes 1376264 | tf_op jit(solution)/shard_map/ppermute | solution.py:43
  13.7 13.8 %collective-permute-start.36 = (bf16[2,64,1792]{2,1,0:T(8,128)(2,1)S(1)}, bf16[2,64,1792]{2,1,0:T(8,128)(2,1)S(1)}, u32[]{:S(2)}, u32[]{:S(2)}) collective-permute-start(bf16[2,64,1792]{2,1,0:T(8,128)(2,1)S(1)} %get-tuple-element.226.refs_0_), channel_id=1, source_target_pairs={{0,24},{1,25},{2,26},{3,27},{4,28},{5,29},{6,30},{7,31},{8,0},{9,1... | collective-permute-start | bytes 1376264 | tf_op jit(solution)/shard_map/ppermute | solution.py:43
  20.1 9.6 %collective-permute-start.31 = (bf16[2,32,1792]{2,1,0:T(8,128)(2,1)S(1)}, bf16[2,32,1792]{2,1,0:T(8,128)(2,1)S(1)}, u32[]{:S(2)}, u32[]{:S(2)}) collective-permute-start(bf16[2,32,1792]{2,1,0:T(8,128)(2,1)S(1)} %slice.16), channel_id=1, source_target_pairs={{0,3},{1,2},{2,1},{3,0},{4,7},{5,6},{6,5},{7,4},{8,11},{9,10},{10,... | collective-permute-start | bytes 688136 | tf_op jit(solution)/shard_map/ppermute | solution.py:43
  22.5 7.6 %collective-permute-start.32 = (bf16[2,32,1792]{2,1,0:T(8,128)(2,1)S(1)}, bf16[2,32,1792]{2,1,0:T(8,128)(2,1)S(1)}, u32[]{:S(2)}, u32[]{:S(2)}) collective-permute-start(bf16[2,32,1792]{2,1,0:T(8,128)(2,1)S(1)} %slice.17), channel_id=1, source_target_pairs={{0,4},{1,5},{2,6},{3,7},{4,0},{5,1},{6,2},{7,3},{8,12},{9,13},{10,... | collective-permute-start | bytes 688136 | tf_op jit(solution)/shard_map/ppermute | solution.py:43
  25.5 10.0 %collective-permute-start.37 = (bf16[2,32,1792]{2,1,0:T(8,128)(2,1)S(1)}, bf16[2,32,1792]{2,1,0:T(8,128)(2,1)S(1)}, u32[]{:S(2)}, u32[]{:S(2)}) collective-permute-start(bf16[2,32,1792]{2,1,0:T(8,128)(2,1)S(1)} %slice.18), channel_id=1, source_target_pairs={{0,8},{1,9},{2,10},{3,11},{4,12},{5,13},{6,14},{7,15},{8,16},{9,17... | collective-permute-start | bytes 688136 | tf_op jit(solution)/shard_map/ppermute | solution.py:43
  27.5 8.0 %collective-permute-start.38 = (bf16[2,32,1792]{2,1,0:T(8,128)(2,1)S(1)}, bf16[2,32,1792]{2,1,0:T(8,128)(2,1)S(1)}, u32[]{:S(2)}, u32[]{:S(2)}) collective-permute-start(bf16[2,32,1792]{2,1,0:T(8,128)(2,1)S(1)} %slice.19), channel_id=1, source_target_pairs={{0,24},{1,25},{2,26},{3,27},{4,28},{5,29},{6,30},{7,31},{8,0},{9,1... | collective-permute-start | bytes 688136 | tf_op jit(solution)/shard_map/ppermute | solution.py:43
  31.5 41.7 %collective-permute-start.33 = (bf16[2,256,1792]{2,1,0:T(8,128)(2,1)}, bf16[2,256,1792]{2,1,0:T(8,128)(2,1)}, u32[]{:S(2)}, u32[]{:S(2)}) collective-permute-start(bf16[2,256,1792]{2,1,0:T(8,128)(2,1)} %shard_map.138.refs_2_.refs_7_), channel_id=1, source_target_pairs={{0,8},{1,9},{2,10},{3,11},{4,12},{5,13},{6,14},{7,15},{8,16},{9,17... | collective-permute-start | bytes 5505032 | tf_op jit(solution)/shard_map/ppermute | solution.py:43
  33.4 39.8 %collective-permute-start.34 = (bf16[2,256,1792]{2,1,0:T(8,128)(2,1)}, bf16[2,256,1792]{2,1,0:T(8,128)(2,1)}, u32[]{:S(2)}, u32[]{:S(2)}) collective-permute-start(bf16[2,256,1792]{2,1,0:T(8,128)(2,1)} %shard_map.138.refs_2_.refs_7_), channel_id=1, source_target_pairs={{0,24},{1,25},{2,26},{3,27},{4,28},{5,29},{6,30},{7,31},{8,0},{9,1... | collective-permute-start | bytes 5505032 | tf_op jit(solution)/shard_map/ppermute | solution.py:43
  37.0 40.7 %collective-permute-start.39 = (bf16[2,256,1792]{2,1,0:T(8,128)(2,1)}, bf16[2,256,1792]{2,1,0:T(8,128)(2,1)}, u32[]{:S(2)}, u32[]{:S(2)}) collective-permute-start(bf16[2,256,1792]{2,1,0:T(8,128)(2,1)} %shard_map.139.refs_3_.refs_8_), channel_id=1, source_target_pairs={{0,4},{1,5},{2,6},{3,7},{4,0},{5,1},{6,2},{7,3},{8,12},{9,13},{10,... | collective-permute-start | bytes 5505032 | tf_op jit(solution)/shard_map/ppermute | solution.py:43
  39.9 40.4 %collective-permute-start.40 = (bf16[2,256,1792]{2,1,0:T(8,128)(2,1)}, bf16[2,256,1792]{2,1,0:T(8,128)(2,1)}, u32[]{:S(2)}, u32[]{:S(2)}) collective-permute-start(bf16[2,256,1792]{2,1,0:T(8,128)(2,1)} %shard_map.139.refs_3_.refs_8_), channel_id=1, source_target_pairs={{0,3},{1,2},{2,1},{3,0},{4,7},{5,6},{6,5},{7,4},{8,11},{9,10},{10,... | collective-permute-start | bytes 5505032 | tf_op jit(solution)/shard_map/ppermute | solution.py:43
  82.5 22.6 %collective-permute-start.41 = (bf16[2,128,1792]{2,1,0:T(8,128)(2,1)S(1)}, bf16[2,128,1792]{2,1,0:T(8,128)(2,1)S(1)}, u32[]{:S(2)}, u32[]{:S(2)}) collective-permute-start(bf16[2,128,1792]{2,1,0:T(8,128)(2,1)S(1)} %get-tuple-element.228.refs_12_), channel_id=1, source_target_pairs={{0,8},{1,9},{2,10},{3,11},{4,12},{5,13},{6,14},{7,15},{8,16},{9,17... | collective-permute-start | bytes 2752520 | tf_op jit(solution)/shard_map/ppermute | solution.py:43
  82.5 22.5 %collective-permute-start.42 = (bf16[2,128,1792]{2,1,0:T(8,128)(2,1)S(1)}, bf16[2,128,1792]{2,1,0:T(8,128)(2,1)S(1)}, u32[]{:S(2)}, u32[]{:S(2)}) collective-permute-start(bf16[2,128,1792]{2,1,0:T(8,128)(2,1)S(1)} %get-tuple-element.229), channel_id=1, source_target_pairs={{0,24},{1,25},{2,26},{3,27},{4,28},{5,29},{6,30},{7,31},{8,0},{9,1... | collective-permute-start | bytes 2752520 | tf_op jit(solution)/shard_map/ppermute | solution.py:43
  85.8 19.3 %collective-permute-start.43 = (bf16[2,128,1792]{2,1,0:T(8,128)(2,1)S(1)}, bf16[2,128,1792]{2,1,0:T(8,128)(2,1)S(1)}, u32[]{:S(2)}, u32[]{:S(2)}) collective-permute-start(bf16[2,128,1792]{2,1,0:T(8,128)(2,1)S(1)} %get-tuple-element.230), channel_id=1, source_target_pairs={{0,3},{1,2},{2,1},{3,0},{4,7},{5,6},{6,5},{7,4},{8,11},{9,10},{10,... | collective-permute-start | bytes 2752520 | tf_op jit(solution)/shard_map/ppermute | solution.py:43
  86.8 18.9 %collective-permute-start.44 = (bf16[2,128,1792]{2,1,0:T(8,128)(2,1)S(1)}, bf16[2,128,1792]{2,1,0:T(8,128)(2,1)S(1)}, u32[]{:S(2)}, u32[]{:S(2)}) collective-permute-start(bf16[2,128,1792]{2,1,0:T(8,128)(2,1)S(1)} %get-tuple-element.231), channel_id=1, source_target_pairs={{0,4},{1,5},{2,6},{3,7},{4,0},{5,1},{6,2},{7,3},{8,12},{9,13},{10,... | collective-permute-start | bytes 2752520 | tf_op jit(solution)/shard_map/ppermute | solution.py:43
  113.4 14.5 %collective-permute-start.15 = (bf16[2,448,256]{2,1,0:T(8,128)(2,1)S(1)}, bf16[2,448,256]{2,1,0:T(8,128)(2,1)S(1)}, u32[]{:S(2)}, u32[]{:S(2)}) collective-permute-start(bf16[2,448,256]{2,1,0:T(8,128)(2,1)S(1)} %get-tuple-element.134), channel_id=1, source_target_pairs={{0,1},{1,0},{2,3},{3,2},{4,5},{5,4},{6,7},{7,6},{8,9},{9,8},{10,11... | collective-permute-start | bytes 1376264 | tf_op jit(solution)/shard_map/cond/branch_1_fun/ppermute | solution.py:43
  113.4 8.1 %copy-start.3 = (bf16[2,2048,1792]{2,1,0:T(8,128)(2,1)S(1)}, bf16[2,2048,1792]{2,1,0:T(8,128)(2,1)}, u32[]{:S(2)}) copy-start(bf16[2,2048,1792]{2,1,0:T(8,128)(2,1)} %get-tuple-element.124.tokens.tokens_in.refs_2_) | copy-start | bytes 44040196 | tf_op jit(solution)/shard_map/cond
  119.5 19.3 %collective-permute-start.14 = (bf16[2,448,256]{2,1,0:T(8,128)(2,1)S(1)}, bf16[2,448,256]{2,1,0:T(8,128)(2,1)S(1)}, u32[]{:S(2)}, u32[]{:S(2)}) collective-permute-start(bf16[2,448,256]{2,1,0:T(8,128)(2,1)S(1)} %get-tuple-element.126.refs_0_), channel_id=1, source_target_pairs={{0,1},{1,0},{2,3},{3,2},{4,5},{5,4},{6,7},{7,6},{8,9},{9,8},{10,11... | collective-permute-start | bytes 1376264 | tf_op jit(solution)/shard_map/cond/branch_1_fun/ppermute | solution.py:43
  130.4 14.8 %collective-permute-start.17 = (bf16[2,448,256]{2,1,0:T(8,128)(2,1)S(1)}, bf16[2,448,256]{2,1,0:T(8,128)(2,1)S(1)}, u32[]{:S(2)}, u32[]{:S(2)}) collective-permute-start(bf16[2,448,256]{2,1,0:T(8,128)(2,1)S(1)} %get-tuple-element.142.refs_0_.refs_9_), channel_id=1, source_target_pairs={{0,32},{32,64},{64,96},{96,0},{1,33},{33,65},{65,97},{97,1},{2,34}... | collective-permute-start | bytes 1376264 | tf_op jit(solution)/shard_map/cond/branch_1_fun/ppermute | solution.py:699
  130.4 14.8 %collective-permute-start.16 = (bf16[2,448,256]{2,1,0:T(8,128)(2,1)S(1)}, bf16[2,448,256]{2,1,0:T(8,128)(2,1)S(1)}, u32[]{:S(2)}, u32[]{:S(2)}) collective-permute-start(bf16[2,448,256]{2,1,0:T(8,128)(2,1)S(1)} %get-tuple-element.145), channel_id=1, source_target_pairs={{0,1},{1,0},{2,3},{3,2},{4,5},{5,4},{6,7},{7,6},{8,9},{9,8},{10,11... | collective-permute-start | bytes 1376264 | tf_op jit(solution)/shard_map/cond/branch_1_fun/ppermute | solution.py:43
  141.2 13.4 %collective-permute-start.20 = (bf16[2,448,256]{2,1,0:T(8,128)(2,1)S(1)}, bf16[2,448,256]{2,1,0:T(8,128)(2,1)S(1)}, u32[]{:S(2)}, u32[]{:S(2)}) collective-permute-start(bf16[2,448,256]{2,1,0:T(8,128)(2,1)S(1)} %get-tuple-element.155), channel_id=1, source_target_pairs={{0,1},{1,0},{2,3},{3,2},{4,5},{5,4},{6,7},{7,6},{8,9},{9,8},{10,11... | collective-permute-start | bytes 1376264 | tf_op jit(solution)/shard_map/cond/branch_1_fun/ppermute | solution.py:43
  141.9 12.8 %collective-permute-start.21 = (bf16[2,448,256]{2,1,0:T(8,128)(2,1)S(1)}, bf16[2,448,256]{2,1,0:T(8,128)(2,1)S(1)}, u32[]{:S(2)}, u32[]{:S(2)}) collective-permute-start(bf16[2,448,256]{2,1,0:T(8,128)(2,1)S(1)} %get-tuple-element.144.refs_3_.refs_9_), channel_id=1, source_target_pairs={{0,32},{32,64},{64,96},{96,0},{1,33},{33,65},{65,97},{97,1},{2,34}... | collective-permute-start | bytes 1376264 | tf_op jit(solution)/shard_map/cond/branch_1_fun/ppermute | solution.py:699
  147.9 16.6 %collective-permute-start.18 = (bf16[2,448,256]{2,1,0:T(8,128)(2,1)S(1)}, bf16[2,448,256]{2,1,0:T(8,128)(2,1)S(1)}, u32[]{:S(2)}, u32[]{:S(2)}) collective-permute-start(bf16[2,448,256]{2,1,0:T(8,128)(2,1)S(1)} %get-tuple-element.154), channel_id=1, source_target_pairs={{0,1},{1,0},{2,3},{3,2},{4,5},{5,4},{6,7},{7,6},{8,9},{9,8},{10,11... | collective-permute-start | bytes 1376264 | tf_op jit(solution)/shard_map/cond/branch_1_fun/ppermute | solution.py:43
  149.3 15.2 %collective-permute-start.19 = (bf16[2,448,256]{2,1,0:T(8,128)(2,1)S(1)}, bf16[2,448,256]{2,1,0:T(8,128)(2,1)S(1)}, u32[]{:S(2)}, u32[]{:S(2)}) collective-permute-start(bf16[2,448,256]{2,1,0:T(8,128)(2,1)S(1)} %get-tuple-element.153.refs_3_.refs_9_), channel_id=1, source_target_pairs={{0,32},{32,64},{64,96},{96,0},{1,33},{33,65},{65,97},{97,1},{2,34}... | collective-permute-start | bytes 1376264 | tf_op jit(solution)/shard_map/cond/branch_1_fun/ppermute | solution.py:699
  157.3 17.0 %collective-permute-start.24 = (bf16[2,448,256]{2,1,0:T(8,128)(2,1)S(1)}, bf16[2,448,256]{2,1,0:T(8,128)(2,1)S(1)}, u32[]{:S(2)}, u32[]{:S(2)}) collective-permute-start(bf16[2,448,256]{2,1,0:T(8,128)(2,1)S(1)} %get-tuple-element.172), channel_id=1, source_target_pairs={{0,1},{1,0},{2,3},{3,2},{4,5},{5,4},{6,7},{7,6},{8,9},{9,8},{10,11... | collective-permute-start | bytes 1376264 | tf_op jit(solution)/shard_map/cond/branch_1_fun/ppermute | solution.py:43
  158.0 16.3 %collective-permute-start.25 = (bf16[2,448,256]{2,1,0:T(8,128)(2,1)S(1)}, bf16[2,448,256]{2,1,0:T(8,128)(2,1)S(1)}, u32[]{:S(2)}, u32[]{:S(2)}) collective-permute-start(bf16[2,448,256]{2,1,0:T(8,128)(2,1)S(1)} %get-tuple-element.173.refs_9_), channel_id=1, source_target_pairs={{0,32},{32,64},{64,96},{96,0},{1,33},{33,65},{65,97},{97,1},{2,34}... | collective-permute-start | bytes 1376264 | tf_op jit(solution)/shard_map/cond/branch_1_fun/ppermute | solution.py:699
  167.1 16.7 %collective-permute-start.22 = (bf16[2,448,256]{2,1,0:T(8,128)(2,1)S(1)}, bf16[2,448,256]{2,1,0:T(8,128)(2,1)S(1)}, u32[]{:S(2)}, u32[]{:S(2)}) collective-permute-start(bf16[2,448,256]{2,1,0:T(8,128)(2,1)S(1)} %get-tuple-element.170), channel_id=1, source_target_pairs={{0,1},{1,0},{2,3},{3,2},{4,5},{5,4},{6,7},{7,6},{8,9},{9,8},{10,11... | collective-permute-start | bytes 1376264 | tf_op jit(solution)/shard_map/cond/branch_1_fun/ppermute | solution.py:43
  167.8 16.1 %collective-permute-start.23 = (bf16[2,448,256]{2,1,0:T(8,128)(2,1)S(1)}, bf16[2,448,256]{2,1,0:T(8,128)(2,1)S(1)}, u32[]{:S(2)}, u32[]{:S(2)}) collective-permute-start(bf16[2,448,256]{2,1,0:T(8,128)(2,1)S(1)} %get-tuple-element.171.refs_9_), channel_id=1, source_target_pairs={{0,32},{32,64},{64,96},{96,0},{1,33},{33,65},{65,97},{97,1},{2,34}... | collective-permute-start | bytes 1376264 | tf_op jit(solution)/shard_map/cond/branch_1_fun/ppermute | solution.py:699
  176.9 9.6 %collective-permute-start.27 = (bf16[2,448,256]{2,1,0:T(8,128)(2,1)S(1)}, bf16[2,448,256]{2,1,0:T(8,128)(2,1)S(1)}, u32[]{:S(2)}, u32[]{:S(2)}) collective-permute-start(bf16[2,448,256]{2,1,0:T(8,128)(2,1)S(1)} %get-tuple-element.187.own), channel_id=1, source_target_pairs={{0,32},{32,64},{64,96},{96,0},{1,33},{33,65},{65,97},{97,1},{2,34}... | collective-permute-start | bytes 1376264 | tf_op jit(solution)/shard_map/cond/branch_1_fun/ppermute | solution.py:699
  186.5 7.9 %collective-permute-start.26 = (bf16[2,448,256]{2,1,0:T(8,128)(2,1)S(1)}, bf16[2,448,256]{2,1,0:T(8,128)(2,1)S(1)}, u32[]{:S(2)}, u32[]{:S(2)}) collective-permute-start(bf16[2,448,256]{2,1,0:T(8,128)(2,1)S(1)} %get-tuple-element.186.own), channel_id=1, source_target_pairs={{0,32},{32,64},{64,96},{96,0},{1,33},{33,65},{65,97},{97,1},{2,34}... | collective-permute-start | bytes 1376264 | tf_op jit(solution)/shard_map/cond/branch_1_fun/ppermute | solution.py:699
  (11 other events, 63.7 us)

commit v2 on v1

--- a/solution.py
+++ b/solution.py
@@ -125,7 +125,7 @@
         in_specs=[ANY] * 2,
         out_specs=[INSIDE] * 2,
         scratch_shapes=[pltpu.VMEM((ROWS, D), jnp.bfloat16), pltpu.SemaphoreType.DMA((3,))],
-        compiler_params=vmem(16),
+        compiler_params=vmem(8),
         cost_estimate=cost(0, 8 * ROWS * D),
     )(inputs, cotangent)
 
@@ -157,7 +157,7 @@
         in_specs=[ANY] * 2,
         out_specs=ANY,
         scratch_shapes=[pltpu.VMEM(shape, jnp.bfloat16)] + [pltpu.SemaphoreType.DMA((4,))] * 2,
-        compiler_params=vmem(16),
+        compiler_params=vmem(8),
         cost_estimate=cost(0, 8 * HELD * D),
     )(up, down)
 
@@ -177,7 +177,7 @@
         out_shape=jax.ShapeDtypeStruct((2, rows, D), jnp.bfloat16),
         in_specs=[INSIDE] * len(pieces) + [ANY] * len(after),
         out_specs=INSIDE,
-        compiler_params=vmem(16),
+        compiler_params=vmem(8),
         cost_estimate=cost(0, 8 * rows * D),
     )(*pieces, *after)
 
@@ -203,7 +203,7 @@
         in_specs=[ANY] * len(operands),
         out_specs=[INSIDE] * len(blocks),
         scratch_shapes=[pltpu.SemaphoreType.DMA((len(blocks),))],
-        compiler_params=vmem(16),
+        compiler_params=vmem(8),
         cost_estimate=cost(0, 8 * rows * D * len(blocks)),
     )(*operands)
 
@@ -293,7 +293,7 @@
             pltpu.SemaphoreType.DMA((len(jobs),)),
             pltpu.SemaphoreType.DMA((1,)),
         ],
-        compiler_params=vmem(36 if len(jobs) > 1 else 24),
+        compiler_params=vmem(30 if len(jobs) > 1 else 16),
         cost_estimate=cost(flops, 4 * (total + top) * D + 4 * top * total),
     )(*operands)
 
@@ -365,7 +365,7 @@
             pltpu.VMEM((HELD, WIDTH), jnp.float32),
             pltpu.SemaphoreType.DMA((5,)),
         ],
-        compiler_params=vmem(24),
+        compiler_params=vmem(20),
         cost_estimate=cost(4 * HELD * (rest * D + TOKENS * FIRST_OWN * WIDTH), 4 * (HELD + rest) * D),
     )(up, down, tokens, pair, *after)
 
@@ -397,7 +397,7 @@
         + [ANY] * len(after),
         out_specs=pl.BlockSpec((1, 2, HELD, WIDTH), lambda j: (j, 0, 0, 0)),
         scratch_shapes=[pltpu.VMEM((HELD, WIDTH), jnp.float32)],
-        compiler_params=vmem(22),
+        compiler_params=vmem(18),
         cost_estimate=cost(4 * HELD * TOKENS * count * WIDTH, 4 * TOKENS * (HELD + count * WIDTH)),
     )(pair, pair_last, tokens, *after)
 
@@ -408,8 +408,8 @@
     weights, tokens, pair, columns, sem, out_sem = refs[10:]
     first, width = 0, WIDTH
     rest = TOKENS - EARLY
-    loads = [pltpu.make_async_copy(weights_in, weights, sem.at[0])]
-    row = 0
+    weights_load = pltpu.make_async_copy(weights_in, weights, sem.at[0])
+    loads, row = [], 0
     for k, ref in enumerate(blocks):
         rows = ref.shape[1]
         loads.append(pltpu.make_async_copy(ref, tokens.at[:, pl.ds(row, rows)], sem.at[1 + k]))
@@ -420,12 +420,9 @@
         pltpu.make_async_copy(pair_in.at[:, :, early], pair.at[:, :, early], sem.at[5]),
         pltpu.make_async_copy(source, columns, sem.at[6]),
     ]
-    for load in loads + more:
+    for load in [*loads[:2], weights_load, *loads[2:], *more]:
         load.start()
-    for load in loads:
-        load.wait()
-    stores = [pltpu.make_async_copy(tokens, tokens_out.at[:, late], out_sem.at[0])]
-    stores[0].start()
+    weights_load.wait()
     tile = 256
 
     def step(i, carry):
@@ -442,7 +439,19 @@
         pair[1, :, to] = value.astype(jnp.bfloat16)
         return carry
 
-    lax.fori_loop(0, rest // tile, step, 0)
+    def arriving(i, carry):
+        for parity in (0, 1):
+
+            @pl.when(i == parity)
+            def _(parity=parity):
+                for load in loads[2 * parity : 2 * parity + 2]:
+                    load.wait()
+
+        return step(i, carry)
+
+    lax.fori_loop(0, rest // tile, arriving, 0)
+    stores = [pltpu.make_async_copy(tokens, tokens_out.at[:, late], out_sem.at[0])]
+    stores[0].start()
     stores.append(pltpu.make_async_copy(pair.at[:, :, late], pair_out.at[:, :, late], out_sem.at[1]))
     stores[1].start()
     for load in more:
@@ -479,7 +488,7 @@
             pltpu.SemaphoreType.DMA((7,)),
             pltpu.SemaphoreType.DMA((2,)),
         ],
-        compiler_params=vmem(22),
+        compiler_params=vmem(16),
         cost_estimate=cost(
             4 * HELD * ((TOKENS - EARLY) * D + TOKENS * width), 4 * (HELD + TOKENS - EARLY) * D
         ),
@@ -538,7 +547,7 @@
             pltpu.VMEM((2, 2, HELD, WIDTH), jnp.bfloat16),
             pltpu.SemaphoreType.DMA((2,)),
         ],
-        compiler_params=vmem(22),
+        compiler_params=vmem(16),
         cost_estimate=cost(4 * HELD * TOKENS * count * WIDTH, 4 * TOKENS * (HELD + count * WIDTH)),
     )(pair, tokens, *after)
 
@@ -607,7 +616,7 @@
         + [ANY] * (len(results) + len(passing)),
         out_specs=[pair_spec] + [column_spec(c)] * 4 + mixing + [ANY] * len(passing),
         input_output_aliases=aliases,
-        compiler_params=vmem(22),
+        compiler_params=vmem(12),
         cost_estimate=cost(0, 60 * HELD * WIDTH),
     )(*operands)
 
@@ -620,7 +629,7 @@
         in_specs=[pair_spec] * 2 + [ANY] * 2,
         out_specs=[column_spec(c)] * 2,
         input_output_aliases={2: 0, 3: 1},
-        compiler_params=vmem(22),
+        compiler_params=vmem(8),
         cost_estimate=cost(0, 12 * HELD * WIDTH),
     )(own, other, *results)
 
@@ -656,7 +665,8 @@
     results = hidden_step((job,), held, [up, down], [a_all, b_all], (), (0, 512), 1)
 
     mid = 2 * half
-    halves = cut([a_up, a_down, b_x, b_y], (0, mid, 0, mid), mid, [results[0]])
+    halves = cut([a_up, a_down], (0, mid), mid, [results[0]])
+    halves += cut([b_x, b_y], (0, mid), mid, [results[0]])
     last = [
         moved(halves[0], z_up),
         moved(halves[1], z_down),
@@ -671,7 +681,7 @@
         results,
         (512, 1024),
         2,
-        halves[:1],
+        halves[::2],
     )
     own_pair = results[0]
     pair, tokens, theirs = last_shared(weights_sent, last, *results[1:])

time: 196 us -> 187 us (0.954)
  waiting for transfers between devices: 66.3 us -> 62.3 us
  Pallas kernels: 84.1 us -> 81.5 us
    ppermute x24, waiting for transfers between devices: 59.4 us -> 55.3 us  [moved(): return lax.ppermute(block, 'fsdp', route)]
  transfers between devices with their start and end apart: 31 -> 31, of which waited for: 12 -> 11; matrix products, arithmetic and copies ran while one was open for 0% -> 0% of each run, Pallas kernels for 38% -> 39%
where the time goes in v2:
time: 187 us
  Pallas kernels  81.5 us (44%)
  waiting for transfers between devices  62.3 us (33%)
  starting transfers between devices  41.3 us (22%)
    ppermute x24, waiting for transfers between devices, moved(): return lax.ppermute(block, 'fsdp', route)  55.3 us
    ppermute x24, starting transfers between devices, moved(): return lax.ppermute(block, 'fsdp', route)  40.8 us
    pallas_call x2, Pallas kernels, hidden_step(): pl.pallas_call(functools.partial(hidden_kernel, jobs, sizes, pieces, skip...  20.7 us
    pallas_call x7, Pallas kernels, adam_chunk(): pl.pallas_call(functools.partial(adam_kernel, (bool(mixed), len(passing))...  18.3 us
    pallas_call x2, Pallas kernels, theirs_chunks(): pl.pallas_call(functools.partial(theirs_kernel, count, len(after)), out_s...  11.8 us
    pallas_call x2, Pallas kernels, own_rest(): pl.pallas_call(kernel, out_shape=jax.ShapeDtypeStruct((count, 2, HELD, WI...  7.21 us
    ppermute x7, waiting for transfers between devices, finish(): others.append(lax.ppermute(out[0], 'rep', route))  6.94 us
    pallas_call x1, Pallas kernels, own_first(): pl.pallas_call(own_first_kernel, out_shape=[jax.ShapeDtypeStruct((FIRST_O...  6.25 us
  transfers between devices with their start and end apart: 31, of which 11 were waited for; matrix products, arithmetic and copies ran while one was open for 0% of the time, Pallas kernels for 39%

profile of v2, /device:TPU:0, one launch (start us, length us, event | category | flops | bytes accessed | tf_op | source)
XLA Modules:
  0.0 187.3 jit_solution(5459225619982656108)
XLA Ops:
  0.7 3.0 %shard_map.136 = bf16[2,448,1792]{2,1,0:T(8,128)(2,1)} custom-call(bf16[448,1792]{1,0:T(8,128)(2,1)} %bitcast.23, bf16[448,1792]{1,0:T(8,128)(2,1)} %bitcast.28), custom_call_target="tpu_custom_call" | custom-call | bytes 6422528 | tf_op jit(solution)/shard_map/pallas_call | solution.py:154
  8.4 2.2 %collective-permute-start.36 = (bf16[2,64,1792]{2,1,0:T(8,128)(2,1)S(1)}, bf16[2,64,1792]{2,1,0:T(8,128)(2,1)S(1)}, u32[]{:S(2)}, u32[]{:S(2)}) collective-permute-start(bf16[2,64,1792]{2,1,0:T(8,128)(2,1)S(1)} %get-tuple-element.226.refs_0_), channel_id=1, source_target_pairs={{0,24},{1,25},{2,26},{3,27},{4,28},{5,29},{6,30},{7,31},{8,0},{9,1... | collective-permute-start | bytes 1376264 | tf_op jit(solution)/shard_map/ppermute | solution.py:43
  10.6 3.0 %collective-permute-start.29 = (bf16[2,64,1792]{2,1,0:T(8,128)(2,1)S(1)}, bf16[2,64,1792]{2,1,0:T(8,128)(2,1)S(1)}, u32[]{:S(2)}, u32[]{:S(2)}) collective-permute-start(bf16[2,64,1792]{2,1,0:T(8,128)(2,1)S(1)} %get-tuple-element.225.refs_0_), channel_id=1, source_target_pairs={{0,4},{1,5},{2,6},{3,7},{4,0},{5,1},{6,2},{7,3},{8,12},{9,13},{10,... | collective-permute-start | bytes 1376264 | tf_op jit(solution)/shard_map/ppermute | solution.py:43
  15.8 5.0 %collective-permute-done.35.refs_1_ = bf16[2,64,1792]{2,1,0:T(8,128)(2,1)S(1)} collective-permute-done((bf16[2,64,1792]{2,1,0:T(8,128)(2,1)S(1)}, bf16[2,64,1792]{2,1,0:T(8,128)(2,1)S(1)}, u32[]{:S(2)}, u32[]{:S(2)}) %collective-permute-start.35) | collective-permute-done | bytes 458784 | tf_op jit(solution)/shard_map/ppermute | solution.py:43
  20.9 3.3 %collective-permute-start.38 = (bf16[2,32,1792]{2,1,0:T(8,128)(2,1)S(1)}, bf16[2,32,1792]{2,1,0:T(8,128)(2,1)S(1)}, u32[]{:S(2)}, u32[]{:S(2)}) collective-permute-start(bf16[2,32,1792]{2,1,0:T(8,128)(2,1)S(1)} %slice.19), channel_id=1, source_target_pairs={{0,24},{1,25},{2,26},{3,27},{4,28},{5,29},{6,30},{7,31},{8,0},{9,1... | collective-permute-start | bytes 688136 | tf_op jit(solution)/shard_map/ppermute | solution.py:43
  24.2 2.3 %collective-permute-start.31 = (bf16[2,32,1792]{2,1,0:T(8,128)(2,1)S(1)}, bf16[2,32,1792]{2,1,0:T(8,128)(2,1)S(1)}, u32[]{:S(2)}, u32[]{:S(2)}) collective-permute-start(bf16[2,32,1792]{2,1,0:T(8,128)(2,1)S(1)} %slice.16), channel_id=1, source_target_pairs={{0,3},{1,2},{2,1},{3,0},{4,7},{5,6},{6,5},{7,4},{8,11},{9,10},{10,... | collective-permute-start | bytes 688136 | tf_op jit(solution)/shard_map/ppermute | solution.py:43
  26.5 3.1 %collective-permute-start.32 = (bf16[2,32,1792]{2,1,0:T(8,128)(2,1)S(1)}, bf16[2,32,1792]{2,1,0:T(8,128)(2,1)S(1)}, u32[]{:S(2)}, u32[]{:S(2)}) collective-permute-start(bf16[2,32,1792]{2,1,0:T(8,128)(2,1)S(1)} %slice.17), channel_id=1, source_target_pairs={{0,4},{1,5},{2,6},{3,7},{4,0},{5,1},{6,2},{7,3},{8,12},{9,13},{10,... | collective-permute-start | bytes 688136 | tf_op jit(solution)/shard_map/ppermute | solution.py:43
  36.7 3.2 %collective-permute-start.34 = (bf16[2,256,1792]{2,1,0:T(8,128)(2,1)}, bf16[2,256,1792]{2,1,0:T(8,128)(2,1)}, u32[]{:S(2)}, u32[]{:S(2)}) collective-permute-start(bf16[2,256,1792]{2,1,0:T(8,128)(2,1)} %shard_map.138.refs_2_.refs_7_), channel_id=1, source_target_pairs={{0,24},{1,25},{2,26},{3,27},{4,28},{5,29},{6,30},{7,31},{8,0},{9,1... | collective-permute-start | bytes 5505032 | tf_op jit(solution)/shard_map/ppermute | solution.py:43
  40.7 5.2 %shard_map.140 = (bf16[2,448,1536]{2,1,0:T(8,128)(2,1)S(1)}, bf16[2,448,2048]{2,1,0:T(8,128)(2,1)S(1)}, bf16[2,2048,1792]{2,1,0:T(8,128)(2,1)}) custom-call(bf16[448,1792]{1,0:T(8,128)(2,1)} %bitcast.24, bf16[448,1792]{1,0:T(8,128)(2,1)} %bitcast.29, bf16[2,256,1792]{2,1,0:T(8,128)(2,1)} %shard_map.138.refs_2_.refs_7_, ...), custom_call_target="tpu_custom_call" | custom-call | flops 3288334336 | bytes 7798784 | tf_op jit(solution)/shard_map/pallas_call | solution.py:281
  45.9 27.6 %collective-permute-done.41.refs_0_.refs_5_ = bf16[2,256,1792]{2,1,0:T(8,128)(2,1)} collective-permute-done((bf16[2,256,1792]{2,1,0:T(8,128)(2,1)}, bf16[2,256,1792]{2,1,0:T(8,128)(2,1)}, u32[]{:S(2)}, u32[]{:S(2)}) %collective-permute-start.41) | collective-permute-done | bytes 1835040 | tf_op jit(solution)/shard_map/ppermute | solution.py:43
  75.7 2.3 %collective-permute-start.43 = (bf16[2,128,1792]{2,1,0:T(8,128)(2,1)S(1)}, bf16[2,128,1792]{2,1,0:T(8,128)(2,1)S(1)}, u32[]{:S(2)}, u32[]{:S(2)}) collective-permute-start(bf16[2,128,1792]{2,1,0:T(8,128)(2,1)S(1)} %get-tuple-element.230.refs_13_), channel_id=1, source_target_pairs={{0,3},{1,2},{2,1},{3,0},{4,7},{5,6},{6,5},{7,4},{8,11},{9,10},{10,... | collective-permute-start | bytes 2752520 | tf_op jit(solution)/shard_map/ppermute | solution.py:43
  80.9 3.1 %collective-permute-start.40 = (bf16[2,128,1792]{2,1,0:T(8,128)(2,1)S(1)}, bf16[2,128,1792]{2,1,0:T(8,128)(2,1)S(1)}, u32[]{:S(2)}, u32[]{:S(2)}) collective-permute-start(bf16[2,128,1792]{2,1,0:T(8,128)(2,1)S(1)} %get-tuple-element.229), channel_id=1, source_target_pairs={{0,24},{1,25},{2,26},{3,27},{4,28},{5,29},{6,30},{7,31},{8,0},{9,1... | collective-permute-start | bytes 2752520 | tf_op jit(solution)/shard_map/ppermute | solution.py:43
  84.0 15.6 %shard_map.143 = (bf16[2,448,1536]{2,1,0:T(8,128)(2,1)S(1)}, bf16[2,448,2048]{2,1,0:T(8,128)(2,1)S(1)}, bf16[2,2048,1792]{2,1,0:T(8,128)(2,1)}) custom-call(bf16[448,1792]{1,0:T(8,128)(2,1)S(1)} %bitcast.25, bf16[448,1792]{1,0:T(8,128)(2,1)S(1)} %bitcast.30, ...), custom_call_target="tpu_custom_call", output_to_operand_aliasing={{0}: (9, {}), {1}: (10, {}), {2}: (11, {})} | custom-call | flops 16441671680 | bytes 22937600 | tf_op jit(solution)/shard_map/pallas_call | solution.py:281
  100.8 5.4 %shard_map.144 = (bf16[2,448,2048]{2,1,0:T(8,128)(2,1)S(1)}, bf16[2,2048,1792]{2,1,0:T(8,128)(2,1)}, bf16[2,448,256]{2,1,0:T(8,128)(2,1)S(1)}) custom-call(bf16[2,448,1792]{2,1,0:T(8,128)(2,1)S(1)} %collective-permute-done.28.refs_2_.refs_0_, ...), custom_call_target="tpu_custom_call", output_to_operand_aliasing={{0}: (5, {}), {1}: (6, {})} | custom-call | flops 5167382528 | bytes 6881280 | tf_op jit(solution)/shard_map/pallas_call | solution.py:473
  106.3 81.0 %conditional.1 = (bf16[448,1792]{1,0:T(8,128)(2,1)}, bf16[448,1792]{1,0:T(8,128)(2,1)}, bf16[448,1792]{1,0:T(8,128)(2,1)}, bf16[448,1792]{1,0:T(8,128)(2,1)}, bf...) conditional(s32[]{:T(128)} %convert_element_type.6, (bf16[2,448,2048]{2,1,0:T(8,128)(2,1)S(1)}, ...), branch_computations={%region_0.1_spmd, %region_1.2_spmd} | conditional | flops 27715960832 | bytes 179962448 | solution.py:723
  106.9 4.9 %branch_1_fun.14 = (bf16[2,448,256]{2,1,0:T(8,128)(2,1)S(1)}, bf16[2,448,256]{2,1,0:T(8,128)(2,1)S(1)}) custom-call(bf16[2,448,2048]{2,1,0:T(8,128)(2,1)S(1)} %get-tuple-element.125.pair, bf16[2,2048,1792]{2,1,0:T(8,128)(2,1)} %get-tuple-element.124.tokens.tokens_in.refs_2_), custom_call_target="tpu_custom_call" | custom-call | flops 3758096384 | bytes 7864320 | tf_op jit(solution)/shard_map/cond/branch_1_fun/pallas_call | solution.py:539
  113.7 6.2 %branch_1_fun.15 = (f32[2,2,448,256]{3,2,1,0:T(8,128)S(1)}, bf16[2,448,512]{2,1,0:T(8,128)(2,1)S(1)}) custom-call(bf16[448,1792]{1,0:T(8,128)(2,1)S(1)} %get-tuple-element.122.up.refs_3_, bf16[448,1792]{1,0:T(8,128)(2,1)S(1)} %get-tuple-element.123.down.refs_6_, bf16[2,2048,1792]{2,1,0:T(8,128)(2,1)S(1)} %copy-done.3, ...), custom_call_target="tpu_custom_call" | custom-call | flops 7046430720 | bytes 6881280 | tf_op jit(solution)/shard_map/cond/branch_1_fun/pallas_call | solution.py:352
  120.0 2.6 %branch_1_fun.16 = (bf16[2,448,256]{2,1,0:T(8,128)(2,1)S(1)}, bf16[448,1792]{1,0:T(8,128)(2,1)}, bf16[448,1792]{1,0:T(8,128)(2,1)}, bf16[448,1792]{1,0:T(8,128)(...) custom-call(f32[2,2,448,256]{3,2,1,0:T(8,128)S(1)} %get-tuple-elemen, ...), custom_call_target="tpu_custom_call", output_to_operand_aliasing={{7}: (9, {})} | custom-call | bytes 6881280 | tf_op jit(solution)/shard_map/cond/branch_1_fun/pallas_call | solution.py:609
  124.0 6.9 %branch_1_fun.17 = (bf16[2,448,256]{2,1,0:T(8,128)(2,1)S(1)}, bf16[2,448,256]{2,1,0:T(8,128)(2,1)S(1)}, bf16[2,448,256]{2,1,0:T(8,128)(2,1)S(1)}, bf16[2,448,256]{2,1,0:T(8,128)(2,1)S(1)}) custom-call(bf16[2,448,2048]{2,1,0:T(8,128)(2,1)S(1)} %get-tuple-element.125.pair, bf16[2,2048,1792]{2,1,0:T(8,128)(2,1)S(1)} %copy-done.3, ...), custom_call_target="tpu_custom_call" | custom-call | flops 7516192768 | bytes 12058624 | tf_op jit(solution)/shard_map/cond/branch_1_fun/pallas_call | solution.py:539
  130.9 2.5 %branch_1_fun.18 = (bf16[2,448,256]{2,1,0:T(8,128)(2,1)S(1)}, bf16[448,1792]{1,0:T(8,128)(2,1)}, bf16[448,1792]{1,0:T(8,128)(2,1)}, bf16[448,1792]{1,0:T(8,128)(...) custom-call(f32[2,2,448,256]{3,2,1,0:T(8,128)S(1)} %get-tuple-elemen, ...), custom_call_target="tpu_custom_call", output_to_operand_aliasing={{1}: (9, {}), {2}: (10, {}), {3}: (11, {}), {4}: (12, {}), ... | custom-call | bytes 6881280 | tf_op jit(solution)/shard_map/cond/branch_1_fun/pallas_call | solution.py:609
  134.2 2.9 %branch_1_fun.19.refs_0_ = f32[2,2,448,256]{3,2,1,0:T(8,128)S(1)} custom-call(bf16[2,448,1536]{2,1,0:T(8,128)(2,1)S(1)} %get-tuple-element.121.pair_in.refs_0_, bf16[2,448,512]{2,1,0:T(8,128)(2,1)S(1)} %get-tuple-element.127.refs_1_, bf16[2,2048,1792]{2,1,0:T(8,128)(2,1)S(1)} %copy-done.3, bf16[2,448,256]{2,1,0:T(8,128)(2,1)S(1)} %get-tuple-element.144.refs_3_.refs_9_), custom_call_target="tpu_custom_call" | custom-call | flops 3758096384 | bytes 7864320 | tf_op jit(solution)/shard_map/cond/branch_1_fun/pallas_call | solution.py:388
  137.1 2.7 %branch_1_fun.20 = (bf16[2,448,256]{2,1,0:T(8,128)(2,1)S(1)}, bf16[448,1792]{1,0:T(8,128)(2,1)}, bf16[448,1792]{1,0:T(8,128)(2,1)}, bf16[448,1792]{1,0:T(8,128)(...) custom-call(f32[2,2,448,256]{3,2,1,0:T(8,128)S(1)} %branch_1_fun.19., ...), custom_call_target="tpu_custom_call", output_to_operand_aliasing={{1}: (11, {}), {2}: (12, {}), {3}: (13, {}), {4}: (14, {}),... | custom-call | bytes 6881280 | tf_op jit(solution)/shard_map/cond/branch_1_fun/pallas_call | solution.py:609
  141.5 5.3 %collective-permute-done.20.refs_2_ = bf16[2,448,256]{2,1,0:T(8,128)(2,1)S(1)} collective-permute-done((bf16[2,448,256]{2,1,0:T(8,128)(2,1)S(1)}, bf16[2,448,256]{2,1,0:T(8,128)(2,1)S(1)}, u32[]{:S(2)}, u32[]{:S(2)}) %collective-permute-start.20) | collective-permute-done | bytes 458784 | tf_op jit(solution)/shard_map/cond/branch_1_fun/ppermute | solution.py:43
  146.7 2.7 %branch_1_fun.22 = (bf16[2,448,256]{2,1,0:T(8,128)(2,1)S(1)}, bf16[448,1792]{1,0:T(8,128)(2,1)}, bf16[448,1792]{1,0:T(8,128)(2,1)}, bf16[448,1792]{1,0:T(8,128)(...) custom-call(f32[2,2,448,256]{3,2,1,0:T(8,128)S(1)} %branch_1_fun.19., ...), custom_call_target="tpu_custom_call", output_to_operand_aliasing={{1}: (11, {}), {2}: (12, {}), {3}: (13, {}), {4}: (14, {}),... | custom-call | bytes 6881280 | tf_op jit(solution)/shard_map/cond/branch_1_fun/pallas_call | solution.py:609
  150.0 4.3 %branch_1_fun.21.refs_0_ = f32[3,2,448,256]{3,2,1,0:T(8,128)S(1)} custom-call(bf16[2,448,1536]{2,1,0:T(8,128)(2,1)S(1)} %get-tuple-element.121.pair_in.refs_0_, bf16[2,448,512]{2,1,0:T(8,128)(2,1)S(1)} %get-tuple-element.127.refs_1_, bf16[2,2048,1792]{2,1,0:T(8,128)(2,1)S(1)} %copy-done.3, bf16[2,448,256]{2,1,0:T(8,128)(2,1)S(1)} %get-tuple-element.153.refs_3_.refs_9_), custom_call_target="tpu_custom_call" | custom-call | flops 5637144576 | bytes 9961472 | tf_op jit(solution)/shard_map/cond/branch_1_fun/pallas_call | solution.py:388
  154.3 2.2 %collective-permute-done.18.refs_2_ = bf16[2,448,256]{2,1,0:T(8,128)(2,1)S(1)} collective-permute-done((bf16[2,448,256]{2,1,0:T(8,128)(2,1)S(1)}, bf16[2,448,256]{2,1,0:T(8,128)(2,1)S(1)}, u32[]{:S(2)}, u32[]{:S(2)}) %collective-permute-start.18) | collective-permute-done | bytes 458784 | tf_op jit(solution)/shard_map/cond/branch_1_fun/ppermute | solution.py:43
  156.6 2.7 %branch_1_fun.23 = (bf16[2,448,256]{2,1,0:T(8,128)(2,1)S(1)}, bf16[448,1792]{1,0:T(8,128)(2,1)}, bf16[448,1792]{1,0:T(8,128)(2,1)}, bf16[448,1792]{1,0:T(8,128)(...) custom-call(f32[3,2,448,256]{3,2,1,0:T(8,128)S(1)} %branch_1_fun.21., ...), custom_call_target="tpu_custom_call", output_to_operand_aliasing={{1}: (11, {}), {2}: (12, {}), {3}: (13, {}), {4}: (14, {}),... | custom-call | bytes 6881280 | tf_op jit(solution)/shard_map/cond/branch_1_fun/pallas_call | solution.py:609
  159.8 6.5 %collective-permute-done.24.refs_2_ = bf16[2,448,256]{2,1,0:T(8,128)(2,1)S(1)} collective-permute-done((bf16[2,448,256]{2,1,0:T(8,128)(2,1)S(1)}, bf16[2,448,256]{2,1,0:T(8,128)(2,1)S(1)}, u32[]{:S(2)}, u32[]{:S(2)}) %collective-permute-start.24) | collective-permute-done | bytes 458784 | tf_op jit(solution)/shard_map/cond/branch_1_fun/ppermute | solution.py:43
  166.4 2.7 %branch_1_fun.24 = (bf16[2,448,256]{2,1,0:T(8,128)(2,1)S(1)}, bf16[448,1792]{1,0:T(8,128)(2,1)}, bf16[448,1792]{1,0:T(8,128)(2,1)}, bf16[448,1792]{1,0:T(8,128)(...) custom-call(f32[3,2,448,256]{3,2,1,0:T(8,128)S(1)} %branch_1_fun.21., ...), custom_call_target="tpu_custom_call", output_to_operand_aliasing={{1}: (11, {}), {2}: (12, {}), {3}: (13, {}), {4}: (14, {}),... | custom-call | bytes 6881280 | tf_op jit(solution)/shard_map/cond/branch_1_fun/pallas_call | solution.py:609
  169.0 6.7 %collective-permute-done.22.refs_2_ = bf16[2,448,256]{2,1,0:T(8,128)(2,1)S(1)} collective-permute-done((bf16[2,448,256]{2,1,0:T(8,128)(2,1)S(1)}, bf16[2,448,256]{2,1,0:T(8,128)(2,1)S(1)}, u32[]{:S(2)}, u32[]{:S(2)}) %collective-permute-start.22) | collective-permute-done | bytes 458784 | tf_op jit(solution)/shard_map/cond/branch_1_fun/ppermute | solution.py:43
  175.8 2.7 %branch_1_fun.25 = (bf16[2,448,256]{2,1,0:T(8,128)(2,1)S(1)}, bf16[448,1792]{1,0:T(8,128)(2,1)}, bf16[448,1792]{1,0:T(8,128)(2,1)}, bf16[448,1792]{1,0:T(8,128)(...) custom-call(f32[3,2,448,256]{3,2,1,0:T(8,128)S(1)} %branch_1_fun.21., ...), custom_call_target="tpu_custom_call", output_to_operand_aliasing={{1}: (11, {}), {2}: (12, {}), {3}: (13, {}), {4}: (14, {}),... | custom-call | bytes 6881280 | tf_op jit(solution)/shard_map/cond/branch_1_fun/pallas_call | solution.py:609
  179.4 6.9 %collective-permute-done.26.other = bf16[2,448,256]{2,1,0:T(8,128)(2,1)S(1)} collective-permute-done((bf16[2,448,256]{2,1,0:T(8,128)(2,1)S(1)}, bf16[2,448,256]{2,1,0:T(8,128)(2,1)S(1)}, u32[]{:S(2)}, u32[]{:S(2)}) %collective-permute-start.26) | collective-permute-done | bytes 458784 | tf_op jit(solution)/shard_map/cond/branch_1_fun/ppermute | solution.py:709
  (77 shorter events, 29.9 us)
Async XLA Ops:
  3.6 80.4 %collective-permute-start.28 = (bf16[2,448,1792]{2,1,0:T(8,128)(2,1)}, bf16[2,448,1792]{2,1,0:T(8,128)(2,1)S(1)}, u32[]{:S(2)}, u32[]{:S(2)}) collective-permute-start(bf16[2,448,1792]{2,1,0:T(8,128)(2,1)} %shard_map.136), channel_id=1, source_target_pairs={{0,1},{1,0},{2,3},{3,2},{4,5},{5,4},{6,7},{7,6},{8,9},{9,8},{10,11... | collective-permute-start | bytes 9633800 | tf_op jit(solution)/shard_map/ppermute | solution.py:43
  6.4 14.3 %collective-permute-start.35 = (bf16[2,64,1792]{2,1,0:T(8,128)(2,1)S(1)}, bf16[2,64,1792]{2,1,0:T(8,128)(2,1)S(1)}, u32[]{:S(2)}, u32[]{:S(2)}) collective-permute-start(bf16[2,64,1792]{2,1,0:T(8,128)(2,1)S(1)} %get-tuple-element.226.refs_0_), channel_id=1, source_target_pairs={{0,8},{1,9},{2,10},{3,11},{4,12},{5,13},{6,14},{7,15},{8,16},{9,17... | collective-permute-start | bytes 1376264 | tf_op jit(solution)/shard_map/ppermute | solution.py:43
  8.4 12.5 %collective-permute-start.36 = (bf16[2,64,1792]{2,1,0:T(8,128)(2,1)S(1)}, bf16[2,64,1792]{2,1,0:T(8,128)(2,1)S(1)}, u32[]{:S(2)}, u32[]{:S(2)}) collective-permute-start(bf16[2,64,1792]{2,1,0:T(8,128)(2,1)S(1)} %get-tuple-element.226.refs_0_), channel_id=1, source_target_pairs={{0,24},{1,25},{2,26},{3,27},{4,28},{5,29},{6,30},{7,31},{8,0},{9,1... | collective-permute-start | bytes 1376264 | tf_op jit(solution)/shard_map/ppermute | solution.py:43
  10.6 13.6 %collective-permute-start.29 = (bf16[2,64,1792]{2,1,0:T(8,128)(2,1)S(1)}, bf16[2,64,1792]{2,1,0:T(8,128)(2,1)S(1)}, u32[]{:S(2)}, u32[]{:S(2)}) collective-permute-start(bf16[2,64,1792]{2,1,0:T(8,128)(2,1)S(1)} %get-tuple-element.225.refs_0_), channel_id=1, source_target_pairs={{0,4},{1,5},{2,6},{3,7},{4,0},{5,1},{6,2},{7,3},{8,12},{9,13},{10,... | collective-permute-start | bytes 1376264 | tf_op jit(solution)/shard_map/ppermute | solution.py:43
  13.6 12.8 %collective-permute-start.30 = (bf16[2,64,1792]{2,1,0:T(8,128)(2,1)S(1)}, bf16[2,64,1792]{2,1,0:T(8,128)(2,1)S(1)}, u32[]{:S(2)}, u32[]{:S(2)}) collective-permute-start(bf16[2,64,1792]{2,1,0:T(8,128)(2,1)S(1)} %get-tuple-element.225.refs_0_), channel_id=1, source_target_pairs={{0,3},{1,2},{2,1},{3,0},{4,7},{5,6},{6,5},{7,4},{8,11},{9,10},{10,... | collective-permute-start | bytes 1376264 | tf_op jit(solution)/shard_map/ppermute | solution.py:43
  20.8 8.8 %collective-permute-start.37 = (bf16[2,32,1792]{2,1,0:T(8,128)(2,1)S(1)}, bf16[2,32,1792]{2,1,0:T(8,128)(2,1)S(1)}, u32[]{:S(2)}, u32[]{:S(2)}) collective-permute-start(bf16[2,32,1792]{2,1,0:T(8,128)(2,1)S(1)} %slice.18), channel_id=1, source_target_pairs={{0,8},{1,9},{2,10},{3,11},{4,12},{5,13},{6,14},{7,15},{8,16},{9,17... | collective-permute-start | bytes 688136 | tf_op jit(solution)/shard_map/ppermute | solution.py:43
  20.9 8.7 %collective-permute-start.38 = (bf16[2,32,1792]{2,1,0:T(8,128)(2,1)S(1)}, bf16[2,32,1792]{2,1,0:T(8,128)(2,1)S(1)}, u32[]{:S(2)}, u32[]{:S(2)}) collective-permute-start(bf16[2,32,1792]{2,1,0:T(8,128)(2,1)S(1)} %slice.19), channel_id=1, source_target_pairs={{0,24},{1,25},{2,26},{3,27},{4,28},{5,29},{6,30},{7,31},{8,0},{9,1... | collective-permute-start | bytes 688136 | tf_op jit(solution)/shard_map/ppermute | solution.py:43
  24.2 11.0 %collective-permute-start.31 = (bf16[2,32,1792]{2,1,0:T(8,128)(2,1)S(1)}, bf16[2,32,1792]{2,1,0:T(8,128)(2,1)S(1)}, u32[]{:S(2)}, u32[]{:S(2)}) collective-permute-start(bf16[2,32,1792]{2,1,0:T(8,128)(2,1)S(1)} %slice.16), channel_id=1, source_target_pairs={{0,3},{1,2},{2,1},{3,0},{4,7},{5,6},{6,5},{7,4},{8,11},{9,10},{10,... | collective-permute-start | bytes 688136 | tf_op jit(solution)/shard_map/ppermute | solution.py:43
  26.5 8.7 %collective-permute-start.32 = (bf16[2,32,1792]{2,1,0:T(8,128)(2,1)S(1)}, bf16[2,32,1792]{2,1,0:T(8,128)(2,1)S(1)}, u32[]{:S(2)}, u32[]{:S(2)}) collective-permute-start(bf16[2,32,1792]{2,1,0:T(8,128)(2,1)S(1)} %slice.17), channel_id=1, source_target_pairs={{0,4},{1,5},{2,6},{3,7},{4,0},{5,1},{6,2},{7,3},{8,12},{9,13},{10,... | collective-permute-start | bytes 688136 | tf_op jit(solution)/shard_map/ppermute | solution.py:43
  31.1 42.5 %collective-permute-start.41 = (bf16[2,256,1792]{2,1,0:T(8,128)(2,1)}, bf16[2,256,1792]{2,1,0:T(8,128)(2,1)}, u32[]{:S(2)}, u32[]{:S(2)}) collective-permute-start(bf16[2,256,1792]{2,1,0:T(8,128)(2,1)} %shard_map.139.refs_3_.refs_8_), channel_id=1, source_target_pairs={{0,4},{1,5},{2,6},{3,7},{4,0},{5,1},{6,2},{7,3},{8,12},{9,13},{10,... | collective-permute-start | bytes 5505032 | tf_op jit(solution)/shard_map/ppermute | solution.py:43
  33.0 41.2 %collective-permute-start.42 = (bf16[2,256,1792]{2,1,0:T(8,128)(2,1)}, bf16[2,256,1792]{2,1,0:T(8,128)(2,1)}, u32[]{:S(2)}, u32[]{:S(2)}) collective-permute-start(bf16[2,256,1792]{2,1,0:T(8,128)(2,1)} %shard_map.139.refs_3_.refs_8_), channel_id=1, source_target_pairs={{0,3},{1,2},{2,1},{3,0},{4,7},{5,6},{6,5},{7,4},{8,11},{9,10},{10,... | collective-permute-start | bytes 5505032 | tf_op jit(solution)/shard_map/ppermute | solution.py:43
  36.6 41.4 %collective-permute-start.33 = (bf16[2,256,1792]{2,1,0:T(8,128)(2,1)}, bf16[2,256,1792]{2,1,0:T(8,128)(2,1)}, u32[]{:S(2)}, u32[]{:S(2)}) collective-permute-start(bf16[2,256,1792]{2,1,0:T(8,128)(2,1)} %shard_map.138.refs_2_.refs_7_), channel_id=1, source_target_pairs={{0,8},{1,9},{2,10},{3,11},{4,12},{5,13},{6,14},{7,15},{8,16},{9,17... | collective-permute-start | bytes 5505032 | tf_op jit(solution)/shard_map/ppermute | solution.py:43
  36.7 41.3 %collective-permute-start.34 = (bf16[2,256,1792]{2,1,0:T(8,128)(2,1)}, bf16[2,256,1792]{2,1,0:T(8,128)(2,1)}, u32[]{:S(2)}, u32[]{:S(2)}) collective-permute-start(bf16[2,256,1792]{2,1,0:T(8,128)(2,1)} %shard_map.138.refs_2_.refs_7_), channel_id=1, source_target_pairs={{0,24},{1,25},{2,26},{3,27},{4,28},{5,29},{6,30},{7,31},{8,0},{9,1... | collective-permute-start | bytes 5505032 | tf_op jit(solution)/shard_map/ppermute | solution.py:43
  75.7 8.3 %copy-start.4 = (bf16[1,448,1792]{2,1,0:T(8,128)(2,1)S(1)}, bf16[1,448,1792]{2,1,0:T(8,128)(2,1)}, u32[]{:S(2)}) copy-start(bf16[1,448,1792]{2,1,0:T(8,128)(2,1)} %param.13) | copy-start | bytes 4816900
  75.7 23.9 %collective-permute-start.43 = (bf16[2,128,1792]{2,1,0:T(8,128)(2,1)S(1)}, bf16[2,128,1792]{2,1,0:T(8,128)(2,1)S(1)}, u32[]{:S(2)}, u32[]{:S(2)}) collective-permute-start(bf16[2,128,1792]{2,1,0:T(8,128)(2,1)S(1)} %get-tuple-element.230.refs_13_), channel_id=1, source_target_pairs={{0,3},{1,2},{2,1},{3,0},{4,7},{5,6},{6,5},{7,4},{8,11},{9,10},{10,... | collective-permute-start | bytes 2752520 | tf_op jit(solution)/shard_map/ppermute | solution.py:43
  79.5 20.9 %collective-permute-start.39 = (bf16[2,128,1792]{2,1,0:T(8,128)(2,1)S(1)}, bf16[2,128,1792]{2,1,0:T(8,128)(2,1)S(1)}, u32[]{:S(2)}, u32[]{:S(2)}) collective-permute-start(bf16[2,128,1792]{2,1,0:T(8,128)(2,1)S(1)} %get-tuple-element.228.refs_12_), channel_id=1, source_target_pairs={{0,8},{1,9},{2,10},{3,11},{4,12},{5,13},{6,14},{7,15},{8,16},{9,17... | collective-permute-start | bytes 2752520 | tf_op jit(solution)/shard_map/ppermute | solution.py:43
  80.0 20.7 %collective-permute-start.44 = (bf16[2,128,1792]{2,1,0:T(8,128)(2,1)S(1)}, bf16[2,128,1792]{2,1,0:T(8,128)(2,1)S(1)}, u32[]{:S(2)}, u32[]{:S(2)}) collective-permute-start(bf16[2,128,1792]{2,1,0:T(8,128)(2,1)S(1)} %get-tuple-element.231), channel_id=1, source_target_pairs={{0,4},{1,5},{2,6},{3,7},{4,0},{5,1},{6,2},{7,3},{8,12},{9,13},{10,... | collective-permute-start | bytes 2752520 | tf_op jit(solution)/shard_map/ppermute | solution.py:43
  80.9 20.0 %collective-permute-start.40 = (bf16[2,128,1792]{2,1,0:T(8,128)(2,1)S(1)}, bf16[2,128,1792]{2,1,0:T(8,128)(2,1)S(1)}, u32[]{:S(2)}, u32[]{:S(2)}) collective-permute-start(bf16[2,128,1792]{2,1,0:T(8,128)(2,1)S(1)} %get-tuple-element.229), channel_id=1, source_target_pairs={{0,24},{1,25},{2,26},{3,27},{4,28},{5,29},{6,30},{7,31},{8,0},{9,1... | collective-permute-start | bytes 2752520 | tf_op jit(solution)/shard_map/ppermute | solution.py:43
  106.6 13.4 %collective-permute-start.15 = (bf16[2,448,256]{2,1,0:T(8,128)(2,1)S(1)}, bf16[2,448,256]{2,1,0:T(8,128)(2,1)S(1)}, u32[]{:S(2)}, u32[]{:S(2)}) collective-permute-start(bf16[2,448,256]{2,1,0:T(8,128)(2,1)S(1)} %get-tuple-element.134), channel_id=1, source_target_pairs={{0,1},{1,0},{2,3},{3,2},{4,5},{5,4},{6,7},{7,6},{8,9},{9,8},{10,11... | collective-permute-start | bytes 1376264 | tf_op jit(solution)/shard_map/cond/branch_1_fun/ppermute | solution.py:43
  111.8 19.1 %collective-permute-start.14 = (bf16[2,448,256]{2,1,0:T(8,128)(2,1)S(1)}, bf16[2,448,256]{2,1,0:T(8,128)(2,1)S(1)}, u32[]{:S(2)}, u32[]{:S(2)}) collective-permute-start(bf16[2,448,256]{2,1,0:T(8,128)(2,1)S(1)} %get-tuple-element.126.refs_0_), channel_id=1, source_target_pairs={{0,1},{1,0},{2,3},{3,2},{4,5},{5,4},{6,7},{7,6},{8,9},{9,8},{10,11... | collective-permute-start | bytes 1376264 | tf_op jit(solution)/shard_map/cond/branch_1_fun/ppermute | solution.py:43
  122.6 14.5 %collective-permute-start.17 = (bf16[2,448,256]{2,1,0:T(8,128)(2,1)S(1)}, bf16[2,448,256]{2,1,0:T(8,128)(2,1)S(1)}, u32[]{:S(2)}, u32[]{:S(2)}) collective-permute-start(bf16[2,448,256]{2,1,0:T(8,128)(2,1)S(1)} %get-tuple-element.142.refs_0_.refs_9_), channel_id=1, source_target_pairs={{0,32},{32,64},{64,96},{96,0},{1,33},{33,65},{65,97},{97,1},{2,34}... | collective-permute-start | bytes 1376264 | tf_op jit(solution)/shard_map/cond/branch_1_fun/ppermute | solution.py:709
  122.6 14.5 %collective-permute-start.16 = (bf16[2,448,256]{2,1,0:T(8,128)(2,1)S(1)}, bf16[2,448,256]{2,1,0:T(8,128)(2,1)S(1)}, u32[]{:S(2)}, u32[]{:S(2)}) collective-permute-start(bf16[2,448,256]{2,1,0:T(8,128)(2,1)S(1)} %get-tuple-element.145), channel_id=1, source_target_pairs={{0,1},{1,0},{2,3},{3,2},{4,5},{5,4},{6,7},{7,6},{8,9},{9,8},{10,11... | collective-permute-start | bytes 1376264 | tf_op jit(solution)/shard_map/cond/branch_1_fun/ppermute | solution.py:43
  133.4 13.3 %collective-permute-start.20 = (bf16[2,448,256]{2,1,0:T(8,128)(2,1)S(1)}, bf16[2,448,256]{2,1,0:T(8,128)(2,1)S(1)}, u32[]{:S(2)}, u32[]{:S(2)}) collective-permute-start(bf16[2,448,256]{2,1,0:T(8,128)(2,1)S(1)} %get-tuple-element.155), channel_id=1, source_target_pairs={{0,1},{1,0},{2,3},{3,2},{4,5},{5,4},{6,7},{7,6},{8,9},{9,8},{10,11... | collective-permute-start | bytes 1376264 | tf_op jit(solution)/shard_map/cond/branch_1_fun/ppermute | solution.py:43
  134.0 12.7 %collective-permute-start.21 = (bf16[2,448,256]{2,1,0:T(8,128)(2,1)S(1)}, bf16[2,448,256]{2,1,0:T(8,128)(2,1)S(1)}, u32[]{:S(2)}, u32[]{:S(2)}) collective-permute-start(bf16[2,448,256]{2,1,0:T(8,128)(2,1)S(1)} %get-tuple-element.144.refs_3_.refs_9_), channel_id=1, source_target_pairs={{0,32},{32,64},{64,96},{96,0},{1,33},{33,65},{65,97},{97,1},{2,34}... | collective-permute-start | bytes 1376264 | tf_op jit(solution)/shard_map/cond/branch_1_fun/ppermute | solution.py:709
  139.8 16.8 %collective-permute-start.18 = (bf16[2,448,256]{2,1,0:T(8,128)(2,1)S(1)}, bf16[2,448,256]{2,1,0:T(8,128)(2,1)S(1)}, u32[]{:S(2)}, u32[]{:S(2)}) collective-permute-start(bf16[2,448,256]{2,1,0:T(8,128)(2,1)S(1)} %get-tuple-element.154), channel_id=1, source_target_pairs={{0,1},{1,0},{2,3},{3,2},{4,5},{5,4},{6,7},{7,6},{8,9},{9,8},{10,11... | collective-permute-start | bytes 1376264 | tf_op jit(solution)/shard_map/cond/branch_1_fun/ppermute | solution.py:43
  141.2 15.4 %collective-permute-start.19 = (bf16[2,448,256]{2,1,0:T(8,128)(2,1)S(1)}, bf16[2,448,256]{2,1,0:T(8,128)(2,1)S(1)}, u32[]{:S(2)}, u32[]{:S(2)}) collective-permute-start(bf16[2,448,256]{2,1,0:T(8,128)(2,1)S(1)} %get-tuple-element.153.refs_3_.refs_9_), channel_id=1, source_target_pairs={{0,32},{32,64},{64,96},{96,0},{1,33},{33,65},{65,97},{97,1},{2,34}... | collective-permute-start | bytes 1376264 | tf_op jit(solution)/shard_map/cond/branch_1_fun/ppermute | solution.py:709
  149.4 17.0 %collective-permute-start.24 = (bf16[2,448,256]{2,1,0:T(8,128)(2,1)S(1)}, bf16[2,448,256]{2,1,0:T(8,128)(2,1)S(1)}, u32[]{:S(2)}, u32[]{:S(2)}) collective-permute-start(bf16[2,448,256]{2,1,0:T(8,128)(2,1)S(1)} %get-tuple-element.172), channel_id=1, source_target_pairs={{0,1},{1,0},{2,3},{3,2},{4,5},{5,4},{6,7},{7,6},{8,9},{9,8},{10,11... | collective-permute-start | bytes 1376264 | tf_op jit(solution)/shard_map/cond/branch_1_fun/ppermute | solution.py:43
  150.0 16.4 %collective-permute-start.25 = (bf16[2,448,256]{2,1,0:T(8,128)(2,1)S(1)}, bf16[2,448,256]{2,1,0:T(8,128)(2,1)S(1)}, u32[]{:S(2)}, u32[]{:S(2)}) collective-permute-start(bf16[2,448,256]{2,1,0:T(8,128)(2,1)S(1)} %get-tuple-element.173.refs_9_), channel_id=1, source_target_pairs={{0,32},{32,64},{64,96},{96,0},{1,33},{33,65},{65,97},{97,1},{2,34}... | collective-permute-start | bytes 1376264 | tf_op jit(solution)/shard_map/cond/branch_1_fun/ppermute | solution.py:709
  159.2 16.5 %collective-permute-start.22 = (bf16[2,448,256]{2,1,0:T(8,128)(2,1)S(1)}, bf16[2,448,256]{2,1,0:T(8,128)(2,1)S(1)}, u32[]{:S(2)}, u32[]{:S(2)}) collective-permute-start(bf16[2,448,256]{2,1,0:T(8,128)(2,1)S(1)} %get-tuple-element.170), channel_id=1, source_target_pairs={{0,1},{1,0},{2,3},{3,2},{4,5},{5,4},{6,7},{7,6},{8,9},{9,8},{10,11... | collective-permute-start | bytes 1376264 | tf_op jit(solution)/shard_map/cond/branch_1_fun/ppermute | solution.py:43
  159.8 15.9 %collective-permute-start.23 = (bf16[2,448,256]{2,1,0:T(8,128)(2,1)S(1)}, bf16[2,448,256]{2,1,0:T(8,128)(2,1)S(1)}, u32[]{:S(2)}, u32[]{:S(2)}) collective-permute-start(bf16[2,448,256]{2,1,0:T(8,128)(2,1)S(1)} %get-tuple-element.171.refs_9_), channel_id=1, source_target_pairs={{0,32},{32,64},{64,96},{96,0},{1,33},{33,65},{65,97},{97,1},{2,34}... | collective-permute-start | bytes 1376264 | tf_op jit(solution)/shard_map/cond/branch_1_fun/ppermute | solution.py:709
  169.0 9.4 %collective-permute-start.27 = (bf16[2,448,256]{2,1,0:T(8,128)(2,1)S(1)}, bf16[2,448,256]{2,1,0:T(8,128)(2,1)S(1)}, u32[]{:S(2)}, u32[]{:S(2)}) collective-permute-start(bf16[2,448,256]{2,1,0:T(8,128)(2,1)S(1)} %get-tuple-element.187.own), channel_id=1, source_target_pairs={{0,32},{32,64},{64,96},{96,0},{1,33},{33,65},{65,97},{97,1},{2,34}... | collective-permute-start | bytes 1376264 | tf_op jit(solution)/shard_map/cond/branch_1_fun/ppermute | solution.py:709
  178.4 7.9 %collective-permute-start.26 = (bf16[2,448,256]{2,1,0:T(8,128)(2,1)S(1)}, bf16[2,448,256]{2,1,0:T(8,128)(2,1)S(1)}, u32[]{:S(2)}, u32[]{:S(2)}) collective-permute-start(bf16[2,448,256]{2,1,0:T(8,128)(2,1)S(1)} %get-tuple-element.186.own), channel_id=1, source_target_pairs={{0,32},{32,64},{64,96},{96,0},{1,33},{33,65},{65,97},{97,1},{2,34}... | collective-permute-start | bytes 1376264 | tf_op jit(solution)/shard_map/cond/branch_1_fun/ppermute | solution.py:709
  (8 other events, 46.3 us)

commit v3 on v2

--- a/solution.py
+++ b/solution.py
@@ -25,10 +25,12 @@
 SHARED = 2 * HELD
 TOKENS = 2048
 WIDTH = 256
-CHUNKS = D // WIDTH
+BLOCKS = D // WIDTH
+CHUNKS = tuple((WIDTH * k, WIDTH) for k in range(BLOCKS - 1)) + ((D - 256, 128), (D - 128, 128))
 FIRST_OWN = 2
 OWN_LATER = ((1, 2, 2), (2, 4, 3))
-MIXING = CHUNKS
+THEIRS_LATER = ((0, 3, 2), (2, 5, 2))
+MIXING = 7
 EARLY = 1536
 NZ, NX, NY = 4, 2, 4
 
@@ -496,25 +498,34 @@
 
 
 def column_spec(c):
-    return pl.BlockSpec((HELD, WIDTH), lambda j: (0, c))
-
-
-pair_spec = pl.BlockSpec((2, HELD, WIDTH), lambda j: (0, 0, 0))
+    first, width = CHUNKS[c]
+    return pl.BlockSpec((HELD, width), lambda j: (0, first // width))
+
+
+def pair_spec(c):
+    return pl.BlockSpec((2, HELD, CHUNKS[c][1]), lambda j: (0, 0, 0))
 
 
 def rows_spec(tokens):
     return pl.BlockSpec((2, HELD, tokens), lambda j: (0, 0, 0))
 
 
-def theirs_kernel(count, skipped, pair, tokens, *refs):
-    outs = refs[skipped : skipped + count]
+def theirs_kernel(targets, skipped, pair, tokens, *refs):
+    outs = refs[skipped : skipped + len(targets)]
     held, sem = refs[-2:]
     j = pl.program_id(0)
     slot = j % 2
 
-    @pl.when(j >= 2)
-    def _():
-        pltpu.make_async_copy(held.at[slot], outs[0], sem.at[slot]).wait()
+    def copy(k):
+        block, first, width = targets[k]
+        source = held.at[block % 2, :, :, pl.ds(first, width)]
+        return pltpu.make_async_copy(source, outs[k], sem.at[k])
+
+    for k, (block, _, _) in enumerate(targets):
+
+        @pl.when(j == block + 2)
+        def _(k=k):
+            copy(k).wait()
 
     def multiply(which, carry):
         scale = jnp.where(which == 0, up_scale, down_scale)
@@ -523,29 +534,36 @@
         return carry
 
     lax.fori_loop(0, 2, multiply, 0)
-    for k, out in enumerate(outs):
-
-        @pl.when(j == k)
-        def _(out=out):
-            pltpu.make_async_copy(held.at[slot], out, sem.at[slot]).start()
-
-    @pl.when(j == count - 1)
+    blocks = targets[-1][0] + 1
+    for k, (block, _, _) in enumerate(targets):
+
+        @pl.when(j == block)
+        def _(k=k):
+            copy(k).start()
+
+    @pl.when(j == blocks - 1)
     def _():
-        for last in range(max(count - 2, 0), count):
-            pltpu.make_async_copy(held.at[last % 2], outs[last], sem.at[last % 2]).wait()
+        for k, (block, _, _) in enumerate(targets):
+            if block >= blocks - 2:
+                copy(k).wait()
 
 
 def theirs_chunks(first, count, pair, tokens, after):
-    return pl.pallas_call(
-        functools.partial(theirs_kernel, count, len(after)),
-        out_shape=[jax.ShapeDtypeStruct((2, HELD, WIDTH), jnp.bfloat16)] * count,
+    targets = tuple(
+        (column // WIDTH - first, column % WIDTH, width)
+        for column, width in CHUNKS
+        if first <= column // WIDTH < first + count
+    )
+    return pl.pallas_call(
+        functools.partial(theirs_kernel, targets, len(after)),
+        out_shape=[jax.ShapeDtypeStruct((2, HELD, w), jnp.bfloat16) for _, _, w in targets],
         grid=(count,),
         in_specs=[rows_spec(TOKENS), pl.BlockSpec((2, TOKENS, WIDTH), lambda j: (0, 0, j + first))]
         + [ANY] * len(after),
-        out_specs=[ANY] * count,
+        out_specs=[ANY] * len(targets),
         scratch_shapes=[
             pltpu.VMEM((2, 2, HELD, WIDTH), jnp.bfloat16),
-            pltpu.SemaphoreType.DMA((2,)),
+            pltpu.SemaphoreType.DMA((len(targets),)),
         ],
         compiler_params=vmem(16),
         cost_estimate=cost(4 * HELD * TOKENS * count * WIDTH, 4 * TOKENS * (HELD + count * WIDTH)),
@@ -603,18 +621,20 @@
         operands += passing
     before = max(c - 2, 0)
     mixing = [column_spec(before)] * 2 if mixed or not results else [ANY] * 2
-    block, place = (1, 2, HELD, WIDTH), own[1]
+    (first, width), place = CHUNKS[c], own[1]
+    block, half = (1, 2, HELD, width), first % WIDTH // width
     smem = pl.BlockSpec(memory_space=pltpu.SMEM)
-    pair = jax.ShapeDtypeStruct((2, HELD, WIDTH), jnp.bfloat16)
+    pair = jax.ShapeDtypeStruct((2, HELD, width), jnp.bfloat16)
+    handed = [jax.ShapeDtypeStruct(p.shape, p.dtype) for p in passing]
     return pl.pallas_call(
         functools.partial(adam_kernel, (bool(mixed), len(passing))),
-        out_shape=[pair] + [whole] * 6 + [pair] * len(passing),
+        out_shape=[pair] + [whole] * 6 + handed,
         grid=(1,),
-        in_specs=[pl.BlockSpec(block, lambda j: (place, 0, 0, 0)), smem, pair_spec]
+        in_specs=[pl.BlockSpec(block, lambda j: (place, 0, 0, half)), smem, pair_spec(c)]
         + [column_spec(c)] * 6
-        + [pair_spec] * len(mixed)
+        + [pair_spec(before)] * len(mixed)
         + [ANY] * (len(results) + len(passing)),
-        out_specs=[pair_spec] + [column_spec(c)] * 4 + mixing + [ANY] * len(passing),
+        out_specs=[pair_spec(c)] + [column_spec(c)] * 4 + mixing + [ANY] * len(passing),
         input_output_aliases=aliases,
         compiler_params=vmem(12),
         cost_estimate=cost(0, 60 * HELD * WIDTH),
@@ -626,7 +646,7 @@
         mix_kernel,
         out_shape=[whole] * 2,
         grid=(1,),
-        in_specs=[pair_spec] * 2 + [ANY] * 2,
+        in_specs=[pair_spec(c)] * 2 + [ANY] * 2,
         out_specs=[column_spec(c)] * 2,
         input_output_aliases={2: 0, 3: 1},
         compiler_params=vmem(8),
@@ -695,28 +715,29 @@
     def finish(hop):
         route = [(g, (g + hop) % 4) for g in range(4)]
         news, updated, others = (), [], []
-        sent = [moved(theirs, y_sharing)]
-        more = theirs_chunks(1, 2, pair, tokens, [])
-        sent.append(moved(more[0], y_sharing))
-        own, last_pair = own_first(up, down, tokens, own_pair, more[:1])
-        place = [(own, c) for c in range(FIRST_OWN)]
-        for c in range(CHUNKS):
+        more = [theirs, *theirs_chunks(1, 2, pair, tokens, [])]
+        sent = [moved(t, y_sharing) for t in more[:2]]
+        own, last_pair = own_first(up, down, tokens, own_pair, more[1:2])
+        place = [(own, k) for k in range(FIRST_OWN)]
+        for c in range(len(CHUNKS)):
             mixed = [updated[c - 2], others[c - 2]] if 2 <= c < MIXING else []
-            passing = more[c + 1 : c + 2]
-            out = adam_chunk(c, place[c], bias, sent[c], state, mixed, news, passing)
+            passing = more[c + 2 : c + 3]
+            block = place[CHUNKS[c][0] // WIDTH]
+            out = adam_chunk(c, block, bias, sent[c], state, mixed, news, passing)
             updated.append(out[0])
             news = out[1:7]
             others.append(lax.ppermute(out[0], "rep", route))
             if passing:
                 sent.append(moved(out[7], y_sharing))
-            if c == 0:
-                more += theirs_chunks(3, CHUNKS - 3, pair, tokens, [out[0]])
+            for after, first, count in THEIRS_LATER:
+                if c == after:
+                    more += theirs_chunks(first, count, pair, tokens, [out[0]])
             for after, first, count in OWN_LATER:
                 if c == after:
                     own = own_rest(first, count, own_pair, last_pair, tokens, [out[0]])
                     place += [(own, k) for k in range(count)]
         mixed = news[4:]
-        for c in range(MIXING - 2, CHUNKS):
+        for c in range(MIXING - 2, len(CHUNKS)):
             mixed = mix_chunk(c, updated[c], others[c], mixed)
         return mixed[0], mixed[1], news[0], news[2], news[1], news[3]
 

time: 187 us -> 184 us (0.984)
  waiting for transfers between devices: 62.3 us -> 54 us
  starting transfers between devices: 41.3 us -> 43.9 us
  Pallas kernels: 81.5 us -> 83.4 us
    ppermute x24 -> x25, waiting for transfers between devices: 55.3 us -> 50.3 us  [moved(): return lax.ppermute(block, 'fsdp', route)]
    ppermute x7 -> x8, waiting for transfers between devices: 6.94 us -> 3.68 us  [finish(): others.append(lax.ppermute(out[0], 'rep', route))]
    ppermute x24 -> x25, starting transfers between devices: 40.8 us -> 43.7 us  [moved(): return lax.ppermute(block, 'fsdp', route)]
    pallas_call x7 -> x8, Pallas kernels: 18.3 us -> 19.7 us  [adam_chunk(): pl.pallas_call(functools.partial(adam_kernel, (bool(mixed), len(passing))...]
    pallas_call x2 -> x3, Pallas kernels: 11.8 us -> 11.6 us  [theirs_chunks(): pl.pallas_call(functools.partial(theirs_kernel, targets, len(after)), out...]
  transfers between devices with their start and end apart: 31 -> 33, of which waited for: 11 -> 16; matrix products, arithmetic and copies ran while one was open for 0% -> 0% of each run, Pallas kernels for 39% -> 40%
where the time goes in v3:
time: 184 us; the launch traced here: 183 us
  Pallas kernels  83.4 us (45%)
  waiting for transfers between devices  54 us (29%)
  starting transfers between devices  43.9 us (24%)
    ppermute x25, waiting for transfers between devices, moved(): return lax.ppermute(block, 'fsdp', route)  50.3 us
    ppermute x25, starting transfers between devices, moved(): return lax.ppermute(block, 'fsdp', route)  43.7 us
    pallas_call x2, Pallas kernels, hidden_step(): pl.pallas_call(functools.partial(hidden_kernel, jobs, sizes, pieces, skip...  20.8 us
    pallas_call x8, Pallas kernels, adam_chunk(): pl.pallas_call(functools.partial(adam_kernel, (bool(mixed), len(passing))...  19.7 us
    pallas_call x3, Pallas kernels, theirs_chunks(): pl.pallas_call(functools.partial(theirs_kernel, targets, len(after)), out...  11.6 us
    pallas_call x2, Pallas kernels, own_rest(): pl.pallas_call(kernel, out_shape=jax.ShapeDtypeStruct((count, 2, HELD, WI...  7.21 us
    pallas_call x1, Pallas kernels, own_first(): pl.pallas_call(own_first_kernel, out_shape=[jax.ShapeDtypeStruct((FIRST_O...  6.24 us
    pallas_call x1, Pallas kernels, last_shared(): pl.pallas_call(last_shared_kernel, out_shape=[jax.ShapeDtypeStruct((2, HE...  5.44 us
  transfers between devices with their start and end apart: 33, of which 16 were waited for; matrix products, arithmetic and copies ran while one was open for 0% of the time, Pallas kernels for 40%

profile of v3, /device:TPU:0, one launch (start us, length us, event | category | flops | bytes accessed | tf_op | source)
XLA Modules:
  0.0 183.4 jit_solution(15270814656438923387)
XLA Ops:
  0.7 3.0 %shard_map.136 = bf16[2,448,1792]{2,1,0:T(8,128)(2,1)} custom-call(bf16[448,1792]{1,0:T(8,128)(2,1)} %bitcast.23, bf16[448,1792]{1,0:T(8,128)(2,1)} %bitcast.28), custom_call_target="tpu_custom_call" | custom-call | bytes 6422528 | tf_op jit(solution)/shard_map/pallas_call | solution.py:156
  8.4 2.2 %collective-permute-start.40 = (bf16[2,64,1792]{2,1,0:T(8,128)(2,1)S(1)}, bf16[2,64,1792]{2,1,0:T(8,128)(2,1)S(1)}, u32[]{:S(2)}, u32[]{:S(2)}) collective-permute-start(bf16[2,64,1792]{2,1,0:T(8,128)(2,1)S(1)} %get-tuple-element.248.refs_0_), channel_id=1, source_target_pairs={{0,24},{1,25},{2,26},{3,27},{4,28},{5,29},{6,30},{7,31},{8,0},{9,1... | collective-permute-start | bytes 1376264 | tf_op jit(solution)/shard_map/ppermute | solution.py:45
  10.6 3.0 %collective-permute-start.33 = (bf16[2,64,1792]{2,1,0:T(8,128)(2,1)S(1)}, bf16[2,64,1792]{2,1,0:T(8,128)(2,1)S(1)}, u32[]{:S(2)}, u32[]{:S(2)}) collective-permute-start(bf16[2,64,1792]{2,1,0:T(8,128)(2,1)S(1)} %get-tuple-element.247.refs_0_), channel_id=1, source_target_pairs={{0,4},{1,5},{2,6},{3,7},{4,0},{5,1},{6,2},{7,3},{8,12},{9,13},{10,... | collective-permute-start | bytes 1376264 | tf_op jit(solution)/shard_map/ppermute | solution.py:45
  13.7 2.2 %collective-permute-start.34 = (bf16[2,64,1792]{2,1,0:T(8,128)(2,1)S(1)}, bf16[2,64,1792]{2,1,0:T(8,128)(2,1)S(1)}, u32[]{:S(2)}, u32[]{:S(2)}) collective-permute-start(bf16[2,64,1792]{2,1,0:T(8,128)(2,1)S(1)} %get-tuple-element.247.refs_0_), channel_id=1, source_target_pairs={{0,3},{1,2},{2,1},{3,0},{4,7},{5,6},{6,5},{7,4},{8,11},{9,10},{10,... | collective-permute-start | bytes 1376264 | tf_op jit(solution)/shard_map/ppermute | solution.py:45
  15.9 5.0 %collective-permute-done.39.refs_1_ = bf16[2,64,1792]{2,1,0:T(8,128)(2,1)S(1)} collective-permute-done((bf16[2,64,1792]{2,1,0:T(8,128)(2,1)S(1)}, bf16[2,64,1792]{2,1,0:T(8,128)(2,1)S(1)}, u32[]{:S(2)}, u32[]{:S(2)}) %collective-permute-start.39) | collective-permute-done | bytes 458784 | tf_op jit(solution)/shard_map/ppermute | solution.py:45
  20.9 3.3 %collective-permute-start.42 = (bf16[2,32,1792]{2,1,0:T(8,128)(2,1)S(1)}, bf16[2,32,1792]{2,1,0:T(8,128)(2,1)S(1)}, u32[]{:S(2)}, u32[]{:S(2)}) collective-permute-start(bf16[2,32,1792]{2,1,0:T(8,128)(2,1)S(1)} %slice.19), channel_id=1, source_target_pairs={{0,24},{1,25},{2,26},{3,27},{4,28},{5,29},{6,30},{7,31},{8,0},{9,1... | collective-permute-start | bytes 688136 | tf_op jit(solution)/shard_map/ppermute | solution.py:45
  24.2 2.3 %collective-permute-start.35 = (bf16[2,32,1792]{2,1,0:T(8,128)(2,1)S(1)}, bf16[2,32,1792]{2,1,0:T(8,128)(2,1)S(1)}, u32[]{:S(2)}, u32[]{:S(2)}) collective-permute-start(bf16[2,32,1792]{2,1,0:T(8,128)(2,1)S(1)} %slice.16), channel_id=1, source_target_pairs={{0,3},{1,2},{2,1},{3,0},{4,7},{5,6},{6,5},{7,4},{8,11},{9,10},{10,... | collective-permute-start | bytes 688136 | tf_op jit(solution)/shard_map/ppermute | solution.py:45
  26.5 3.1 %collective-permute-start.36 = (bf16[2,32,1792]{2,1,0:T(8,128)(2,1)S(1)}, bf16[2,32,1792]{2,1,0:T(8,128)(2,1)S(1)}, u32[]{:S(2)}, u32[]{:S(2)}) collective-permute-start(bf16[2,32,1792]{2,1,0:T(8,128)(2,1)S(1)} %slice.17), channel_id=1, source_target_pairs={{0,4},{1,5},{2,6},{3,7},{4,0},{5,1},{6,2},{7,3},{8,12},{9,13},{10,... | collective-permute-start | bytes 688136 | tf_op jit(solution)/shard_map/ppermute | solution.py:45
  36.7 3.1 %collective-permute-start.38 = (bf16[2,256,1792]{2,1,0:T(8,128)(2,1)}, bf16[2,256,1792]{2,1,0:T(8,128)(2,1)}, u32[]{:S(2)}, u32[]{:S(2)}) collective-permute-start(bf16[2,256,1792]{2,1,0:T(8,128)(2,1)} %shard_map.138.refs_2_.refs_7_), channel_id=1, source_target_pairs={{0,24},{1,25},{2,26},{3,27},{4,28},{5,29},{6,30},{7,31},{8,0},{9,1... | collective-permute-start | bytes 5505032 | tf_op jit(solution)/shard_map/ppermute | solution.py:45
  40.7 5.2 %shard_map.140 = (bf16[2,448,1536]{2,1,0:T(8,128)(2,1)S(1)}, bf16[2,448,2048]{2,1,0:T(8,128)(2,1)S(1)}, bf16[2,2048,1792]{2,1,0:T(8,128)(2,1)}) custom-call(bf16[448,1792]{1,0:T(8,128)(2,1)} %bitcast.24, bf16[448,1792]{1,0:T(8,128)(2,1)} %bitcast.29, bf16[2,256,1792]{2,1,0:T(8,128)(2,1)} %shard_map.138.refs_2_.refs_7_, ...), custom_call_target="tpu_custom_call" | custom-call | flops 3288334336 | bytes 7798784 | tf_op jit(solution)/shard_map/pallas_call | solution.py:283
  45.9 27.7 %collective-permute-done.45.refs_0_.refs_5_ = bf16[2,256,1792]{2,1,0:T(8,128)(2,1)} collective-permute-done((bf16[2,256,1792]{2,1,0:T(8,128)(2,1)}, bf16[2,256,1792]{2,1,0:T(8,128)(2,1)}, u32[]{:S(2)}, u32[]{:S(2)}) %collective-permute-start.45) | collective-permute-done | bytes 1835040 | tf_op jit(solution)/shard_map/ppermute | solution.py:45
  75.8 2.3 %collective-permute-start.47 = (bf16[2,128,1792]{2,1,0:T(8,128)(2,1)S(1)}, bf16[2,128,1792]{2,1,0:T(8,128)(2,1)S(1)}, u32[]{:S(2)}, u32[]{:S(2)}) collective-permute-start(bf16[2,128,1792]{2,1,0:T(8,128)(2,1)S(1)} %get-tuple-element.252.refs_13_), channel_id=1, source_target_pairs={{0,3},{1,2},{2,1},{3,0},{4,7},{5,6},{6,5},{7,4},{8,11},{9,10},{10,... | collective-permute-start | bytes 2752520 | tf_op jit(solution)/shard_map/ppermute | solution.py:45
  80.9 3.1 %collective-permute-start.44 = (bf16[2,128,1792]{2,1,0:T(8,128)(2,1)S(1)}, bf16[2,128,1792]{2,1,0:T(8,128)(2,1)S(1)}, u32[]{:S(2)}, u32[]{:S(2)}) collective-permute-start(bf16[2,128,1792]{2,1,0:T(8,128)(2,1)S(1)} %get-tuple-element.251), channel_id=1, source_target_pairs={{0,24},{1,25},{2,26},{3,27},{4,28},{5,29},{6,30},{7,31},{8,0},{9,1... | collective-permute-start | bytes 2752520 | tf_op jit(solution)/shard_map/ppermute | solution.py:45
  84.0 15.6 %shard_map.143 = (bf16[2,448,1536]{2,1,0:T(8,128)(2,1)S(1)}, bf16[2,448,2048]{2,1,0:T(8,128)(2,1)S(1)}, bf16[2,2048,1792]{2,1,0:T(8,128)(2,1)}) custom-call(bf16[448,1792]{1,0:T(8,128)(2,1)S(1)} %bitcast.25, bf16[448,1792]{1,0:T(8,128)(2,1)S(1)} %bitcast.30, ...), custom_call_target="tpu_custom_call", output_to_operand_aliasing={{0}: (9, {}), {1}: (10, {}), {2}: (11, {})} | custom-call | flops 16441671680 | bytes 22937600 | tf_op jit(solution)/shard_map/pallas_call | solution.py:283
  100.9 5.4 %shard_map.144 = (bf16[2,448,2048]{2,1,0:T(8,128)(2,1)S(1)}, bf16[2,2048,1792]{2,1,0:T(8,128)(2,1)}, bf16[2,448,256]{2,1,0:T(8,128)(2,1)S(1)}) custom-call(bf16[2,448,1792]{2,1,0:T(8,128)(2,1)S(1)} %collective-permute-done.32.refs_2_.refs_0_, ...), custom_call_target="tpu_custom_call", output_to_operand_aliasing={{0}: (5, {}), {1}: (6, {})} | custom-call | flops 5167382528 | bytes 6881280 | tf_op jit(solution)/shard_map/pallas_call | solution.py:475
  106.4 77.0 %conditional.1 = (bf16[448,1792]{1,0:T(8,128)(2,1)}, bf16[448,1792]{1,0:T(8,128)(2,1)}, bf16[448,1792]{1,0:T(8,128)(2,1)}, bf16[448,1792]{1,0:T(8,128)(2,1)}, bf...) conditional(s32[]{:T(128)} %convert_element_type.6, (bf16[2,448,2048]{2,1,0:T(8,128)(2,1)S(1)}, ...), branch_computations={%region_0.1_spmd, %region_1.2_spmd} | conditional | flops 27715960832 | bytes 191890064 | solution.py:744
  106.9 4.9 %branch_1_fun.17 = (bf16[2,448,256]{2,1,0:T(8,128)(2,1)S(1)}, bf16[2,448,256]{2,1,0:T(8,128)(2,1)S(1)}) custom-call(bf16[2,448,2048]{2,1,0:T(8,128)(2,1)S(1)} %get-tuple-element.136.pair, bf16[2,2048,1792]{2,1,0:T(8,128)(2,1)} %get-tuple-element.135.tokens.tokens_in.refs_2_), custom_call_target="tpu_custom_call" | custom-call | flops 3758096384 | bytes 7864320 | tf_op jit(solution)/shard_map/cond/branch_1_fun/pallas_call | solution.py:557
  113.7 6.2 %branch_1_fun.18 = (f32[2,2,448,256]{3,2,1,0:T(8,128)S(1)}, bf16[2,448,512]{2,1,0:T(8,128)(2,1)S(1)}) custom-call(bf16[448,1792]{1,0:T(8,128)(2,1)S(1)} %get-tuple-element.133.up.refs_3_, bf16[448,1792]{1,0:T(8,128)(2,1)S(1)} %get-tuple-element.134.down.refs_6_, bf16[2,2048,1792]{2,1,0:T(8,128)(2,1)S(1)} %copy-done.3, ...), custom_call_target="tpu_custom_call" | custom-call | flops 7046430720 | bytes 6881280 | tf_op jit(solution)/shard_map/cond/branch_1_fun/pallas_call | solution.py:354
  120.1 2.6 %branch_1_fun.19 = (bf16[2,448,256]{2,1,0:T(8,128)(2,1)S(1)}, bf16[448,1792]{1,0:T(8,128)(2,1)}, bf16[448,1792]{1,0:T(8,128)(2,1)}, bf16[448,1792]{1,0:T(8,128)(...) custom-call(f32[2,2,448,256]{3,2,1,0:T(8,128)S(1)} %get-tuple-elemen, ...), custom_call_target="tpu_custom_call", output_to_operand_aliasing={{7}: (9, {})} | custom-call | bytes 6881280 | tf_op jit(solution)/shard_map/cond/branch_1_fun/pallas_call | solution.py:629
  124.0 3.5 %branch_1_fun.20 = (bf16[2,448,256]{2,1,0:T(8,128)(2,1)S(1)}, bf16[2,448,256]{2,1,0:T(8,128)(2,1)S(1)}) custom-call(bf16[2,448,2048]{2,1,0:T(8,128)(2,1)S(1)} %get-tuple-element.136.pair, bf16[2,2048,1792]{2,1,0:T(8,128)(2,1)S(1)} %copy-done.3, bf16[2,448,256]{2,1,0:T(8,128)(2,1)S(1)} %get-tuple-element.153.refs_0_.refs_9_), custom_call_target="tpu_custom_call" | custom-call | flops 3758096384 | bytes 7864320 | tf_op jit(solution)/shard_map/cond/branch_1_fun/pallas_call | solution.py:557
  127.5 2.5 %branch_1_fun.21 = (bf16[2,448,256]{2,1,0:T(8,128)(2,1)S(1)}, bf16[448,1792]{1,0:T(8,128)(2,1)}, bf16[448,1792]{1,0:T(8,128)(2,1)}, bf16[448,1792]{1,0:T(8,128)(...) custom-call(f32[2,2,448,256]{3,2,1,0:T(8,128)S(1)} %get-tuple-elemen, ...), custom_call_target="tpu_custom_call", output_to_operand_aliasing={{1}: (9, {}), {2}: (10, {}), {3}: (11, {}), {4}: (12, {}), ... | custom-call | bytes 6881280 | tf_op jit(solution)/shard_map/cond/branch_1_fun/pallas_call | solution.py:629
  130.8 2.9 %branch_1_fun.22.refs_0_ = f32[2,2,448,256]{3,2,1,0:T(8,128)S(1)} custom-call(bf16[2,448,1536]{2,1,0:T(8,128)(2,1)S(1)} %get-tuple-element.132.pair_in.refs_0_, bf16[2,448,512]{2,1,0:T(8,128)(2,1)S(1)} %get-tuple-element.138.refs_1_, bf16[2,2048,1792]{2,1,0:T(8,128)(2,1)S(1)} %copy-done.3, bf16[2,448,256]{2,1,0:T(8,128)(2,1)S(1)} %get-tuple-element.155.refs_3_.refs_9_), custom_call_target="tpu_custom_call" | custom-call | flops 3758096384 | bytes 7864320 | tf_op jit(solution)/shard_map/cond/branch_1_fun/pallas_call | solution.py:390
  133.7 2.4 %collective-permute-done.18.refs_2_ = bf16[2,448,256]{2,1,0:T(8,128)(2,1)S(1)} collective-permute-done((bf16[2,448,256]{2,1,0:T(8,128)(2,1)S(1)}, bf16[2,448,256]{2,1,0:T(8,128)(2,1)S(1)}, u32[]{:S(2)}, u32[]{:S(2)}) %collective-permute-start.18) | collective-permute-done | bytes 458784 | tf_op jit(solution)/shard_map/cond/branch_1_fun/ppermute | solution.py:45
  136.0 2.7 %branch_1_fun.23 = (bf16[2,448,256]{2,1,0:T(8,128)(2,1)S(1)}, bf16[448,1792]{1,0:T(8,128)(2,1)}, bf16[448,1792]{1,0:T(8,128)(2,1)}, bf16[448,1792]{1,0:T(8,128)(...) custom-call(f32[2,2,448,256]{3,2,1,0:T(8,128)S(1)} %branch_1_fun.22., ...), custom_call_target="tpu_custom_call", output_to_operand_aliasing={{1}: (11, {}), {2}: (12, {}), {3}: (13, {}), {4}: (14, {}),... | custom-call | bytes 6881280 | tf_op jit(solution)/shard_map/cond/branch_1_fun/pallas_call | solution.py:629
  140.1 3.3 %branch_1_fun.25 = (bf16[2,448,256]{2,1,0:T(8,128)(2,1)S(1)}, bf16[2,448,128]{2,1,0:T(8,128)(2,1)S(1)}, bf16[2,448,128]{2,1,0:T(8,128)(2,1)S(1)}) custom-call(bf16[2,448,2048]{2,1,0:T(8,128)(2,1)S(1)} %get-tuple-element.136.pair, bf16[2,2048,1792]{2,1,0:T(8,128)(2,1)S(1)} %copy-done.3, bf16[2,448,256]{2,1,0:T(8,128)(2,1)S(1)} %get-tuple-element.164.refs_3_.refs_0_.refs_9_), custom_call_target="tpu_custom_call" | custom-call | flops 3758096384 | bytes 7864320 | tf_op jit(solution)/shard_map/cond/branch_1_fun/pallas_call | solution.py:557
  143.4 2.5 %collective-permute-done.20.refs_2_ = bf16[2,448,256]{2,1,0:T(8,128)(2,1)S(1)} collective-permute-done((bf16[2,448,256]{2,1,0:T(8,128)(2,1)S(1)}, bf16[2,448,256]{2,1,0:T(8,128)(2,1)S(1)}, u32[]{:S(2)}, u32[]{:S(2)}) %collective-permute-start.20) | collective-permute-done | bytes 458784 | tf_op jit(solution)/shard_map/cond/branch_1_fun/ppermute | solution.py:45
  145.9 2.7 %branch_1_fun.26 = (bf16[2,448,256]{2,1,0:T(8,128)(2,1)S(1)}, bf16[448,1792]{1,0:T(8,128)(2,1)}, bf16[448,1792]{1,0:T(8,128)(2,1)}, bf16[448,1792]{1,0:T(8,128)(...) custom-call(f32[2,2,448,256]{3,2,1,0:T(8,128)S(1)} %branch_1_fun.22., ...), custom_call_target="tpu_custom_call", output_to_operand_aliasing={{1}: (11, {}), {2}: (12, {}), {3}: (13, {}), {4}: (14, {}),... | custom-call | bytes 6881280 | tf_op jit(solution)/shard_map/cond/branch_1_fun/pallas_call | solution.py:629
  149.9 4.3 %branch_1_fun.24.refs_0_ = f32[3,2,448,256]{3,2,1,0:T(8,128)S(1)} custom-call(bf16[2,448,1536]{2,1,0:T(8,128)(2,1)S(1)} %get-tuple-element.132.pair_in.refs_0_, bf16[2,448,512]{2,1,0:T(8,128)(2,1)S(1)} %get-tuple-element.138.refs_1_, bf16[2,2048,1792]{2,1,0:T(8,128)(2,1)S(1)} %copy-done.3, bf16[2,448,256]{2,1,0:T(8,128)(2,1)S(1)} %get-tuple-element.164.refs_3_.refs_0_.refs_9_), custom_call_target="tpu_custom_call" | custom-call | flops 5637144576 | bytes 9961472 | tf_op jit(solution)/shard_map/cond/branch_1_fun/pallas_call | solution.py:390
  155.7 2.7 %branch_1_fun.27 = (bf16[2,448,256]{2,1,0:T(8,128)(2,1)S(1)}, bf16[448,1792]{1,0:T(8,128)(2,1)}, bf16[448,1792]{1,0:T(8,128)(2,1)}, bf16[448,1792]{1,0:T(8,128)(...) custom-call(f32[3,2,448,256]{3,2,1,0:T(8,128)S(1)} %branch_1_fun.24., ...), custom_call_target="tpu_custom_call", output_to_operand_aliasing={{1}: (11, {}), {2}: (12, {}), {3}: (13, {}), {4}: (14, {}),... | custom-call | bytes 6881280 | tf_op jit(solution)/shard_map/cond/branch_1_fun/pallas_call | solution.py:629
  159.7 5.8 %collective-permute-done.22.refs_2_ = bf16[2,448,256]{2,1,0:T(8,128)(2,1)S(1)} collective-permute-done((bf16[2,448,256]{2,1,0:T(8,128)(2,1)S(1)}, bf16[2,448,256]{2,1,0:T(8,128)(2,1)S(1)}, u32[]{:S(2)}, u32[]{:S(2)}) %collective-permute-start.22) | collective-permute-done | bytes 458784 | tf_op jit(solution)/shard_map/cond/branch_1_fun/ppermute | solution.py:45
  165.5 2.7 %branch_1_fun.28 = (bf16[2,448,256]{2,1,0:T(8,128)(2,1)S(1)}, bf16[448,1792]{1,0:T(8,128)(2,1)}, bf16[448,1792]{1,0:T(8,128)(2,1)}, bf16[448,1792]{1,0:T(8,128)(...) custom-call(f32[3,2,448,256]{3,2,1,0:T(8,128)S(1)} %branch_1_fun.24., ...), custom_call_target="tpu_custom_call", output_to_operand_aliasing={{1}: (11, {}), {2}: (12, {}), {3}: (13, {}), {4}: (14, {}),... | custom-call | bytes 6881280 | tf_op jit(solution)/shard_map/cond/branch_1_fun/pallas_call | solution.py:629
  172.3 3.0 %collective-permute-done.26.refs_2_ = bf16[2,448,128]{2,1,0:T(8,128)(2,1)S(1)} collective-permute-done((bf16[2,448,128]{2,1,0:T(8,128)(2,1)S(1)}, bf16[2,448,128]{2,1,0:T(8,128)(2,1)S(1)}, u32[]{:S(2)}, u32[]{:S(2)}) %collective-permute-start.26) | collective-permute-done | bytes 229408 | tf_op jit(solution)/shard_map/cond/branch_1_fun/ppermute | solution.py:45
  (84 shorter events, 40.7 us)
Async XLA Ops:
  3.6 80.4 %collective-permute-start.32 = (bf16[2,448,1792]{2,1,0:T(8,128)(2,1)}, bf16[2,448,1792]{2,1,0:T(8,128)(2,1)S(1)}, u32[]{:S(2)}, u32[]{:S(2)}) collective-permute-start(bf16[2,448,1792]{2,1,0:T(8,128)(2,1)} %shard_map.136), channel_id=1, source_target_pairs={{0,1},{1,0},{2,3},{3,2},{4,5},{5,4},{6,7},{7,6},{8,9},{9,8},{10,11... | collective-permute-start | bytes 9633800 | tf_op jit(solution)/shard_map/ppermute | solution.py:45
  6.5 14.3 %collective-permute-start.39 = (bf16[2,64,1792]{2,1,0:T(8,128)(2,1)S(1)}, bf16[2,64,1792]{2,1,0:T(8,128)(2,1)S(1)}, u32[]{:S(2)}, u32[]{:S(2)}) collective-permute-start(bf16[2,64,1792]{2,1,0:T(8,128)(2,1)S(1)} %get-tuple-element.248.refs_0_), channel_id=1, source_target_pairs={{0,8},{1,9},{2,10},{3,11},{4,12},{5,13},{6,14},{7,15},{8,16},{9,17... | collective-permute-start | bytes 1376264 | tf_op jit(solution)/shard_map/ppermute | solution.py:45
  8.4 12.5 %collective-permute-start.40 = (bf16[2,64,1792]{2,1,0:T(8,128)(2,1)S(1)}, bf16[2,64,1792]{2,1,0:T(8,128)(2,1)S(1)}, u32[]{:S(2)}, u32[]{:S(2)}) collective-permute-start(bf16[2,64,1792]{2,1,0:T(8,128)(2,1)S(1)} %get-tuple-element.248.refs_0_), channel_id=1, source_target_pairs={{0,24},{1,25},{2,26},{3,27},{4,28},{5,29},{6,30},{7,31},{8,0},{9,1... | collective-permute-start | bytes 1376264 | tf_op jit(solution)/shard_map/ppermute | solution.py:45
  10.6 13.6 %collective-permute-start.33 = (bf16[2,64,1792]{2,1,0:T(8,128)(2,1)S(1)}, bf16[2,64,1792]{2,1,0:T(8,128)(2,1)S(1)}, u32[]{:S(2)}, u32[]{:S(2)}) collective-permute-start(bf16[2,64,1792]{2,1,0:T(8,128)(2,1)S(1)} %get-tuple-element.247.refs_0_), channel_id=1, source_target_pairs={{0,4},{1,5},{2,6},{3,7},{4,0},{5,1},{6,2},{7,3},{8,12},{9,13},{10,... | collective-permute-start | bytes 1376264 | tf_op jit(solution)/shard_map/ppermute | solution.py:45
  13.7 12.8 %collective-permute-start.34 = (bf16[2,64,1792]{2,1,0:T(8,128)(2,1)S(1)}, bf16[2,64,1792]{2,1,0:T(8,128)(2,1)S(1)}, u32[]{:S(2)}, u32[]{:S(2)}) collective-permute-start(bf16[2,64,1792]{2,1,0:T(8,128)(2,1)S(1)} %get-tuple-element.247.refs_0_), channel_id=1, source_target_pairs={{0,3},{1,2},{2,1},{3,0},{4,7},{5,6},{6,5},{7,4},{8,11},{9,10},{10,... | collective-permute-start | bytes 1376264 | tf_op jit(solution)/shard_map/ppermute | solution.py:45
  20.8 8.8 %collective-permute-start.41 = (bf16[2,32,1792]{2,1,0:T(8,128)(2,1)S(1)}, bf16[2,32,1792]{2,1,0:T(8,128)(2,1)S(1)}, u32[]{:S(2)}, u32[]{:S(2)}) collective-permute-start(bf16[2,32,1792]{2,1,0:T(8,128)(2,1)S(1)} %slice.18), channel_id=1, source_target_pairs={{0,8},{1,9},{2,10},{3,11},{4,12},{5,13},{6,14},{7,15},{8,16},{9,17... | collective-permute-start | bytes 688136 | tf_op jit(solution)/shard_map/ppermute | solution.py:45
  20.9 8.7 %collective-permute-start.42 = (bf16[2,32,1792]{2,1,0:T(8,128)(2,1)S(1)}, bf16[2,32,1792]{2,1,0:T(8,128)(2,1)S(1)}, u32[]{:S(2)}, u32[]{:S(2)}) collective-permute-start(bf16[2,32,1792]{2,1,0:T(8,128)(2,1)S(1)} %slice.19), channel_id=1, source_target_pairs={{0,24},{1,25},{2,26},{3,27},{4,28},{5,29},{6,30},{7,31},{8,0},{9,1... | collective-permute-start | bytes 688136 | tf_op jit(solution)/shard_map/ppermute | solution.py:45
  24.2 11.0 %collective-permute-start.35 = (bf16[2,32,1792]{2,1,0:T(8,128)(2,1)S(1)}, bf16[2,32,1792]{2,1,0:T(8,128)(2,1)S(1)}, u32[]{:S(2)}, u32[]{:S(2)}) collective-permute-start(bf16[2,32,1792]{2,1,0:T(8,128)(2,1)S(1)} %slice.16), channel_id=1, source_target_pairs={{0,3},{1,2},{2,1},{3,0},{4,7},{5,6},{6,5},{7,4},{8,11},{9,10},{10,... | collective-permute-start | bytes 688136 | tf_op jit(solution)/shard_map/ppermute | solution.py:45
  26.5 8.7 %collective-permute-start.36 = (bf16[2,32,1792]{2,1,0:T(8,128)(2,1)S(1)}, bf16[2,32,1792]{2,1,0:T(8,128)(2,1)S(1)}, u32[]{:S(2)}, u32[]{:S(2)}) collective-permute-start(bf16[2,32,1792]{2,1,0:T(8,128)(2,1)S(1)} %slice.17), channel_id=1, source_target_pairs={{0,4},{1,5},{2,6},{3,7},{4,0},{5,1},{6,2},{7,3},{8,12},{9,13},{10,... | collective-permute-start | bytes 688136 | tf_op jit(solution)/shard_map/ppermute | solution.py:45
  31.1 42.5 %collective-permute-start.45 = (bf16[2,256,1792]{2,1,0:T(8,128)(2,1)}, bf16[2,256,1792]{2,1,0:T(8,128)(2,1)}, u32[]{:S(2)}, u32[]{:S(2)}) collective-permute-start(bf16[2,256,1792]{2,1,0:T(8,128)(2,1)} %shard_map.139.refs_3_.refs_8_), channel_id=1, source_target_pairs={{0,4},{1,5},{2,6},{3,7},{4,0},{5,1},{6,2},{7,3},{8,12},{9,13},{10,... | collective-permute-start | bytes 5505032 | tf_op jit(solution)/shard_map/ppermute | solution.py:45
  33.0 41.2 %collective-permute-start.46 = (bf16[2,256,1792]{2,1,0:T(8,128)(2,1)}, bf16[2,256,1792]{2,1,0:T(8,128)(2,1)}, u32[]{:S(2)}, u32[]{:S(2)}) collective-permute-start(bf16[2,256,1792]{2,1,0:T(8,128)(2,1)} %shard_map.139.refs_3_.refs_8_), channel_id=1, source_target_pairs={{0,3},{1,2},{2,1},{3,0},{4,7},{5,6},{6,5},{7,4},{8,11},{9,10},{10,... | collective-permute-start | bytes 5505032 | tf_op jit(solution)/shard_map/ppermute | solution.py:45
  36.6 41.4 %collective-permute-start.37 = (bf16[2,256,1792]{2,1,0:T(8,128)(2,1)}, bf16[2,256,1792]{2,1,0:T(8,128)(2,1)}, u32[]{:S(2)}, u32[]{:S(2)}) collective-permute-start(bf16[2,256,1792]{2,1,0:T(8,128)(2,1)} %shard_map.138.refs_2_.refs_7_), channel_id=1, source_target_pairs={{0,8},{1,9},{2,10},{3,11},{4,12},{5,13},{6,14},{7,15},{8,16},{9,17... | collective-permute-start | bytes 5505032 | tf_op jit(solution)/shard_map/ppermute | solution.py:45
  36.7 41.3 %collective-permute-start.38 = (bf16[2,256,1792]{2,1,0:T(8,128)(2,1)}, bf16[2,256,1792]{2,1,0:T(8,128)(2,1)}, u32[]{:S(2)}, u32[]{:S(2)}) collective-permute-start(bf16[2,256,1792]{2,1,0:T(8,128)(2,1)} %shard_map.138.refs_2_.refs_7_), channel_id=1, source_target_pairs={{0,24},{1,25},{2,26},{3,27},{4,28},{5,29},{6,30},{7,31},{8,0},{9,1... | collective-permute-start | bytes 5505032 | tf_op jit(solution)/shard_map/ppermute | solution.py:45
  75.8 23.9 %collective-permute-start.47 = (bf16[2,128,1792]{2,1,0:T(8,128)(2,1)S(1)}, bf16[2,128,1792]{2,1,0:T(8,128)(2,1)S(1)}, u32[]{:S(2)}, u32[]{:S(2)}) collective-permute-start(bf16[2,128,1792]{2,1,0:T(8,128)(2,1)S(1)} %get-tuple-element.252.refs_13_), channel_id=1, source_target_pairs={{0,3},{1,2},{2,1},{3,0},{4,7},{5,6},{6,5},{7,4},{8,11},{9,10},{10,... | collective-permute-start | bytes 2752520 | tf_op jit(solution)/shard_map/ppermute | solution.py:45
  79.5 20.9 %collective-permute-start.43 = (bf16[2,128,1792]{2,1,0:T(8,128)(2,1)S(1)}, bf16[2,128,1792]{2,1,0:T(8,128)(2,1)S(1)}, u32[]{:S(2)}, u32[]{:S(2)}) collective-permute-start(bf16[2,128,1792]{2,1,0:T(8,128)(2,1)S(1)} %get-tuple-element.250.refs_12_), channel_id=1, source_target_pairs={{0,8},{1,9},{2,10},{3,11},{4,12},{5,13},{6,14},{7,15},{8,16},{9,17... | collective-permute-start | bytes 2752520 | tf_op jit(solution)/shard_map/ppermute | solution.py:45
  80.0 20.8 %collective-permute-start.48 = (bf16[2,128,1792]{2,1,0:T(8,128)(2,1)S(1)}, bf16[2,128,1792]{2,1,0:T(8,128)(2,1)S(1)}, u32[]{:S(2)}, u32[]{:S(2)}) collective-permute-start(bf16[2,128,1792]{2,1,0:T(8,128)(2,1)S(1)} %get-tuple-element.253), channel_id=1, source_target_pairs={{0,4},{1,5},{2,6},{3,7},{4,0},{5,1},{6,2},{7,3},{8,12},{9,13},{10,... | collective-permute-start | bytes 2752520 | tf_op jit(solution)/shard_map/ppermute | solution.py:45
  80.9 20.0 %collective-permute-start.44 = (bf16[2,128,1792]{2,1,0:T(8,128)(2,1)S(1)}, bf16[2,128,1792]{2,1,0:T(8,128)(2,1)S(1)}, u32[]{:S(2)}, u32[]{:S(2)}) collective-permute-start(bf16[2,128,1792]{2,1,0:T(8,128)(2,1)S(1)} %get-tuple-element.251), channel_id=1, source_target_pairs={{0,24},{1,25},{2,26},{3,27},{4,28},{5,29},{6,30},{7,31},{8,0},{9,1... | collective-permute-start | bytes 2752520 | tf_op jit(solution)/shard_map/ppermute | solution.py:45
  106.6 13.5 %collective-permute-start.17 = (bf16[2,448,256]{2,1,0:T(8,128)(2,1)S(1)}, bf16[2,448,256]{2,1,0:T(8,128)(2,1)S(1)}, u32[]{:S(2)}, u32[]{:S(2)}) collective-permute-start(bf16[2,448,256]{2,1,0:T(8,128)(2,1)S(1)} %get-tuple-element.145), channel_id=1, source_target_pairs={{0,1},{1,0},{2,3},{3,2},{4,5},{5,4},{6,7},{7,6},{8,9},{9,8},{10,11... | collective-permute-start | bytes 1376264 | tf_op jit(solution)/shard_map/cond/branch_1_fun/ppermute | solution.py:45
  111.8 15.7 %collective-permute-start.16 = (bf16[2,448,256]{2,1,0:T(8,128)(2,1)S(1)}, bf16[2,448,256]{2,1,0:T(8,128)(2,1)S(1)}, u32[]{:S(2)}, u32[]{:S(2)}) collective-permute-start(bf16[2,448,256]{2,1,0:T(8,128)(2,1)S(1)} %get-tuple-element.137.refs_0_), channel_id=1, source_target_pairs={{0,1},{1,0},{2,3},{3,2},{4,5},{5,4},{6,7},{7,6},{8,9},{9,8},{10,11... | collective-permute-start | bytes 1376264 | tf_op jit(solution)/shard_map/cond/branch_1_fun/ppermute | solution.py:45
  122.6 11.0 %collective-permute-start.19 = (bf16[2,448,256]{2,1,0:T(8,128)(2,1)S(1)}, bf16[2,448,256]{2,1,0:T(8,128)(2,1)S(1)}, u32[]{:S(2)}, u32[]{:S(2)}) collective-permute-start(bf16[2,448,256]{2,1,0:T(8,128)(2,1)S(1)} %get-tuple-element.153.refs_0_.refs_9_), channel_id=1, source_target_pairs={{0,32},{32,64},{64,96},{96,0},{1,33},{33,65},{65,97},{97,1},{2,34}... | collective-permute-start | bytes 1376264 | tf_op jit(solution)/shard_map/cond/branch_1_fun/ppermute | solution.py:729
  122.6 13.4 %collective-permute-start.18 = (bf16[2,448,256]{2,1,0:T(8,128)(2,1)S(1)}, bf16[2,448,256]{2,1,0:T(8,128)(2,1)S(1)}, u32[]{:S(2)}, u32[]{:S(2)}) collective-permute-start(bf16[2,448,256]{2,1,0:T(8,128)(2,1)S(1)} %get-tuple-element.156), channel_id=1, source_target_pairs={{0,1},{1,0},{2,3},{3,2},{4,5},{5,4},{6,7},{7,6},{8,9},{9,8},{10,11... | collective-permute-start | bytes 1376264 | tf_op jit(solution)/shard_map/cond/branch_1_fun/ppermute | solution.py:45
  130.0 15.9 %collective-permute-start.20 = (bf16[2,448,256]{2,1,0:T(8,128)(2,1)S(1)}, bf16[2,448,256]{2,1,0:T(8,128)(2,1)S(1)}, u32[]{:S(2)}, u32[]{:S(2)}) collective-permute-start(bf16[2,448,256]{2,1,0:T(8,128)(2,1)S(1)} %get-tuple-element.165), channel_id=1, source_target_pairs={{0,1},{1,0},{2,3},{3,2},{4,5},{5,4},{6,7},{7,6},{8,9},{9,8},{10,11... | collective-permute-start | bytes 1376264 | tf_op jit(solution)/shard_map/cond/branch_1_fun/ppermute | solution.py:45
  130.6 15.3 %collective-permute-start.21 = (bf16[2,448,256]{2,1,0:T(8,128)(2,1)S(1)}, bf16[2,448,256]{2,1,0:T(8,128)(2,1)S(1)}, u32[]{:S(2)}, u32[]{:S(2)}) collective-permute-start(bf16[2,448,256]{2,1,0:T(8,128)(2,1)S(1)} %get-tuple-element.155.refs_3_.refs_9_), channel_id=1, source_target_pairs={{0,32},{32,64},{64,96},{96,0},{1,33},{33,65},{65,97},{97,1},{2,34}... | collective-permute-start | bytes 1376264 | tf_op jit(solution)/shard_map/cond/branch_1_fun/ppermute | solution.py:729
  138.7 17.0 %collective-permute-start.24 = (bf16[2,448,256]{2,1,0:T(8,128)(2,1)S(1)}, bf16[2,448,256]{2,1,0:T(8,128)(2,1)S(1)}, u32[]{:S(2)}, u32[]{:S(2)}) collective-permute-start(bf16[2,448,256]{2,1,0:T(8,128)(2,1)S(1)} %get-tuple-element.175), channel_id=1, source_target_pairs={{0,1},{1,0},{2,3},{3,2},{4,5},{5,4},{6,7},{7,6},{8,9},{9,8},{10,11... | collective-permute-start | bytes 1376264 | tf_op jit(solution)/shard_map/cond/branch_1_fun/ppermute | solution.py:45
  140.1 15.6 %collective-permute-start.25 = (bf16[2,448,256]{2,1,0:T(8,128)(2,1)S(1)}, bf16[2,448,256]{2,1,0:T(8,128)(2,1)S(1)}, u32[]{:S(2)}, u32[]{:S(2)}) collective-permute-start(bf16[2,448,256]{2,1,0:T(8,128)(2,1)S(1)} %get-tuple-element.164.refs_3_.refs_0_.refs_9_), channel_id=1, source_target_pairs={{0,32},{32,64},{64,96},{96,0},{1,33},{33,65},{65,97},{97,1},{2,34}... | collective-permute-start | bytes 1376264 | tf_op jit(solution)/shard_map/cond/branch_1_fun/ppermute | solution.py:729
  148.5 17.0 %collective-permute-start.22 = (bf16[2,448,256]{2,1,0:T(8,128)(2,1)S(1)}, bf16[2,448,256]{2,1,0:T(8,128)(2,1)S(1)}, u32[]{:S(2)}, u32[]{:S(2)}) collective-permute-start(bf16[2,448,256]{2,1,0:T(8,128)(2,1)S(1)} %get-tuple-element.173), channel_id=1, source_target_pairs={{0,1},{1,0},{2,3},{3,2},{4,5},{5,4},{6,7},{7,6},{8,9},{9,8},{10,11... | collective-permute-start | bytes 1376264 | tf_op jit(solution)/shard_map/cond/branch_1_fun/ppermute | solution.py:45
  149.9 15.6 %collective-permute-start.23 = (bf16[2,448,256]{2,1,0:T(8,128)(2,1)S(1)}, bf16[2,448,256]{2,1,0:T(8,128)(2,1)S(1)}, u32[]{:S(2)}, u32[]{:S(2)}) collective-permute-start(bf16[2,448,256]{2,1,0:T(8,128)(2,1)S(1)} %get-tuple-element.174.refs_9_), channel_id=1, source_target_pairs={{0,32},{32,64},{64,96},{96,0},{1,33},{33,65},{65,97},{97,1},{2,34}... | collective-permute-start | bytes 1376264 | tf_op jit(solution)/shard_map/cond/branch_1_fun/ppermute | solution.py:729
  158.4 11.8 %collective-permute-start.28 = (bf16[2,448,256]{2,1,0:T(8,128)(2,1)S(1)}, bf16[2,448,256]{2,1,0:T(8,128)(2,1)S(1)}, u32[]{:S(2)}, u32[]{:S(2)}) collective-permute-start(bf16[2,448,256]{2,1,0:T(8,128)(2,1)S(1)} %get-tuple-element.192.refs_9_), channel_id=1, source_target_pairs={{0,32},{32,64},{64,96},{96,0},{1,33},{33,65},{65,97},{97,1},{2,34}... | collective-permute-start | bytes 1376264 | tf_op jit(solution)/shard_map/cond/branch_1_fun/ppermute | solution.py:729
  158.4 11.8 %collective-permute-start.27 = (bf16[2,448,128]{2,1,0:T(8,128)(2,1)S(1)}, bf16[2,448,128]{2,1,0:T(8,128)(2,1)S(1)}, u32[]{:S(2)}, u32[]{:S(2)}) collective-permute-start(bf16[2,448,128]{2,1,0:T(8,128)(2,1)S(1)} %get-tuple-element.191), channel_id=1, source_target_pairs={{0,1},{1,0},{2,3},{3,2},{4,5},{5,4},{6,7},{7,6},{8,9},{9,8},{10,11... | collective-permute-start | bytes 688136 | tf_op jit(solution)/shard_map/cond/branch_1_fun/ppermute | solution.py:45
  168.2 7.0 %collective-permute-start.26 = (bf16[2,448,128]{2,1,0:T(8,128)(2,1)S(1)}, bf16[2,448,128]{2,1,0:T(8,128)(2,1)S(1)}, u32[]{:S(2)}, u32[]{:S(2)}) collective-permute-start(bf16[2,448,128]{2,1,0:T(8,128)(2,1)S(1)} %get-tuple-element.190), channel_id=1, source_target_pairs={{0,1},{1,0},{2,3},{3,2},{4,5},{5,4},{6,7},{7,6},{8,9},{9,8},{10,11... | collective-permute-start | bytes 688136 | tf_op jit(solution)/shard_map/cond/branch_1_fun/ppermute | solution.py:45
  169.6 7.9 %collective-permute-start.31 = (bf16[2,448,256]{2,1,0:T(8,128)(2,1)S(1)}, bf16[2,448,256]{2,1,0:T(8,128)(2,1)S(1)}, u32[]{:S(2)}, u32[]{:S(2)}) collective-permute-start(bf16[2,448,256]{2,1,0:T(8,128)(2,1)S(1)} %get-tuple-element.207.own), channel_id=1, source_target_pairs={{0,32},{32,64},{64,96},{96,0},{1,33},{33,65},{65,97},{97,1},{2,34}... | collective-permute-start | bytes 1376264 | tf_op jit(solution)/shard_map/cond/branch_1_fun/ppermute | solution.py:729
  172.3 7.7 %collective-permute-start.30 = (bf16[2,448,128]{2,1,0:T(8,128)(2,1)S(1)}, bf16[2,448,128]{2,1,0:T(8,128)(2,1)S(1)}, u32[]{:S(2)}, u32[]{:S(2)}) collective-permute-start(bf16[2,448,128]{2,1,0:T(8,128)(2,1)S(1)} %get-tuple-element.206.own), channel_id=1, source_target_pairs={{0,32},{32,64},{64,96},{96,0},{1,33},{33,65},{65,97},{97,1},{2,34}... | collective-permute-start | bytes 688136 | tf_op jit(solution)/shard_map/cond/branch_1_fun/ppermute | solution.py:729
  (10 other events, 60.2 us)

commit v4 on v3

--- a/solution.py
+++ b/solution.py
@@ -210,7 +210,7 @@
     )(*operands)
 
 
-def hidden_kernel(jobs, sizes, pieces, skipped, kept, tile, both, *refs):
+def hidden_kernel(jobs, sizes, pieces, skipped, kept, tile, both, chunk, *refs):
     arrays = refs[: len(pieces)]
     blocks = refs[len(pieces) : len(pieces) + len(sizes)]
     refs = refs[len(pieces) + len(sizes) + skipped :]
@@ -222,22 +222,27 @@
         if which is not None:
             target = weights.at[which, pl.ds(first, rows)]
         loads.append(pltpu.make_async_copy(ref, target, weight_sem.at[k]))
-    first = 0
+    first, arriving = 0, {}
     for k, (ref, count) in enumerate(zip(blocks, sizes)):
-        loads.append(pltpu.make_async_copy(ref, tokens.at[:, pl.ds(first, count)], token_sem.at[k]))
+        load = pltpu.make_async_copy(ref, tokens.at[:, pl.ds(first, count)], token_sem.at[k])
+        at = first // tile
+        at = at * (top // HELD) if at < both else at + (top // HELD - 1) * both
+        arriving.setdefault(at, []).append(load)
         first += count
-    for load in loads:
+    for load in [*arriving[0], *loads, *sum((l for at, l in arriving.items() if at), [])]:
         load.start()
     for load in loads:
         load.wait()
     stores = []
-    if kept is not None:
-        source = tokens.at[:, pl.ds(0, kept[1])]
-        target = refs[2].at[:, pl.ds(kept[0], kept[1])]
-        stores.append(pltpu.make_async_copy(source, target, keep_sem.at[0]))
-        stores[-1].start()
 
     def step(i, carry):
+        for at, expected in arriving.items():
+
+            @pl.when(i == at)
+            def _(expected=expected):
+                for load in expected:
+                    load.wait()
+
         blocks = top // HELD
         here = i < blocks * both
         row = jnp.where(here, i % blocks, blocks - 1) * HELD
@@ -265,26 +270,41 @@
             )
         )
         stores[-1].start()
+    if kept is not None:
+        source = tokens.at[:, pl.ds(0, kept[1])]
+        target = refs[2].at[:, pl.ds(kept[0], kept[1])]
+        stores.append(pltpu.make_async_copy(source, target, keep_sem.at[0]))
+        stores[-1].start()
+    if chunk:
+
+        def multiply(which, carry):
+            refs[3][which] = jnp.dot(
+                pair[which, HELD:], tokens[which, :, :WIDTH], preferred_element_type=jnp.float32
+            )
+            return carry
+
+        lax.fori_loop(0, 2, multiply, 0)
     for store in stores:
         store.wait()
 
 
-def hidden_step(jobs, pieces, arrays, blocks, results, kept, both, after=()):
+def hidden_step(jobs, pieces, arrays, blocks, results, kept, both, after=(), chunk=False):
     sizes = tuple(b.shape[1] for b in blocks)
     total = sum(sizes)
     top = max(first + rows for _, first, rows in pieces)
     shapes = ((2, HELD, EARLY), (2, HELD, TOKENS), (2, TOKENS, D))
     out = [jax.ShapeDtypeStruct(shape, jnp.bfloat16) for shape in shapes]
+    out += [jax.ShapeDtypeStruct((2, HELD, WIDTH), jnp.float32)] * chunk
     operands = [*arrays, *blocks]
     aliases = {len(operands) + k: k for k in range(len(results))}
     operands += [*results, *after]
     flops = sum(4 * HELD * count * D for _, _, count, _ in jobs)
     skipped = len(results) + len(after)
     return pl.pallas_call(
-        functools.partial(hidden_kernel, jobs, sizes, pieces, skipped, kept, 512, both),
+        functools.partial(hidden_kernel, jobs, sizes, pieces, skipped, kept, 512, both, chunk),
         out_shape=out,
         in_specs=[ANY] * len(operands),
-        out_specs=[ANY] * 3,
+        out_specs=[ANY] * 3 + [INSIDE] * chunk,
         input_output_aliases=aliases,
         scratch_shapes=[
             pltpu.VMEM((2, top, D), jnp.bfloat16),
@@ -406,8 +426,8 @@
 
 def last_shared_kernel(*refs):
     weights_in, blocks = refs[0], refs[1:5]
-    pair_in, tokens_in, pair_out, tokens_out, chunk = refs[5:10]
-    weights, tokens, pair, columns, sem, out_sem = refs[10:]
+    partial, pair_out, tokens_out, chunk = refs[7:11]
+    weights, tokens, pair, early, sem, out_sem = refs[11:]
     first, width = 0, WIDTH
     rest = TOKENS - EARLY
     weights_load = pltpu.make_async_copy(weights_in, weights, sem.at[0])
@@ -416,12 +436,8 @@
         rows = ref.shape[1]
         loads.append(pltpu.make_async_copy(ref, tokens.at[:, pl.ds(row, rows)], sem.at[1 + k]))
         row += rows
-    early, late = pl.ds(0, EARLY), pl.ds(EARLY, rest)
-    source = tokens_in.at[:, early, pl.ds(first, width)]
-    more = [
-        pltpu.make_async_copy(pair_in.at[:, :, early], pair.at[:, :, early], sem.at[5]),
-        pltpu.make_async_copy(source, columns, sem.at[6]),
-    ]
+    late = pl.ds(EARLY, rest)
+    more = [pltpu.make_async_copy(partial, early, sem.at[5])]
     for load in [*loads[:2], weights_load, *loads[2:], *more]:
         load.start()
     weights_load.wait()
@@ -429,7 +445,6 @@
 
     def step(i, carry):
         at = pl.ds(pl.multiple_of(i * tile, tile), tile)
-        to = pl.ds(pl.multiple_of(EARLY + i * tile, tile), tile)
         pre = up_scale * lax.dot_general(
             weights[0], tokens[0, at], contract_last, preferred_element_type=jnp.float32
         )
@@ -437,8 +452,8 @@
             weights[1], tokens[1, at], contract_last, preferred_element_type=jnp.float32
         )
         value, slope = gelu_pair(pre)
-        pair[0, :, to] = (back * slope).astype(jnp.bfloat16)
-        pair[1, :, to] = value.astype(jnp.bfloat16)
+        pair[0, :, at] = (back * slope).astype(jnp.bfloat16)
+        pair[1, :, at] = value.astype(jnp.bfloat16)
         return carry
 
     def arriving(i, carry):
@@ -454,14 +469,13 @@
     lax.fori_loop(0, rest // tile, arriving, 0)
     stores = [pltpu.make_async_copy(tokens, tokens_out.at[:, late], out_sem.at[0])]
     stores[0].start()
-    stores.append(pltpu.make_async_copy(pair.at[:, :, late], pair_out.at[:, :, late], out_sem.at[1]))
+    stores.append(pltpu.make_async_copy(pair, pair_out.at[:, :, late], out_sem.at[1]))
     stores[1].start()
     for load in more:
         load.wait()
     for which, scale in enumerate((up_scale, down_scale)):
-        grad = jnp.dot(pair[which, :, :EARLY], columns[which], preferred_element_type=jnp.float32)
-        grad += jnp.dot(
-            pair[which, :, EARLY:],
+        grad = early[which] + jnp.dot(
+            pair[which],
             tokens[which, :, first : first + width],
             preferred_element_type=jnp.float32,
         )
@@ -470,7 +484,7 @@
         store.wait()
 
 
-def last_shared(weights, blocks, pair, tokens):
+def last_shared(weights, blocks, pair, tokens, partial):
     width = WIDTH
     return pl.pallas_call(
         last_shared_kernel,
@@ -479,22 +493,22 @@
             jax.ShapeDtypeStruct((2, TOKENS, D), jnp.bfloat16),
             jax.ShapeDtypeStruct((2, HELD, width), jnp.bfloat16),
         ],
-        in_specs=[ANY] * 7,
+        in_specs=[ANY] * 8,
         out_specs=[ANY] * 2 + [INSIDE],
         input_output_aliases={5: 0, 6: 1},
         scratch_shapes=[
             pltpu.VMEM((2, HELD, D), jnp.bfloat16),
             pltpu.VMEM((2, TOKENS - EARLY, D), jnp.bfloat16),
-            pltpu.VMEM((2, HELD, TOKENS), jnp.bfloat16),
-            pltpu.VMEM((2, EARLY, width), jnp.bfloat16),
-            pltpu.SemaphoreType.DMA((7,)),
+            pltpu.VMEM((2, HELD, TOKENS - EARLY), jnp.bfloat16),
+            pltpu.VMEM((2, HELD, width), jnp.float32),
+            pltpu.SemaphoreType.DMA((6,)),
             pltpu.SemaphoreType.DMA((2,)),
         ],
         compiler_params=vmem(16),
         cost_estimate=cost(
             4 * HELD * ((TOKENS - EARLY) * D + TOKENS * width), 4 * (HELD + TOKENS - EARLY) * D
         ),
-    )(weights, *blocks, pair, tokens)
+    )(weights, *blocks, pair, tokens, partial)
 
 
 def column_spec(c):
@@ -702,6 +716,7 @@
         (512, 1024),
         2,
         halves[::2],
+        True,
     )
     own_pair = results[0]
     pair, tokens, theirs = last_shared(weights_sent, last, *results[1:])

time: 184 us -> 186 us (1.011); the launches traced: 183 us -> 190 us
  waiting for transfers between devices: 54 us -> 60 us
    ppermute x8, waiting for transfers between devices: 3.68 us -> 10.5 us  [finish(): others.append(lax.ppermute(out[0], 'rep', route))]
    ppermute x25, starting transfers between devices: 43.7 us -> 39 us  [moved(): return lax.ppermute(block, 'fsdp', route)]
    ppermute x8, starting transfers between devices: 0.17 us -> 4.37 us  [finish(): others.append(lax.ppermute(out[0], 'rep', route))]
    pallas_call x2, Pallas kernels: 20.8 us -> 22.9 us  [hidden_step(): pl.pallas_call(functools.partial(hidden_kernel, jobs, sizes, pieces, skip...]
  transfers between devices with their start and end apart: 33 -> 33, of which waited for: 16 -> 17; matrix products, arithmetic and copies ran while one was open for 0% -> 0% of each run, Pallas kernels for 40% -> 40%
where the time goes in v4:
time: 186 us; the launch traced here: 190 us
  Pallas kernels  84.4 us (45%)
  waiting for transfers between devices  60 us (32%)
  starting transfers between devices  43.4 us (23%)
    ppermute x25, waiting for transfers between devices, moved(): return lax.ppermute(block, 'fsdp', route)  49.5 us
    ppermute x25, starting transfers between devices, moved(): return lax.ppermute(block, 'fsdp', route)  39 us
    pallas_call x2, Pallas kernels, hidden_step(): pl.pallas_call(functools.partial(hidden_kernel, jobs, sizes, pieces, skip...  22.9 us
    pallas_call x8, Pallas kernels, adam_chunk(): pl.pallas_call(functools.partial(adam_kernel, (bool(mixed), len(passing))...  19.7 us
    pallas_call x3, Pallas kernels, theirs_chunks(): pl.pallas_call(functools.partial(theirs_kernel, targets, len(after)), out...  11.6 us
    ppermute x8, waiting for transfers between devices, finish(): others.append(lax.ppermute(out[0], 'rep', route))  10.5 us
    pallas_call x2, Pallas kernels, own_rest(): pl.pallas_call(kernel, out_shape=jax.ShapeDtypeStruct((count, 2, HELD, WI...  7.21 us
    pallas_call x1, Pallas kernels, own_first(): pl.pallas_call(own_first_kernel, out_shape=[jax.ShapeDtypeStruct((FIRST_O...  6.24 us
  transfers between devices with their start and end apart: 33, of which 17 were waited for; matrix products, arithmetic and copies ran while one was open for 0% of the time, Pallas kernels for 40%

profile of v4, /device:TPU:0, one launch (start us, length us, event | category | flops | bytes accessed | tf_op | source)
XLA Modules:
  0.0 189.8 jit_solution(18044889171882381071)
XLA Ops:
  0.7 3.0 %shard_map.136 = bf16[2,448,1792]{2,1,0:T(8,128)(2,1)} custom-call(bf16[448,1792]{1,0:T(8,128)(2,1)} %bitcast.23, bf16[448,1792]{1,0:T(8,128)(2,1)} %bitcast.28), custom_call_target="tpu_custom_call" | custom-call | bytes 6422528 | tf_op jit(solution)/shard_map/pallas_call | solution.py:156
  10.6 3.0 %collective-permute-start.33 = (bf16[2,64,1792]{2,1,0:T(8,128)(2,1)S(1)}, bf16[2,64,1792]{2,1,0:T(8,128)(2,1)S(1)}, u32[]{:S(2)}, u32[]{:S(2)}) collective-permute-start(bf16[2,64,1792]{2,1,0:T(8,128)(2,1)S(1)} %get-tuple-element.248.refs_0_), channel_id=1, source_target_pairs={{0,4},{1,5},{2,6},{3,7},{4,0},{5,1},{6,2},{7,3},{8,12},{9,13},{10,... | collective-permute-start | bytes 1376264 | tf_op jit(solution)/shard_map/ppermute | solution.py:45
  15.9 5.0 %collective-permute-done.39.refs_1_ = bf16[2,64,1792]{2,1,0:T(8,128)(2,1)S(1)} collective-permute-done((bf16[2,64,1792]{2,1,0:T(8,128)(2,1)S(1)}, bf16[2,64,1792]{2,1,0:T(8,128)(2,1)S(1)}, u32[]{:S(2)}, u32[]{:S(2)}) %collective-permute-start.39) | collective-permute-done | bytes 458784 | tf_op jit(solution)/shard_map/ppermute | solution.py:45
  20.9 3.3 %collective-permute-start.42 = (bf16[2,32,1792]{2,1,0:T(8,128)(2,1)S(1)}, bf16[2,32,1792]{2,1,0:T(8,128)(2,1)S(1)}, u32[]{:S(2)}, u32[]{:S(2)}) collective-permute-start(bf16[2,32,1792]{2,1,0:T(8,128)(2,1)S(1)} %slice.19), channel_id=1, source_target_pairs={{0,24},{1,25},{2,26},{3,27},{4,28},{5,29},{6,30},{7,31},{8,0},{9,1... | collective-permute-start | bytes 688136 | tf_op jit(solution)/shard_map/ppermute | solution.py:45
  24.2 2.3 %collective-permute-start.35 = (bf16[2,32,1792]{2,1,0:T(8,128)(2,1)S(1)}, bf16[2,32,1792]{2,1,0:T(8,128)(2,1)S(1)}, u32[]{:S(2)}, u32[]{:S(2)}) collective-permute-start(bf16[2,32,1792]{2,1,0:T(8,128)(2,1)S(1)} %slice.16), channel_id=1, source_target_pairs={{0,3},{1,2},{2,1},{3,0},{4,7},{5,6},{6,5},{7,4},{8,11},{9,10},{10,... | collective-permute-start | bytes 688136 | tf_op jit(solution)/shard_map/ppermute | solution.py:45
  26.5 3.1 %collective-permute-start.36 = (bf16[2,32,1792]{2,1,0:T(8,128)(2,1)S(1)}, bf16[2,32,1792]{2,1,0:T(8,128)(2,1)S(1)}, u32[]{:S(2)}, u32[]{:S(2)}) collective-permute-start(bf16[2,32,1792]{2,1,0:T(8,128)(2,1)S(1)} %slice.17), channel_id=1, source_target_pairs={{0,4},{1,5},{2,6},{3,7},{4,0},{5,1},{6,2},{7,3},{8,12},{9,13},{10,... | collective-permute-start | bytes 688136 | tf_op jit(solution)/shard_map/ppermute | solution.py:45
  36.7 3.1 %collective-permute-start.38 = (bf16[2,256,1792]{2,1,0:T(8,128)(2,1)}, bf16[2,256,1792]{2,1,0:T(8,128)(2,1)}, u32[]{:S(2)}, u32[]{:S(2)}) collective-permute-start(bf16[2,256,1792]{2,1,0:T(8,128)(2,1)} %shard_map.138.refs_2_.refs_7_), channel_id=1, source_target_pairs={{0,24},{1,25},{2,26},{3,27},{4,28},{5,29},{6,30},{7,31},{8,0},{9,1... | collective-permute-start | bytes 5505032 | tf_op jit(solution)/shard_map/ppermute | solution.py:45
  40.7 7.0 %shard_map.140 = (bf16[2,448,1536]{2,1,0:T(8,128)(2,1)S(1)}, bf16[2,448,2048]{2,1,0:T(8,128)(2,1)S(1)}, bf16[2,2048,1792]{2,1,0:T(8,128)(2,1)}) custom-call(bf16[448,1792]{1,0:T(8,128)(2,1)} %bitcast.24, bf16[448,1792]{1,0:T(8,128)(2,1)} %bitcast.29, bf16[2,256,1792]{2,1,0:T(8,128)(2,1)} %shard_map.138.refs_2_.refs_7_, ...), custom_call_target="tpu_custom_call" | custom-call | flops 3288334336 | bytes 7798784 | tf_op jit(solution)/shard_map/pallas_call | solution.py:303
  47.8 25.8 %collective-permute-done.45.refs_0_.refs_5_ = bf16[2,256,1792]{2,1,0:T(8,128)(2,1)} collective-permute-done((bf16[2,256,1792]{2,1,0:T(8,128)(2,1)}, bf16[2,256,1792]{2,1,0:T(8,128)(2,1)}, u32[]{:S(2)}, u32[]{:S(2)}) %collective-permute-start.45) | collective-permute-done | bytes 1835040 | tf_op jit(solution)/shard_map/ppermute | solution.py:45
  75.8 2.3 %collective-permute-start.47 = (bf16[2,128,1792]{2,1,0:T(8,128)(2,1)S(1)}, bf16[2,128,1792]{2,1,0:T(8,128)(2,1)S(1)}, u32[]{:S(2)}, u32[]{:S(2)}) collective-permute-start(bf16[2,128,1792]{2,1,0:T(8,128)(2,1)S(1)} %get-tuple-element.253.refs_13_), channel_id=1, source_target_pairs={{0,3},{1,2},{2,1},{3,0},{4,7},{5,6},{6,5},{7,4},{8,11},{9,10},{10,... | collective-permute-start | bytes 2752520 | tf_op jit(solution)/shard_map/ppermute | solution.py:45
  80.9 3.1 %collective-permute-start.44 = (bf16[2,128,1792]{2,1,0:T(8,128)(2,1)S(1)}, bf16[2,128,1792]{2,1,0:T(8,128)(2,1)S(1)}, u32[]{:S(2)}, u32[]{:S(2)}) collective-permute-start(bf16[2,128,1792]{2,1,0:T(8,128)(2,1)S(1)} %get-tuple-element.252), channel_id=1, source_target_pairs={{0,24},{1,25},{2,26},{3,27},{4,28},{5,29},{6,30},{7,31},{8,0},{9,1... | collective-permute-start | bytes 2752520 | tf_op jit(solution)/shard_map/ppermute | solution.py:45
  84.0 15.9 %shard_map.143 = (bf16[2,448,1536]{2,1,0:T(8,128)(2,1)S(1)}, bf16[2,448,2048]{2,1,0:T(8,128)(2,1)S(1)}, bf16[2,2048,1792]{2,1,0:T(8,128)(2,1)}, f32[2,448,256]{2,1,0:T(8,128)S(1)}) custom-call(bf16[448,1792]{1,0:T(8,128)(2,1)S(1)} %bitcast.25, bf16[448,1792]{1,0:T(8,128)(2,1)S(1)} %bitcast.30, ...), custom_call_target="tpu_custom_call", output_to_operand_aliasing={{0}: (9, {}), {1}: (10, {}), {2}: (11, {})} | custom-call | flops 16441671680 | bytes 22937600 | tf_op jit(solution)/shard_map/pallas_call | solution.py:303
  100.9 4.3 %shard_map.144 = (bf16[2,448,2048]{2,1,0:T(8,128)(2,1)S(1)}, bf16[2,2048,1792]{2,1,0:T(8,128)(2,1)}, bf16[2,448,256]{2,1,0:T(8,128)(2,1)S(1)}) custom-call(bf16[2,448,1792]{2,1,0:T(8,128)(2,1)S(1)} %collective-permute-done.32.refs_2_.refs_0_, ...), custom_call_target="tpu_custom_call", output_to_operand_aliasing={{0}: (5, {}), {1}: (6, {})} | custom-call | flops 5167382528 | bytes 6881280 | tf_op jit(solution)/shard_map/pallas_call | solution.py:489
  105.3 84.5 %conditional.1 = (bf16[448,1792]{1,0:T(8,128)(2,1)}, bf16[448,1792]{1,0:T(8,128)(2,1)}, bf16[448,1792]{1,0:T(8,128)(2,1)}, bf16[448,1792]{1,0:T(8,128)(2,1)}, bf...) conditional(s32[]{:T(128)} %convert_element_type.6, (bf16[2,448,2048]{2,1,0:T(8,128)(2,1)S(1)}, ...), branch_computations={%region_0.1_spmd, %region_1.2_spmd} | conditional | flops 27715960832 | bytes 191890064 | solution.py:759
  105.7 4.9 %branch_0_fun.17 = (bf16[2,448,256]{2,1,0:T(8,128)(2,1)S(1)}, bf16[2,448,256]{2,1,0:T(8,128)(2,1)S(1)}) custom-call(bf16[2,448,2048]{2,1,0:T(8,128)(2,1)S(1)} %get-tuple-element.48.pair, bf16[2,2048,1792]{2,1,0:T(8,128)(2,1)} %get-tuple-element.47.tokens.tokens_in.refs_2_), custom_call_target="tpu_custom_call" | custom-call | flops 3758096384 | bytes 7864320 | tf_op jit(solution)/shard_map/cond/branch_0_fun/pallas_call | solution.py:571
  112.6 6.2 %branch_0_fun.18 = (f32[2,2,448,256]{3,2,1,0:T(8,128)S(1)}, bf16[2,448,512]{2,1,0:T(8,128)(2,1)S(1)}) custom-call(bf16[448,1792]{1,0:T(8,128)(2,1)S(1)} %get-tuple-element.45.up.refs_3_, bf16[448,1792]{1,0:T(8,128)(2,1)S(1)} %get-tuple-element.46.down.refs_6_, bf16[2,2048,1792]{2,1,0:T(8,128)(2,1)S(1)} %copy-done.2, ...), custom_call_target="tpu_custom_call" | custom-call | flops 7046430720 | bytes 6881280 | tf_op jit(solution)/shard_map/cond/branch_0_fun/pallas_call | solution.py:374
  118.9 2.6 %branch_0_fun.19 = (bf16[2,448,256]{2,1,0:T(8,128)(2,1)S(1)}, bf16[448,1792]{1,0:T(8,128)(2,1)}, bf16[448,1792]{1,0:T(8,128)(2,1)}, bf16[448,1792]{1,0:T(8,128)(...) custom-call(f32[2,2,448,256]{3,2,1,0:T(8,128)S(1)} %get-tuple-elemen, ...), custom_call_target="tpu_custom_call", output_to_operand_aliasing={{7}: (9, {})} | custom-call | bytes 6881280 | tf_op jit(solution)/shard_map/cond/branch_0_fun/pallas_call | solution.py:643
  123.5 3.5 %branch_0_fun.20 = (bf16[2,448,256]{2,1,0:T(8,128)(2,1)S(1)}, bf16[2,448,256]{2,1,0:T(8,128)(2,1)S(1)}) custom-call(bf16[2,448,2048]{2,1,0:T(8,128)(2,1)S(1)} %get-tuple-element.48.pair, bf16[2,2048,1792]{2,1,0:T(8,128)(2,1)S(1)} %copy-done.2, bf16[2,448,256]{2,1,0:T(8,128)(2,1)S(1)} %get-tuple-element.65.refs_0_.refs_9_), custom_call_target="tpu_custom_call" | custom-call | flops 3758096384 | bytes 7864320 | tf_op jit(solution)/shard_map/cond/branch_0_fun/pallas_call | solution.py:571
  128.1 2.4 %branch_0_fun.21 = (bf16[2,448,256]{2,1,0:T(8,128)(2,1)S(1)}, bf16[448,1792]{1,0:T(8,128)(2,1)}, bf16[448,1792]{1,0:T(8,128)(2,1)}, bf16[448,1792]{1,0:T(8,128)(...) custom-call(f32[2,2,448,256]{3,2,1,0:T(8,128)S(1)} %get-tuple-elemen, ...), custom_call_target="tpu_custom_call", output_to_operand_aliasing={{1}: (9, {}), {2}: (10, {}), {3}: (11, {}), {4}: (12, {}), ... | custom-call | bytes 6881280 | tf_op jit(solution)/shard_map/cond/branch_0_fun/pallas_call | solution.py:643
  131.5 2.9 %branch_0_fun.22.refs_0_ = f32[2,2,448,256]{3,2,1,0:T(8,128)S(1)} custom-call(bf16[2,448,1536]{2,1,0:T(8,128)(2,1)S(1)} %get-tuple-element.44.pair_in.refs_0_, bf16[2,448,512]{2,1,0:T(8,128)(2,1)S(1)} %get-tuple-element.50.refs_1_, bf16[2,2048,1792]{2,1,0:T(8,128)(2,1)S(1)} %copy-done.2, bf16[2,448,256]{2,1,0:T(8,128)(2,1)S(1)} %get-tuple-element.67.refs_3_.refs_9_), custom_call_target="tpu_custom_call" | custom-call | flops 3758096384 | bytes 7864320 | tf_op jit(solution)/shard_map/cond/branch_0_fun/pallas_call | solution.py:410
  134.4 3.5 %collective-permute-done.2.refs_2_ = bf16[2,448,256]{2,1,0:T(8,128)(2,1)S(1)} collective-permute-done((bf16[2,448,256]{2,1,0:T(8,128)(2,1)S(1)}, bf16[2,448,256]{2,1,0:T(8,128)(2,1)S(1)}, u32[]{:S(2)}, u32[]{:S(2)}) %collective-permute-start.2) | collective-permute-done | bytes 458784 | tf_op jit(solution)/shard_map/cond/branch_0_fun/ppermute | solution.py:45
  137.9 2.7 %branch_0_fun.23 = (bf16[2,448,256]{2,1,0:T(8,128)(2,1)S(1)}, bf16[448,1792]{1,0:T(8,128)(2,1)}, bf16[448,1792]{1,0:T(8,128)(2,1)}, bf16[448,1792]{1,0:T(8,128)(...) custom-call(f32[2,2,448,256]{3,2,1,0:T(8,128)S(1)} %branch_0_fun.22., ...), custom_call_target="tpu_custom_call", output_to_operand_aliasing={{1}: (11, {}), {2}: (12, {}), {3}: (13, {}), {4}: (14, {}),... | custom-call | bytes 6881280 | tf_op jit(solution)/shard_map/cond/branch_0_fun/pallas_call | solution.py:643
  141.0 3.3 %branch_0_fun.25 = (bf16[2,448,256]{2,1,0:T(8,128)(2,1)S(1)}, bf16[2,448,128]{2,1,0:T(8,128)(2,1)S(1)}, bf16[2,448,128]{2,1,0:T(8,128)(2,1)S(1)}) custom-call(bf16[2,448,2048]{2,1,0:T(8,128)(2,1)S(1)} %get-tuple-element.48.pair, bf16[2,2048,1792]{2,1,0:T(8,128)(2,1)S(1)} %copy-done.2, bf16[2,448,256]{2,1,0:T(8,128)(2,1)S(1)} %get-tuple-element.76.refs_3_.refs_0_.refs_9_), custom_call_target="tpu_custom_call" | custom-call | flops 3758096384 | bytes 7864320 | tf_op jit(solution)/shard_map/cond/branch_0_fun/pallas_call | solution.py:571
  144.3 3.5 %collective-permute-done.4.refs_2_ = bf16[2,448,256]{2,1,0:T(8,128)(2,1)S(1)} collective-permute-done((bf16[2,448,256]{2,1,0:T(8,128)(2,1)S(1)}, bf16[2,448,256]{2,1,0:T(8,128)(2,1)S(1)}, u32[]{:S(2)}, u32[]{:S(2)}) %collective-permute-start.4) | collective-permute-done | bytes 458784 | tf_op jit(solution)/shard_map/cond/branch_0_fun/ppermute | solution.py:45
  147.8 2.7 %branch_0_fun.26 = (bf16[2,448,256]{2,1,0:T(8,128)(2,1)S(1)}, bf16[448,1792]{1,0:T(8,128)(2,1)}, bf16[448,1792]{1,0:T(8,128)(2,1)}, bf16[448,1792]{1,0:T(8,128)(...) custom-call(f32[2,2,448,256]{3,2,1,0:T(8,128)S(1)} %branch_0_fun.22., ...), custom_call_target="tpu_custom_call", output_to_operand_aliasing={{1}: (11, {}), {2}: (12, {}), {3}: (13, {}), {4}: (14, {}),... | custom-call | bytes 6881280 | tf_op jit(solution)/shard_map/cond/branch_0_fun/pallas_call | solution.py:643
  150.8 4.3 %branch_0_fun.24.refs_0_ = f32[3,2,448,256]{3,2,1,0:T(8,128)S(1)} custom-call(bf16[2,448,1536]{2,1,0:T(8,128)(2,1)S(1)} %get-tuple-element.44.pair_in.refs_0_, bf16[2,448,512]{2,1,0:T(8,128)(2,1)S(1)} %get-tuple-element.50.refs_1_, bf16[2,2048,1792]{2,1,0:T(8,128)(2,1)S(1)} %copy-done.2, bf16[2,448,256]{2,1,0:T(8,128)(2,1)S(1)} %get-tuple-element.76.refs_3_.refs_0_.refs_9_), custom_call_target="tpu_custom_call" | custom-call | flops 5637144576 | bytes 9961472 | tf_op jit(solution)/shard_map/cond/branch_0_fun/pallas_call | solution.py:410
  155.2 2.4 %collective-permute-done.8.refs_2_ = bf16[2,448,256]{2,1,0:T(8,128)(2,1)S(1)} collective-permute-done((bf16[2,448,256]{2,1,0:T(8,128)(2,1)S(1)}, bf16[2,448,256]{2,1,0:T(8,128)(2,1)S(1)}, u32[]{:S(2)}, u32[]{:S(2)}) %collective-permute-start.8) | collective-permute-done | bytes 458784 | tf_op jit(solution)/shard_map/cond/branch_0_fun/ppermute | solution.py:45
  157.6 2.7 %branch_0_fun.27 = (bf16[2,448,256]{2,1,0:T(8,128)(2,1)S(1)}, bf16[448,1792]{1,0:T(8,128)(2,1)}, bf16[448,1792]{1,0:T(8,128)(2,1)}, bf16[448,1792]{1,0:T(8,128)(...) custom-call(f32[3,2,448,256]{3,2,1,0:T(8,128)S(1)} %branch_0_fun.24., ...), custom_call_target="tpu_custom_call", output_to_operand_aliasing={{1}: (11, {}), {2}: (12, {}), {3}: (13, {}), {4}: (14, {}),... | custom-call | bytes 6881280 | tf_op jit(solution)/shard_map/cond/branch_0_fun/pallas_call | solution.py:643
  161.5 5.4 %collective-permute-done.6.refs_2_ = bf16[2,448,256]{2,1,0:T(8,128)(2,1)S(1)} collective-permute-done((bf16[2,448,256]{2,1,0:T(8,128)(2,1)S(1)}, bf16[2,448,256]{2,1,0:T(8,128)(2,1)S(1)}, u32[]{:S(2)}, u32[]{:S(2)}) %collective-permute-start.6) | collective-permute-done | bytes 458784 | tf_op jit(solution)/shard_map/cond/branch_0_fun/ppermute | solution.py:45
  166.9 2.7 %branch_0_fun.28 = (bf16[2,448,256]{2,1,0:T(8,128)(2,1)S(1)}, bf16[448,1792]{1,0:T(8,128)(2,1)}, bf16[448,1792]{1,0:T(8,128)(2,1)}, bf16[448,1792]{1,0:T(8,128)(...) custom-call(f32[3,2,448,256]{3,2,1,0:T(8,128)S(1)} %branch_0_fun.24., ...), custom_call_target="tpu_custom_call", output_to_operand_aliasing={{1}: (11, {}), {2}: (12, {}), {3}: (13, {}), {4}: (14, {}),... | custom-call | bytes 6881280 | tf_op jit(solution)/shard_map/cond/branch_0_fun/pallas_call | solution.py:643
  178.7 4.3 %collective-permute-done.15.other = bf16[2,448,256]{2,1,0:T(8,128)(2,1)S(1)} collective-permute-done((bf16[2,448,256]{2,1,0:T(8,128)(2,1)S(1)}, bf16[2,448,256]{2,1,0:T(8,128)(2,1)S(1)}, u32[]{:S(2)}, u32[]{:S(2)}) %collective-permute-start.15) | collective-permute-done | bytes 458784 | tf_op jit(solution)/shard_map/cond/branch_0_fun/ppermute | solution.py:744
  184.0 2.5 %collective-permute-done.14.other = bf16[2,448,128]{2,1,0:T(8,128)(2,1)S(1)} collective-permute-done((bf16[2,448,128]{2,1,0:T(8,128)(2,1)S(1)}, bf16[2,448,128]{2,1,0:T(8,128)(2,1)S(1)}, u32[]{:S(2)}, u32[]{:S(2)}) %collective-permute-start.14) | collective-permute-done | bytes 229408 | tf_op jit(solution)/shard_map/cond/branch_0_fun/ppermute | solution.py:744
  (84 shorter events, 44.5 us)
Async XLA Ops:
  3.6 80.4 %collective-permute-start.32 = (bf16[2,448,1792]{2,1,0:T(8,128)(2,1)}, bf16[2,448,1792]{2,1,0:T(8,128)(2,1)S(1)}, u32[]{:S(2)}, u32[]{:S(2)}) collective-permute-start(bf16[2,448,1792]{2,1,0:T(8,128)(2,1)} %shard_map.136), channel_id=1, source_target_pairs={{0,1},{1,0},{2,3},{3,2},{4,5},{5,4},{6,7},{7,6},{8,9},{9,8},{10,11... | collective-permute-start | bytes 9633800 | tf_op jit(solution)/shard_map/ppermute | solution.py:45
  6.5 14.3 %collective-permute-start.39 = (bf16[2,64,1792]{2,1,0:T(8,128)(2,1)S(1)}, bf16[2,64,1792]{2,1,0:T(8,128)(2,1)S(1)}, u32[]{:S(2)}, u32[]{:S(2)}) collective-permute-start(bf16[2,64,1792]{2,1,0:T(8,128)(2,1)S(1)} %get-tuple-element.249.refs_0_), channel_id=1, source_target_pairs={{0,8},{1,9},{2,10},{3,11},{4,12},{5,13},{6,14},{7,15},{8,16},{9,17... | collective-permute-start | bytes 1376264 | tf_op jit(solution)/shard_map/ppermute | solution.py:45
  8.4 12.5 %collective-permute-start.40 = (bf16[2,64,1792]{2,1,0:T(8,128)(2,1)S(1)}, bf16[2,64,1792]{2,1,0:T(8,128)(2,1)S(1)}, u32[]{:S(2)}, u32[]{:S(2)}) collective-permute-start(bf16[2,64,1792]{2,1,0:T(8,128)(2,1)S(1)} %get-tuple-element.249.refs_0_), channel_id=1, source_target_pairs={{0,24},{1,25},{2,26},{3,27},{4,28},{5,29},{6,30},{7,31},{8,0},{9,1... | collective-permute-start | bytes 1376264 | tf_op jit(solution)/shard_map/ppermute | solution.py:45
  10.6 13.6 %collective-permute-start.33 = (bf16[2,64,1792]{2,1,0:T(8,128)(2,1)S(1)}, bf16[2,64,1792]{2,1,0:T(8,128)(2,1)S(1)}, u32[]{:S(2)}, u32[]{:S(2)}) collective-permute-start(bf16[2,64,1792]{2,1,0:T(8,128)(2,1)S(1)} %get-tuple-element.248.refs_0_), channel_id=1, source_target_pairs={{0,4},{1,5},{2,6},{3,7},{4,0},{5,1},{6,2},{7,3},{8,12},{9,13},{10,... | collective-permute-start | bytes 1376264 | tf_op jit(solution)/shard_map/ppermute | solution.py:45
  13.7 12.8 %collective-permute-start.34 = (bf16[2,64,1792]{2,1,0:T(8,128)(2,1)S(1)}, bf16[2,64,1792]{2,1,0:T(8,128)(2,1)S(1)}, u32[]{:S(2)}, u32[]{:S(2)}) collective-permute-start(bf16[2,64,1792]{2,1,0:T(8,128)(2,1)S(1)} %get-tuple-element.248.refs_0_), channel_id=1, source_target_pairs={{0,3},{1,2},{2,1},{3,0},{4,7},{5,6},{6,5},{7,4},{8,11},{9,10},{10,... | collective-permute-start | bytes 1376264 | tf_op jit(solution)/shard_map/ppermute | solution.py:45
  20.8 8.8 %collective-permute-start.41 = (bf16[2,32,1792]{2,1,0:T(8,128)(2,1)S(1)}, bf16[2,32,1792]{2,1,0:T(8,128)(2,1)S(1)}, u32[]{:S(2)}, u32[]{:S(2)}) collective-permute-start(bf16[2,32,1792]{2,1,0:T(8,128)(2,1)S(1)} %slice.18), channel_id=1, source_target_pairs={{0,8},{1,9},{2,10},{3,11},{4,12},{5,13},{6,14},{7,15},{8,16},{9,17... | collective-permute-start | bytes 688136 | tf_op jit(solution)/shard_map/ppermute | solution.py:45
  20.9 8.7 %collective-permute-start.42 = (bf16[2,32,1792]{2,1,0:T(8,128)(2,1)S(1)}, bf16[2,32,1792]{2,1,0:T(8,128)(2,1)S(1)}, u32[]{:S(2)}, u32[]{:S(2)}) collective-permute-start(bf16[2,32,1792]{2,1,0:T(8,128)(2,1)S(1)} %slice.19), channel_id=1, source_target_pairs={{0,24},{1,25},{2,26},{3,27},{4,28},{5,29},{6,30},{7,31},{8,0},{9,1... | collective-permute-start | bytes 688136 | tf_op jit(solution)/shard_map/ppermute | solution.py:45
  24.2 11.0 %collective-permute-start.35 = (bf16[2,32,1792]{2,1,0:T(8,128)(2,1)S(1)}, bf16[2,32,1792]{2,1,0:T(8,128)(2,1)S(1)}, u32[]{:S(2)}, u32[]{:S(2)}) collective-permute-start(bf16[2,32,1792]{2,1,0:T(8,128)(2,1)S(1)} %slice.16), channel_id=1, source_target_pairs={{0,3},{1,2},{2,1},{3,0},{4,7},{5,6},{6,5},{7,4},{8,11},{9,10},{10,... | collective-permute-start | bytes 688136 | tf_op jit(solution)/shard_map/ppermute | solution.py:45
  26.5 8.7 %collective-permute-start.36 = (bf16[2,32,1792]{2,1,0:T(8,128)(2,1)S(1)}, bf16[2,32,1792]{2,1,0:T(8,128)(2,1)S(1)}, u32[]{:S(2)}, u32[]{:S(2)}) collective-permute-start(bf16[2,32,1792]{2,1,0:T(8,128)(2,1)S(1)} %slice.17), channel_id=1, source_target_pairs={{0,4},{1,5},{2,6},{3,7},{4,0},{5,1},{6,2},{7,3},{8,12},{9,13},{10,... | collective-permute-start | bytes 688136 | tf_op jit(solution)/shard_map/ppermute | solution.py:45
  31.1 42.5 %collective-permute-start.45 = (bf16[2,256,1792]{2,1,0:T(8,128)(2,1)}, bf16[2,256,1792]{2,1,0:T(8,128)(2,1)}, u32[]{:S(2)}, u32[]{:S(2)}) collective-permute-start(bf16[2,256,1792]{2,1,0:T(8,128)(2,1)} %shard_map.139.refs_3_.refs_8_), channel_id=1, source_target_pairs={{0,4},{1,5},{2,6},{3,7},{4,0},{5,1},{6,2},{7,3},{8,12},{9,13},{10,... | collective-permute-start | bytes 5505032 | tf_op jit(solution)/shard_map/ppermute | solution.py:45
  33.0 41.2 %collective-permute-start.46 = (bf16[2,256,1792]{2,1,0:T(8,128)(2,1)}, bf16[2,256,1792]{2,1,0:T(8,128)(2,1)}, u32[]{:S(2)}, u32[]{:S(2)}) collective-permute-start(bf16[2,256,1792]{2,1,0:T(8,128)(2,1)} %shard_map.139.refs_3_.refs_8_), channel_id=1, source_target_pairs={{0,3},{1,2},{2,1},{3,0},{4,7},{5,6},{6,5},{7,4},{8,11},{9,10},{10,... | collective-permute-start | bytes 5505032 | tf_op jit(solution)/shard_map/ppermute | solution.py:45
  36.6 41.4 %collective-permute-start.37 = (bf16[2,256,1792]{2,1,0:T(8,128)(2,1)}, bf16[2,256,1792]{2,1,0:T(8,128)(2,1)}, u32[]{:S(2)}, u32[]{:S(2)}) collective-permute-start(bf16[2,256,1792]{2,1,0:T(8,128)(2,1)} %shard_map.138.refs_2_.refs_7_), channel_id=1, source_target_pairs={{0,8},{1,9},{2,10},{3,11},{4,12},{5,13},{6,14},{7,15},{8,16},{9,17... | collective-permute-start | bytes 5505032 | tf_op jit(solution)/shard_map/ppermute | solution.py:45
  36.7 41.3 %collective-permute-start.38 = (bf16[2,256,1792]{2,1,0:T(8,128)(2,1)}, bf16[2,256,1792]{2,1,0:T(8,128)(2,1)}, u32[]{:S(2)}, u32[]{:S(2)}) collective-permute-start(bf16[2,256,1792]{2,1,0:T(8,128)(2,1)} %shard_map.138.refs_2_.refs_7_), channel_id=1, source_target_pairs={{0,24},{1,25},{2,26},{3,27},{4,28},{5,29},{6,30},{7,31},{8,0},{9,1... | collective-permute-start | bytes 5505032 | tf_op jit(solution)/shard_map/ppermute | solution.py:45
  75.8 24.2 %collective-permute-start.47 = (bf16[2,128,1792]{2,1,0:T(8,128)(2,1)S(1)}, bf16[2,128,1792]{2,1,0:T(8,128)(2,1)S(1)}, u32[]{:S(2)}, u32[]{:S(2)}) collective-permute-start(bf16[2,128,1792]{2,1,0:T(8,128)(2,1)S(1)} %get-tuple-element.253.refs_13_), channel_id=1, source_target_pairs={{0,3},{1,2},{2,1},{3,0},{4,7},{5,6},{6,5},{7,4},{8,11},{9,10},{10,... | collective-permute-start | bytes 2752520 | tf_op jit(solution)/shard_map/ppermute | solution.py:45
  79.5 20.9 %collective-permute-start.43 = (bf16[2,128,1792]{2,1,0:T(8,128)(2,1)S(1)}, bf16[2,128,1792]{2,1,0:T(8,128)(2,1)S(1)}, u32[]{:S(2)}, u32[]{:S(2)}) collective-permute-start(bf16[2,128,1792]{2,1,0:T(8,128)(2,1)S(1)} %get-tuple-element.251.refs_12_), channel_id=1, source_target_pairs={{0,8},{1,9},{2,10},{3,11},{4,12},{5,13},{6,14},{7,15},{8,16},{9,17... | collective-permute-start | bytes 2752520 | tf_op jit(solution)/shard_map/ppermute | solution.py:45
  80.0 20.8 %collective-permute-start.48 = (bf16[2,128,1792]{2,1,0:T(8,128)(2,1)S(1)}, bf16[2,128,1792]{2,1,0:T(8,128)(2,1)S(1)}, u32[]{:S(2)}, u32[]{:S(2)}) collective-permute-start(bf16[2,128,1792]{2,1,0:T(8,128)(2,1)S(1)} %get-tuple-element.254), channel_id=1, source_target_pairs={{0,4},{1,5},{2,6},{3,7},{4,0},{5,1},{6,2},{7,3},{8,12},{9,13},{10,... | collective-permute-start | bytes 2752520 | tf_op jit(solution)/shard_map/ppermute | solution.py:45
  80.9 20.0 %collective-permute-start.44 = (bf16[2,128,1792]{2,1,0:T(8,128)(2,1)S(1)}, bf16[2,128,1792]{2,1,0:T(8,128)(2,1)S(1)}, u32[]{:S(2)}, u32[]{:S(2)}) collective-permute-start(bf16[2,128,1792]{2,1,0:T(8,128)(2,1)S(1)} %get-tuple-element.252), channel_id=1, source_target_pairs={{0,24},{1,25},{2,26},{3,27},{4,28},{5,29},{6,30},{7,31},{8,0},{9,1... | collective-permute-start | bytes 2752520 | tf_op jit(solution)/shard_map/ppermute | solution.py:45
  105.3 13.6 %collective-permute-start.1 = (bf16[2,448,256]{2,1,0:T(8,128)(2,1)S(1)}, bf16[2,448,256]{2,1,0:T(8,128)(2,1)S(1)}, u32[]{:S(2)}, u32[]{:S(2)}) collective-permute-start(bf16[2,448,256]{2,1,0:T(8,128)(2,1)S(1)} %get-tuple-element.57), channel_id=1, source_target_pairs={{0,1},{1,0},{2,3},{3,2},{4,5},{5,4},{6,7},{7,6},{8,9},{9,8},{10,11... | collective-permute-start | bytes 1376264 | tf_op jit(solution)/shard_map/cond/branch_0_fun/ppermute | solution.py:45
  110.7 17.4 %collective-permute-start = (bf16[2,448,256]{2,1,0:T(8,128)(2,1)S(1)}, bf16[2,448,256]{2,1,0:T(8,128)(2,1)S(1)}, u32[]{:S(2)}, u32[]{:S(2)}) collective-permute-start(bf16[2,448,256]{2,1,0:T(8,128)(2,1)S(1)} %get-tuple-element.49.refs_0_), channel_id=1, source_target_pairs={{0,1},{1,0},{2,3},{3,2},{4,5},{5,4},{6,7},{7,6},{8,9},{9,8},{10,11... | collective-permute-start | bytes 1376264 | tf_op jit(solution)/shard_map/cond/branch_0_fun/ppermute | solution.py:45
  121.5 12.9 %collective-permute-start.3 = (bf16[2,448,256]{2,1,0:T(8,128)(2,1)S(1)}, bf16[2,448,256]{2,1,0:T(8,128)(2,1)S(1)}, u32[]{:S(2)}, u32[]{:S(2)}) collective-permute-start(bf16[2,448,256]{2,1,0:T(8,128)(2,1)S(1)} %get-tuple-element.65.refs_0_.refs_9_), channel_id=1, source_target_pairs={{0,64},{32,96},{64,0},{96,32},{1,65},{33,97},{65,1},{97,33},{2,66}... | collective-permute-start | bytes 1376264 | tf_op jit(solution)/shard_map/cond/branch_0_fun/ppermute | solution.py:744
  122.1 15.9 %collective-permute-start.2 = (bf16[2,448,256]{2,1,0:T(8,128)(2,1)S(1)}, bf16[2,448,256]{2,1,0:T(8,128)(2,1)S(1)}, u32[]{:S(2)}, u32[]{:S(2)}) collective-permute-start(bf16[2,448,256]{2,1,0:T(8,128)(2,1)S(1)} %get-tuple-element.68), channel_id=1, source_target_pairs={{0,1},{1,0},{2,3},{3,2},{4,5},{5,4},{6,7},{7,6},{8,9},{9,8},{10,11... | collective-permute-start | bytes 1376264 | tf_op jit(solution)/shard_map/cond/branch_0_fun/ppermute | solution.py:45
  130.5 17.2 %collective-permute-start.4 = (bf16[2,448,256]{2,1,0:T(8,128)(2,1)S(1)}, bf16[2,448,256]{2,1,0:T(8,128)(2,1)S(1)}, u32[]{:S(2)}, u32[]{:S(2)}) collective-permute-start(bf16[2,448,256]{2,1,0:T(8,128)(2,1)S(1)} %get-tuple-element.77), channel_id=1, source_target_pairs={{0,1},{1,0},{2,3},{3,2},{4,5},{5,4},{6,7},{7,6},{8,9},{9,8},{10,11... | collective-permute-start | bytes 1376264 | tf_op jit(solution)/shard_map/cond/branch_0_fun/ppermute | solution.py:45
  130.5 17.2 %collective-permute-start.5 = (bf16[2,448,256]{2,1,0:T(8,128)(2,1)S(1)}, bf16[2,448,256]{2,1,0:T(8,128)(2,1)S(1)}, u32[]{:S(2)}, u32[]{:S(2)}) collective-permute-start(bf16[2,448,256]{2,1,0:T(8,128)(2,1)S(1)} %get-tuple-element.67.refs_3_.refs_9_), channel_id=1, source_target_pairs={{0,64},{32,96},{64,0},{96,32},{1,65},{33,97},{65,1},{97,33},{2,66}... | collective-permute-start | bytes 1376264 | tf_op jit(solution)/shard_map/cond/branch_0_fun/ppermute | solution.py:744
  140.6 17.0 %collective-permute-start.8 = (bf16[2,448,256]{2,1,0:T(8,128)(2,1)S(1)}, bf16[2,448,256]{2,1,0:T(8,128)(2,1)S(1)}, u32[]{:S(2)}, u32[]{:S(2)}) collective-permute-start(bf16[2,448,256]{2,1,0:T(8,128)(2,1)S(1)} %get-tuple-element.87), channel_id=1, source_target_pairs={{0,1},{1,0},{2,3},{3,2},{4,5},{5,4},{6,7},{7,6},{8,9},{9,8},{10,11... | collective-permute-start | bytes 1376264 | tf_op jit(solution)/shard_map/cond/branch_0_fun/ppermute | solution.py:45
  140.6 17.0 %collective-permute-start.9 = (bf16[2,448,256]{2,1,0:T(8,128)(2,1)S(1)}, bf16[2,448,256]{2,1,0:T(8,128)(2,1)S(1)}, u32[]{:S(2)}, u32[]{:S(2)}) collective-permute-start(bf16[2,448,256]{2,1,0:T(8,128)(2,1)S(1)} %get-tuple-element.76.refs_3_.refs_0_.refs_9_), channel_id=1, source_target_pairs={{0,64},{32,96},{64,0},{96,32},{1,65},{33,97},{65,1},{97,33},{2,66}... | collective-permute-start | bytes 1376264 | tf_op jit(solution)/shard_map/cond/branch_0_fun/ppermute | solution.py:744
  150.4 16.5 %collective-permute-start.6 = (bf16[2,448,256]{2,1,0:T(8,128)(2,1)S(1)}, bf16[2,448,256]{2,1,0:T(8,128)(2,1)S(1)}, u32[]{:S(2)}, u32[]{:S(2)}) collective-permute-start(bf16[2,448,256]{2,1,0:T(8,128)(2,1)S(1)} %get-tuple-element.85), channel_id=1, source_target_pairs={{0,1},{1,0},{2,3},{3,2},{4,5},{5,4},{6,7},{7,6},{8,9},{9,8},{10,11... | collective-permute-start | bytes 1376264 | tf_op jit(solution)/shard_map/cond/branch_0_fun/ppermute | solution.py:45
  150.4 16.5 %collective-permute-start.7 = (bf16[2,448,256]{2,1,0:T(8,128)(2,1)S(1)}, bf16[2,448,256]{2,1,0:T(8,128)(2,1)S(1)}, u32[]{:S(2)}, u32[]{:S(2)}) collective-permute-start(bf16[2,448,256]{2,1,0:T(8,128)(2,1)S(1)} %get-tuple-element.86.refs_9_), channel_id=1, source_target_pairs={{0,64},{32,96},{64,0},{96,32},{1,65},{33,97},{65,1},{97,33},{2,66}... | collective-permute-start | bytes 1376264 | tf_op jit(solution)/shard_map/cond/branch_0_fun/ppermute | solution.py:744
  160.3 12.5 %collective-permute-start.12 = (bf16[2,448,256]{2,1,0:T(8,128)(2,1)S(1)}, bf16[2,448,256]{2,1,0:T(8,128)(2,1)S(1)}, u32[]{:S(2)}, u32[]{:S(2)}) collective-permute-start(bf16[2,448,256]{2,1,0:T(8,128)(2,1)S(1)} %get-tuple-element.104.refs_9_), channel_id=1, source_target_pairs={{0,64},{32,96},{64,0},{96,32},{1,65},{33,97},{65,1},{97,33},{2,66}... | collective-permute-start | bytes 1376264 | tf_op jit(solution)/shard_map/cond/branch_0_fun/ppermute | solution.py:744
  160.3 10.4 %collective-permute-start.11 = (bf16[2,448,128]{2,1,0:T(8,128)(2,1)S(1)}, bf16[2,448,128]{2,1,0:T(8,128)(2,1)S(1)}, u32[]{:S(2)}, u32[]{:S(2)}) collective-permute-start(bf16[2,448,128]{2,1,0:T(8,128)(2,1)S(1)} %get-tuple-element.103), channel_id=1, source_target_pairs={{0,1},{1,0},{2,3},{3,2},{4,5},{5,4},{6,7},{7,6},{8,9},{9,8},{10,11... | collective-permute-start | bytes 688136 | tf_op jit(solution)/shard_map/cond/branch_0_fun/ppermute | solution.py:45
  169.6 13.5 %collective-permute-start.15 = (bf16[2,448,256]{2,1,0:T(8,128)(2,1)S(1)}, bf16[2,448,256]{2,1,0:T(8,128)(2,1)S(1)}, u32[]{:S(2)}, u32[]{:S(2)}) collective-permute-start(bf16[2,448,256]{2,1,0:T(8,128)(2,1)S(1)} %get-tuple-element.119.own), channel_id=1, source_target_pairs={{0,64},{32,96},{64,0},{96,32},{1,65},{33,97},{65,1},{97,33},{2,66}... | collective-permute-start | bytes 1376264 | tf_op jit(solution)/shard_map/cond/branch_0_fun/ppermute | solution.py:744
  174.8 11.7 %collective-permute-start.14 = (bf16[2,448,128]{2,1,0:T(8,128)(2,1)S(1)}, bf16[2,448,128]{2,1,0:T(8,128)(2,1)S(1)}, u32[]{:S(2)}, u32[]{:S(2)}) collective-permute-start(bf16[2,448,128]{2,1,0:T(8,128)(2,1)S(1)} %get-tuple-element.118.own), channel_id=1, source_target_pairs={{0,64},{32,96},{64,0},{96,32},{1,65},{33,97},{65,1},{97,33},{2,66}... | collective-permute-start | bytes 688136 | tf_op jit(solution)/shard_map/cond/branch_0_fun/ppermute | solution.py:744
  177.6 11.4 %collective-permute-start.13 = (bf16[2,448,128]{2,1,0:T(8,128)(2,1)S(1)}, bf16[2,448,128]{2,1,0:T(8,128)(2,1)S(1)}, u32[]{:S(2)}, u32[]{:S(2)}) collective-permute-start(bf16[2,448,128]{2,1,0:T(8,128)(2,1)S(1)} %get-tuple-element.117.own), channel_id=1, source_target_pairs={{0,64},{32,96},{64,0},{96,32},{1,65},{33,97},{65,1},{97,33},{2,66}... | collective-permute-start | bytes 688136 | tf_op jit(solution)/shard_map/cond/branch_0_fun/ppermute | solution.py:744
  (10 other events, 56.4 us)

commit v5 on v4

--- a/solution.py
+++ b/solution.py
@@ -704,8 +704,8 @@
     last = [
         moved(halves[0], z_up),
         moved(halves[1], z_down),
+        moved(halves[3], x_other),
         moved(halves[2], y_same_half),
-        moved(halves[3], x_other),
     ]
     results = hidden_step(
         ((0, 0, 1024, 512), (1, 0, 1024, 512), (1, 1024, 512, 0)),

time: 186 us -> 183 us (0.984); the launches traced: 190 us -> 182 us
  waiting for transfers between devices: 60 us -> 51.8 us
    ppermute x8, waiting for transfers between devices: 10.5 us -> 3.68 us  [finish(): others.append(lax.ppermute(out[0], 'rep', route))]
    ppermute x25, starting transfers between devices: 39 us -> 43.8 us  [moved(): return lax.ppermute(block, 'fsdp', route)]
    ppermute x8, starting transfers between devices: 4.37 us -> 0.17 us  [finish(): others.append(lax.ppermute(out[0], 'rep', route))]
  transfers between devices with their start and end apart: 33 -> 33, of which waited for: 17 -> 16; matrix products, arithmetic and copies ran while one was open for 0% -> 0% of each run, Pallas kernels for 40% -> 42%
where the time goes in v5:
time: 183 us; the launch traced here: 182 us
  Pallas kernels  84.4 us (46%)
  waiting for transfers between devices  51.8 us (28%)
  starting transfers between devices  43.9 us (24%)
    ppermute x25, waiting for transfers between devices, moved(): return lax.ppermute(block, 'fsdp', route)  48.1 us
    ppermute x25, starting transfers between devices, moved(): return lax.ppermute(block, 'fsdp', route)  43.8 us
    pallas_call x2, Pallas kernels, hidden_step(): pl.pallas_call(functools.partial(hidden_kernel, jobs, sizes, pieces, skip...  22.9 us
    pallas_call x8, Pallas kernels, adam_chunk(): pl.pallas_call(functools.partial(adam_kernel, (bool(mixed), len(passing))...  19.7 us
    pallas_call x3, Pallas kernels, theirs_chunks(): pl.pallas_call(functools.partial(theirs_kernel, targets, len(after)), out...  11.6 us
    pallas_call x2, Pallas kernels, own_rest(): pl.pallas_call(kernel, out_shape=jax.ShapeDtypeStruct((count, 2, HELD, WI...  7.21 us
    pallas_call x1, Pallas kernels, own_first(): pl.pallas_call(own_first_kernel, out_shape=[jax.ShapeDtypeStruct((FIRST_O...  6.24 us
    pallas_call x1, Pallas kernels, last_shared(): pl.pallas_call(last_shared_kernel, out_shape=[jax.ShapeDtypeStruct((2, HE...  4.33 us
  transfers between devices with their start and end apart: 33, of which 16 were waited for; matrix products, arithmetic and copies ran while one was open for 0% of the time, Pallas kernels for 42%

profile of v5, /device:TPU:0, one launch (start us, length us, event | category | flops | bytes accessed | tf_op | source)
XLA Modules:
  0.0 182.3 jit_solution(18092788751083869494)
XLA Ops:
  0.7 3.0 %shard_map.136 = bf16[2,448,1792]{2,1,0:T(8,128)(2,1)} custom-call(bf16[448,1792]{1,0:T(8,128)(2,1)} %bitcast.23, bf16[448,1792]{1,0:T(8,128)(2,1)} %bitcast.28), custom_call_target="tpu_custom_call" | custom-call | bytes 6422528 | tf_op jit(solution)/shard_map/pallas_call | solution.py:156
  8.4 2.2 %collective-permute-start.40 = (bf16[2,64,1792]{2,1,0:T(8,128)(2,1)S(1)}, bf16[2,64,1792]{2,1,0:T(8,128)(2,1)S(1)}, u32[]{:S(2)}, u32[]{:S(2)}) collective-permute-start(bf16[2,64,1792]{2,1,0:T(8,128)(2,1)S(1)} %get-tuple-element.249.refs_0_), channel_id=1, source_target_pairs={{0,24},{1,25},{2,26},{3,27},{4,28},{5,29},{6,30},{7,31},{8,0},{9,1... | collective-permute-start | bytes 1376264 | tf_op jit(solution)/shard_map/ppermute | solution.py:45
  10.6 3.0 %collective-permute-start.33 = (bf16[2,64,1792]{2,1,0:T(8,128)(2,1)S(1)}, bf16[2,64,1792]{2,1,0:T(8,128)(2,1)S(1)}, u32[]{:S(2)}, u32[]{:S(2)}) collective-permute-start(bf16[2,64,1792]{2,1,0:T(8,128)(2,1)S(1)} %get-tuple-element.248.refs_0_), channel_id=1, source_target_pairs={{0,4},{1,5},{2,6},{3,7},{4,0},{5,1},{6,2},{7,3},{8,12},{9,13},{10,... | collective-permute-start | bytes 1376264 | tf_op jit(solution)/shard_map/ppermute | solution.py:45
  13.7 2.2 %collective-permute-start.34 = (bf16[2,64,1792]{2,1,0:T(8,128)(2,1)S(1)}, bf16[2,64,1792]{2,1,0:T(8,128)(2,1)S(1)}, u32[]{:S(2)}, u32[]{:S(2)}) collective-permute-start(bf16[2,64,1792]{2,1,0:T(8,128)(2,1)S(1)} %get-tuple-element.248.refs_0_), channel_id=1, source_target_pairs={{0,3},{1,2},{2,1},{3,0},{4,7},{5,6},{6,5},{7,4},{8,11},{9,10},{10,... | collective-permute-start | bytes 1376264 | tf_op jit(solution)/shard_map/ppermute | solution.py:45
  15.9 5.0 %collective-permute-done.39.refs_1_ = bf16[2,64,1792]{2,1,0:T(8,128)(2,1)S(1)} collective-permute-done((bf16[2,64,1792]{2,1,0:T(8,128)(2,1)S(1)}, bf16[2,64,1792]{2,1,0:T(8,128)(2,1)S(1)}, u32[]{:S(2)}, u32[]{:S(2)}) %collective-permute-start.39) | collective-permute-done | bytes 458784 | tf_op jit(solution)/shard_map/ppermute | solution.py:45
  20.9 3.3 %collective-permute-start.42 = (bf16[2,32,1792]{2,1,0:T(8,128)(2,1)S(1)}, bf16[2,32,1792]{2,1,0:T(8,128)(2,1)S(1)}, u32[]{:S(2)}, u32[]{:S(2)}) collective-permute-start(bf16[2,32,1792]{2,1,0:T(8,128)(2,1)S(1)} %slice.19), channel_id=1, source_target_pairs={{0,24},{1,25},{2,26},{3,27},{4,28},{5,29},{6,30},{7,31},{8,0},{9,1... | collective-permute-start | bytes 688136 | tf_op jit(solution)/shard_map/ppermute | solution.py:45
  24.2 2.3 %collective-permute-start.35 = (bf16[2,32,1792]{2,1,0:T(8,128)(2,1)S(1)}, bf16[2,32,1792]{2,1,0:T(8,128)(2,1)S(1)}, u32[]{:S(2)}, u32[]{:S(2)}) collective-permute-start(bf16[2,32,1792]{2,1,0:T(8,128)(2,1)S(1)} %slice.16), channel_id=1, source_target_pairs={{0,3},{1,2},{2,1},{3,0},{4,7},{5,6},{6,5},{7,4},{8,11},{9,10},{10,... | collective-permute-start | bytes 688136 | tf_op jit(solution)/shard_map/ppermute | solution.py:45
  26.5 3.1 %collective-permute-start.36 = (bf16[2,32,1792]{2,1,0:T(8,128)(2,1)S(1)}, bf16[2,32,1792]{2,1,0:T(8,128)(2,1)S(1)}, u32[]{:S(2)}, u32[]{:S(2)}) collective-permute-start(bf16[2,32,1792]{2,1,0:T(8,128)(2,1)S(1)} %slice.17), channel_id=1, source_target_pairs={{0,4},{1,5},{2,6},{3,7},{4,0},{5,1},{6,2},{7,3},{8,12},{9,13},{10,... | collective-permute-start | bytes 688136 | tf_op jit(solution)/shard_map/ppermute | solution.py:45
  36.7 3.1 %collective-permute-start.38 = (bf16[2,256,1792]{2,1,0:T(8,128)(2,1)}, bf16[2,256,1792]{2,1,0:T(8,128)(2,1)}, u32[]{:S(2)}, u32[]{:S(2)}) collective-permute-start(bf16[2,256,1792]{2,1,0:T(8,128)(2,1)} %shard_map.138.refs_2_.refs_7_), channel_id=1, source_target_pairs={{0,24},{1,25},{2,26},{3,27},{4,28},{5,29},{6,30},{7,31},{8,0},{9,1... | collective-permute-start | bytes 5505032 | tf_op jit(solution)/shard_map/ppermute | solution.py:45
  40.7 7.0 %shard_map.140 = (bf16[2,448,1536]{2,1,0:T(8,128)(2,1)S(1)}, bf16[2,448,2048]{2,1,0:T(8,128)(2,1)S(1)}, bf16[2,2048,1792]{2,1,0:T(8,128)(2,1)}) custom-call(bf16[448,1792]{1,0:T(8,128)(2,1)} %bitcast.24, bf16[448,1792]{1,0:T(8,128)(2,1)} %bitcast.29, bf16[2,256,1792]{2,1,0:T(8,128)(2,1)} %shard_map.138.refs_2_.refs_7_, ...), custom_call_target="tpu_custom_call" | custom-call | flops 3288334336 | bytes 7798784 | tf_op jit(solution)/shard_map/pallas_call | solution.py:303
  47.8 25.8 %collective-permute-done.45.refs_0_.refs_5_ = bf16[2,256,1792]{2,1,0:T(8,128)(2,1)} collective-permute-done((bf16[2,256,1792]{2,1,0:T(8,128)(2,1)}, bf16[2,256,1792]{2,1,0:T(8,128)(2,1)}, u32[]{:S(2)}, u32[]{:S(2)}) %collective-permute-start.45) | collective-permute-done | bytes 1835040 | tf_op jit(solution)/shard_map/ppermute | solution.py:45
  75.8 2.3 %collective-permute-start.48 = (bf16[2,128,1792]{2,1,0:T(8,128)(2,1)S(1)}, bf16[2,128,1792]{2,1,0:T(8,128)(2,1)S(1)}, u32[]{:S(2)}, u32[]{:S(2)}) collective-permute-start(bf16[2,128,1792]{2,1,0:T(8,128)(2,1)S(1)} %get-tuple-element.254.refs_13_), channel_id=1, source_target_pairs={{0,3},{1,2},{2,1},{3,0},{4,7},{5,6},{6,5},{7,4},{8,11},{9,10},{10,... | collective-permute-start | bytes 2752520 | tf_op jit(solution)/shard_map/ppermute | solution.py:45
  80.9 3.1 %collective-permute-start.44 = (bf16[2,128,1792]{2,1,0:T(8,128)(2,1)S(1)}, bf16[2,128,1792]{2,1,0:T(8,128)(2,1)S(1)}, u32[]{:S(2)}, u32[]{:S(2)}) collective-permute-start(bf16[2,128,1792]{2,1,0:T(8,128)(2,1)S(1)} %get-tuple-element.252), channel_id=1, source_target_pairs={{0,24},{1,25},{2,26},{3,27},{4,28},{5,29},{6,30},{7,31},{8,0},{9,1... | collective-permute-start | bytes 2752520 | tf_op jit(solution)/shard_map/ppermute | solution.py:45
  84.0 15.9 %shard_map.143 = (bf16[2,448,1536]{2,1,0:T(8,128)(2,1)S(1)}, bf16[2,448,2048]{2,1,0:T(8,128)(2,1)S(1)}, bf16[2,2048,1792]{2,1,0:T(8,128)(2,1)}, f32[2,448,256]{2,1,0:T(8,128)S(1)}) custom-call(bf16[448,1792]{1,0:T(8,128)(2,1)S(1)} %bitcast.25, bf16[448,1792]{1,0:T(8,128)(2,1)S(1)} %bitcast.30, ...), custom_call_target="tpu_custom_call", output_to_operand_aliasing={{0}: (9, {}), {1}: (10, {}), {2}: (11, {})} | custom-call | flops 16441671680 | bytes 22937600 | tf_op jit(solution)/shard_map/pallas_call | solution.py:303
  100.9 4.3 %shard_map.144 = (bf16[2,448,2048]{2,1,0:T(8,128)(2,1)S(1)}, bf16[2,2048,1792]{2,1,0:T(8,128)(2,1)}, bf16[2,448,256]{2,1,0:T(8,128)(2,1)S(1)}) custom-call(bf16[2,448,1792]{2,1,0:T(8,128)(2,1)S(1)} %collective-permute-done.32.refs_2_.refs_0_, ...), custom_call_target="tpu_custom_call", output_to_operand_aliasing={{0}: (5, {}), {1}: (6, {})} | custom-call | flops 5167382528 | bytes 6881280 | tf_op jit(solution)/shard_map/pallas_call | solution.py:489
  105.3 77.0 %conditional.1 = (bf16[448,1792]{1,0:T(8,128)(2,1)}, bf16[448,1792]{1,0:T(8,128)(2,1)}, bf16[448,1792]{1,0:T(8,128)(2,1)}, bf16[448,1792]{1,0:T(8,128)(2,1)}, bf...) conditional(s32[]{:T(128)} %convert_element_type.6, (bf16[2,448,2048]{2,1,0:T(8,128)(2,1)S(1)}, ...), branch_computations={%region_0.1_spmd, %region_1.2_spmd} | conditional | flops 27715960832 | bytes 191890064 | solution.py:759
  105.8 4.9 %branch_1_fun.17 = (bf16[2,448,256]{2,1,0:T(8,128)(2,1)S(1)}, bf16[2,448,256]{2,1,0:T(8,128)(2,1)S(1)}) custom-call(bf16[2,448,2048]{2,1,0:T(8,128)(2,1)S(1)} %get-tuple-element.136.pair, bf16[2,2048,1792]{2,1,0:T(8,128)(2,1)} %get-tuple-element.135.tokens.tokens_in.refs_2_), custom_call_target="tpu_custom_call" | custom-call | flops 3758096384 | bytes 7864320 | tf_op jit(solution)/shard_map/cond/branch_1_fun/pallas_call | solution.py:571
  112.6 6.2 %branch_1_fun.18 = (f32[2,2,448,256]{3,2,1,0:T(8,128)S(1)}, bf16[2,448,512]{2,1,0:T(8,128)(2,1)S(1)}) custom-call(bf16[448,1792]{1,0:T(8,128)(2,1)S(1)} %get-tuple-element.133.up.refs_3_, bf16[448,1792]{1,0:T(8,128)(2,1)S(1)} %get-tuple-element.134.down.refs_6_, bf16[2,2048,1792]{2,1,0:T(8,128)(2,1)S(1)} %copy-done.3, ...), custom_call_target="tpu_custom_call" | custom-call | flops 7046430720 | bytes 6881280 | tf_op jit(solution)/shard_map/cond/branch_1_fun/pallas_call | solution.py:374
  119.0 2.6 %branch_1_fun.19 = (bf16[2,448,256]{2,1,0:T(8,128)(2,1)S(1)}, bf16[448,1792]{1,0:T(8,128)(2,1)}, bf16[448,1792]{1,0:T(8,128)(2,1)}, bf16[448,1792]{1,0:T(8,128)(...) custom-call(f32[2,2,448,256]{3,2,1,0:T(8,128)S(1)} %get-tuple-elemen, ...), custom_call_target="tpu_custom_call", output_to_operand_aliasing={{7}: (9, {})} | custom-call | bytes 6881280 | tf_op jit(solution)/shard_map/cond/branch_1_fun/pallas_call | solution.py:643
  122.9 3.5 %branch_1_fun.20 = (bf16[2,448,256]{2,1,0:T(8,128)(2,1)S(1)}, bf16[2,448,256]{2,1,0:T(8,128)(2,1)S(1)}) custom-call(bf16[2,448,2048]{2,1,0:T(8,128)(2,1)S(1)} %get-tuple-element.136.pair, bf16[2,2048,1792]{2,1,0:T(8,128)(2,1)S(1)} %copy-done.3, bf16[2,448,256]{2,1,0:T(8,128)(2,1)S(1)} %get-tuple-element.153.refs_0_.refs_9_), custom_call_target="tpu_custom_call" | custom-call | flops 3758096384 | bytes 7864320 | tf_op jit(solution)/shard_map/cond/branch_1_fun/pallas_call | solution.py:571
  126.4 2.5 %branch_1_fun.21 = (bf16[2,448,256]{2,1,0:T(8,128)(2,1)S(1)}, bf16[448,1792]{1,0:T(8,128)(2,1)}, bf16[448,1792]{1,0:T(8,128)(2,1)}, bf16[448,1792]{1,0:T(8,128)(...) custom-call(f32[2,2,448,256]{3,2,1,0:T(8,128)S(1)} %get-tuple-elemen, ...), custom_call_target="tpu_custom_call", output_to_operand_aliasing={{1}: (9, {}), {2}: (10, {}), {3}: (11, {}), {4}: (12, {}), ... | custom-call | bytes 6881280 | tf_op jit(solution)/shard_map/cond/branch_1_fun/pallas_call | solution.py:643
  129.7 2.9 %branch_1_fun.22.refs_0_ = f32[2,2,448,256]{3,2,1,0:T(8,128)S(1)} custom-call(bf16[2,448,1536]{2,1,0:T(8,128)(2,1)S(1)} %get-tuple-element.132.pair_in.refs_0_, bf16[2,448,512]{2,1,0:T(8,128)(2,1)S(1)} %get-tuple-element.138.refs_1_, bf16[2,2048,1792]{2,1,0:T(8,128)(2,1)S(1)} %copy-done.3, bf16[2,448,256]{2,1,0:T(8,128)(2,1)S(1)} %get-tuple-element.155.refs_3_.refs_9_), custom_call_target="tpu_custom_call" | custom-call | flops 3758096384 | bytes 7864320 | tf_op jit(solution)/shard_map/cond/branch_1_fun/pallas_call | solution.py:410
  132.6 2.4 %collective-permute-done.18.refs_2_ = bf16[2,448,256]{2,1,0:T(8,128)(2,1)S(1)} collective-permute-done((bf16[2,448,256]{2,1,0:T(8,128)(2,1)S(1)}, bf16[2,448,256]{2,1,0:T(8,128)(2,1)S(1)}, u32[]{:S(2)}, u32[]{:S(2)}) %collective-permute-start.18) | collective-permute-done | bytes 458784 | tf_op jit(solution)/shard_map/cond/branch_1_fun/ppermute | solution.py:45
  134.9 2.7 %branch_1_fun.23 = (bf16[2,448,256]{2,1,0:T(8,128)(2,1)S(1)}, bf16[448,1792]{1,0:T(8,128)(2,1)}, bf16[448,1792]{1,0:T(8,128)(2,1)}, bf16[448,1792]{1,0:T(8,128)(...) custom-call(f32[2,2,448,256]{3,2,1,0:T(8,128)S(1)} %branch_1_fun.22., ...), custom_call_target="tpu_custom_call", output_to_operand_aliasing={{1}: (11, {}), {2}: (12, {}), {3}: (13, {}), {4}: (14, {}),... | custom-call | bytes 6881280 | tf_op jit(solution)/shard_map/cond/branch_1_fun/pallas_call | solution.py:643
  139.0 3.3 %branch_1_fun.25 = (bf16[2,448,256]{2,1,0:T(8,128)(2,1)S(1)}, bf16[2,448,128]{2,1,0:T(8,128)(2,1)S(1)}, bf16[2,448,128]{2,1,0:T(8,128)(2,1)S(1)}) custom-call(bf16[2,448,2048]{2,1,0:T(8,128)(2,1)S(1)} %get-tuple-element.136.pair, bf16[2,2048,1792]{2,1,0:T(8,128)(2,1)S(1)} %copy-done.3, bf16[2,448,256]{2,1,0:T(8,128)(2,1)S(1)} %get-tuple-element.164.refs_3_.refs_0_.refs_9_), custom_call_target="tpu_custom_call" | custom-call | flops 3758096384 | bytes 7864320 | tf_op jit(solution)/shard_map/cond/branch_1_fun/pallas_call | solution.py:571
  142.3 2.5 %collective-permute-done.20.refs_2_ = bf16[2,448,256]{2,1,0:T(8,128)(2,1)S(1)} collective-permute-done((bf16[2,448,256]{2,1,0:T(8,128)(2,1)S(1)}, bf16[2,448,256]{2,1,0:T(8,128)(2,1)S(1)}, u32[]{:S(2)}, u32[]{:S(2)}) %collective-permute-start.20) | collective-permute-done | bytes 458784 | tf_op jit(solution)/shard_map/cond/branch_1_fun/ppermute | solution.py:45
  144.8 2.7 %branch_1_fun.26 = (bf16[2,448,256]{2,1,0:T(8,128)(2,1)S(1)}, bf16[448,1792]{1,0:T(8,128)(2,1)}, bf16[448,1792]{1,0:T(8,128)(2,1)}, bf16[448,1792]{1,0:T(8,128)(...) custom-call(f32[2,2,448,256]{3,2,1,0:T(8,128)S(1)} %branch_1_fun.22., ...), custom_call_target="tpu_custom_call", output_to_operand_aliasing={{1}: (11, {}), {2}: (12, {}), {3}: (13, {}), {4}: (14, {}),... | custom-call | bytes 6881280 | tf_op jit(solution)/shard_map/cond/branch_1_fun/pallas_call | solution.py:643
  148.8 4.3 %branch_1_fun.24.refs_0_ = f32[3,2,448,256]{3,2,1,0:T(8,128)S(1)} custom-call(bf16[2,448,1536]{2,1,0:T(8,128)(2,1)S(1)} %get-tuple-element.132.pair_in.refs_0_, bf16[2,448,512]{2,1,0:T(8,128)(2,1)S(1)} %get-tuple-element.138.refs_1_, bf16[2,2048,1792]{2,1,0:T(8,128)(2,1)S(1)} %copy-done.3, bf16[2,448,256]{2,1,0:T(8,128)(2,1)S(1)} %get-tuple-element.164.refs_3_.refs_0_.refs_9_), custom_call_target="tpu_custom_call" | custom-call | flops 5637144576 | bytes 9961472 | tf_op jit(solution)/shard_map/cond/branch_1_fun/pallas_call | solution.py:410
  154.6 2.7 %branch_1_fun.27 = (bf16[2,448,256]{2,1,0:T(8,128)(2,1)S(1)}, bf16[448,1792]{1,0:T(8,128)(2,1)}, bf16[448,1792]{1,0:T(8,128)(2,1)}, bf16[448,1792]{1,0:T(8,128)(...) custom-call(f32[3,2,448,256]{3,2,1,0:T(8,128)S(1)} %branch_1_fun.24., ...), custom_call_target="tpu_custom_call", output_to_operand_aliasing={{1}: (11, {}), {2}: (12, {}), {3}: (13, {}), {4}: (14, {}),... | custom-call | bytes 6881280 | tf_op jit(solution)/shard_map/cond/branch_1_fun/pallas_call | solution.py:643
  158.6 5.8 %collective-permute-done.22.refs_2_ = bf16[2,448,256]{2,1,0:T(8,128)(2,1)S(1)} collective-permute-done((bf16[2,448,256]{2,1,0:T(8,128)(2,1)S(1)}, bf16[2,448,256]{2,1,0:T(8,128)(2,1)S(1)}, u32[]{:S(2)}, u32[]{:S(2)}) %collective-permute-start.22) | collective-permute-done | bytes 458784 | tf_op jit(solution)/shard_map/cond/branch_1_fun/ppermute | solution.py:45
  164.4 2.7 %branch_1_fun.28 = (bf16[2,448,256]{2,1,0:T(8,128)(2,1)S(1)}, bf16[448,1792]{1,0:T(8,128)(2,1)}, bf16[448,1792]{1,0:T(8,128)(2,1)}, bf16[448,1792]{1,0:T(8,128)(...) custom-call(f32[3,2,448,256]{3,2,1,0:T(8,128)S(1)} %branch_1_fun.24., ...), custom_call_target="tpu_custom_call", output_to_operand_aliasing={{1}: (11, {}), {2}: (12, {}), {3}: (13, {}), {4}: (14, {}),... | custom-call | bytes 6881280 | tf_op jit(solution)/shard_map/cond/branch_1_fun/pallas_call | solution.py:643
  171.2 3.0 %collective-permute-done.26.refs_2_ = bf16[2,448,128]{2,1,0:T(8,128)(2,1)S(1)} collective-permute-done((bf16[2,448,128]{2,1,0:T(8,128)(2,1)S(1)}, bf16[2,448,128]{2,1,0:T(8,128)(2,1)S(1)}, u32[]{:S(2)}, u32[]{:S(2)}) %collective-permute-start.26) | collective-permute-done | bytes 229408 | tf_op jit(solution)/shard_map/cond/branch_1_fun/ppermute | solution.py:45
  (84 shorter events, 40.4 us)
Async XLA Ops:
  3.6 80.4 %collective-permute-start.32 = (bf16[2,448,1792]{2,1,0:T(8,128)(2,1)}, bf16[2,448,1792]{2,1,0:T(8,128)(2,1)S(1)}, u32[]{:S(2)}, u32[]{:S(2)}) collective-permute-start(bf16[2,448,1792]{2,1,0:T(8,128)(2,1)} %shard_map.136), channel_id=1, source_target_pairs={{0,1},{1,0},{2,3},{3,2},{4,5},{5,4},{6,7},{7,6},{8,9},{9,8},{10,11... | collective-permute-start | bytes 9633800 | tf_op jit(solution)/shard_map/ppermute | solution.py:45
  6.5 14.3 %collective-permute-start.39 = (bf16[2,64,1792]{2,1,0:T(8,128)(2,1)S(1)}, bf16[2,64,1792]{2,1,0:T(8,128)(2,1)S(1)}, u32[]{:S(2)}, u32[]{:S(2)}) collective-permute-start(bf16[2,64,1792]{2,1,0:T(8,128)(2,1)S(1)} %get-tuple-element.249.refs_0_), channel_id=1, source_target_pairs={{0,8},{1,9},{2,10},{3,11},{4,12},{5,13},{6,14},{7,15},{8,16},{9,17... | collective-permute-start | bytes 1376264 | tf_op jit(solution)/shard_map/ppermute | solution.py:45
  8.4 12.5 %collective-permute-start.40 = (bf16[2,64,1792]{2,1,0:T(8,128)(2,1)S(1)}, bf16[2,64,1792]{2,1,0:T(8,128)(2,1)S(1)}, u32[]{:S(2)}, u32[]{:S(2)}) collective-permute-start(bf16[2,64,1792]{2,1,0:T(8,128)(2,1)S(1)} %get-tuple-element.249.refs_0_), channel_id=1, source_target_pairs={{0,24},{1,25},{2,26},{3,27},{4,28},{5,29},{6,30},{7,31},{8,0},{9,1... | collective-permute-start | bytes 1376264 | tf_op jit(solution)/shard_map/ppermute | solution.py:45
  10.6 13.6 %collective-permute-start.33 = (bf16[2,64,1792]{2,1,0:T(8,128)(2,1)S(1)}, bf16[2,64,1792]{2,1,0:T(8,128)(2,1)S(1)}, u32[]{:S(2)}, u32[]{:S(2)}) collective-permute-start(bf16[2,64,1792]{2,1,0:T(8,128)(2,1)S(1)} %get-tuple-element.248.refs_0_), channel_id=1, source_target_pairs={{0,4},{1,5},{2,6},{3,7},{4,0},{5,1},{6,2},{7,3},{8,12},{9,13},{10,... | collective-permute-start | bytes 1376264 | tf_op jit(solution)/shard_map/ppermute | solution.py:45
  13.7 12.8 %collective-permute-start.34 = (bf16[2,64,1792]{2,1,0:T(8,128)(2,1)S(1)}, bf16[2,64,1792]{2,1,0:T(8,128)(2,1)S(1)}, u32[]{:S(2)}, u32[]{:S(2)}) collective-permute-start(bf16[2,64,1792]{2,1,0:T(8,128)(2,1)S(1)} %get-tuple-element.248.refs_0_), channel_id=1, source_target_pairs={{0,3},{1,2},{2,1},{3,0},{4,7},{5,6},{6,5},{7,4},{8,11},{9,10},{10,... | collective-permute-start | bytes 1376264 | tf_op jit(solution)/shard_map/ppermute | solution.py:45
  20.8 8.8 %collective-permute-start.41 = (bf16[2,32,1792]{2,1,0:T(8,128)(2,1)S(1)}, bf16[2,32,1792]{2,1,0:T(8,128)(2,1)S(1)}, u32[]{:S(2)}, u32[]{:S(2)}) collective-permute-start(bf16[2,32,1792]{2,1,0:T(8,128)(2,1)S(1)} %slice.18), channel_id=1, source_target_pairs={{0,8},{1,9},{2,10},{3,11},{4,12},{5,13},{6,14},{7,15},{8,16},{9,17... | collective-permute-start | bytes 688136 | tf_op jit(solution)/shard_map/ppermute | solution.py:45
  20.9 8.7 %collective-permute-start.42 = (bf16[2,32,1792]{2,1,0:T(8,128)(2,1)S(1)}, bf16[2,32,1792]{2,1,0:T(8,128)(2,1)S(1)}, u32[]{:S(2)}, u32[]{:S(2)}) collective-permute-start(bf16[2,32,1792]{2,1,0:T(8,128)(2,1)S(1)} %slice.19), channel_id=1, source_target_pairs={{0,24},{1,25},{2,26},{3,27},{4,28},{5,29},{6,30},{7,31},{8,0},{9,1... | collective-permute-start | bytes 688136 | tf_op jit(solution)/shard_map/ppermute | solution.py:45
  24.2 11.0 %collective-permute-start.35 = (bf16[2,32,1792]{2,1,0:T(8,128)(2,1)S(1)}, bf16[2,32,1792]{2,1,0:T(8,128)(2,1)S(1)}, u32[]{:S(2)}, u32[]{:S(2)}) collective-permute-start(bf16[2,32,1792]{2,1,0:T(8,128)(2,1)S(1)} %slice.16), channel_id=1, source_target_pairs={{0,3},{1,2},{2,1},{3,0},{4,7},{5,6},{6,5},{7,4},{8,11},{9,10},{10,... | collective-permute-start | bytes 688136 | tf_op jit(solution)/shard_map/ppermute | solution.py:45
  26.5 8.7 %collective-permute-start.36 = (bf16[2,32,1792]{2,1,0:T(8,128)(2,1)S(1)}, bf16[2,32,1792]{2,1,0:T(8,128)(2,1)S(1)}, u32[]{:S(2)}, u32[]{:S(2)}) collective-permute-start(bf16[2,32,1792]{2,1,0:T(8,128)(2,1)S(1)} %slice.17), channel_id=1, source_target_pairs={{0,4},{1,5},{2,6},{3,7},{4,0},{5,1},{6,2},{7,3},{8,12},{9,13},{10,... | collective-permute-start | bytes 688136 | tf_op jit(solution)/shard_map/ppermute | solution.py:45
  31.1 42.5 %collective-permute-start.45 = (bf16[2,256,1792]{2,1,0:T(8,128)(2,1)}, bf16[2,256,1792]{2,1,0:T(8,128)(2,1)}, u32[]{:S(2)}, u32[]{:S(2)}) collective-permute-start(bf16[2,256,1792]{2,1,0:T(8,128)(2,1)} %shard_map.139.refs_3_.refs_8_), channel_id=1, source_target_pairs={{0,4},{1,5},{2,6},{3,7},{4,0},{5,1},{6,2},{7,3},{8,12},{9,13},{10,... | collective-permute-start | bytes 5505032 | tf_op jit(solution)/shard_map/ppermute | solution.py:45
  33.0 41.2 %collective-permute-start.46 = (bf16[2,256,1792]{2,1,0:T(8,128)(2,1)}, bf16[2,256,1792]{2,1,0:T(8,128)(2,1)}, u32[]{:S(2)}, u32[]{:S(2)}) collective-permute-start(bf16[2,256,1792]{2,1,0:T(8,128)(2,1)} %shard_map.139.refs_3_.refs_8_), channel_id=1, source_target_pairs={{0,3},{1,2},{2,1},{3,0},{4,7},{5,6},{6,5},{7,4},{8,11},{9,10},{10,... | collective-permute-start | bytes 5505032 | tf_op jit(solution)/shard_map/ppermute | solution.py:45
  36.6 41.4 %collective-permute-start.37 = (bf16[2,256,1792]{2,1,0:T(8,128)(2,1)}, bf16[2,256,1792]{2,1,0:T(8,128)(2,1)}, u32[]{:S(2)}, u32[]{:S(2)}) collective-permute-start(bf16[2,256,1792]{2,1,0:T(8,128)(2,1)} %shard_map.138.refs_2_.refs_7_), channel_id=1, source_target_pairs={{0,8},{1,9},{2,10},{3,11},{4,12},{5,13},{6,14},{7,15},{8,16},{9,17... | collective-permute-start | bytes 5505032 | tf_op jit(solution)/shard_map/ppermute | solution.py:45
  36.7 41.3 %collective-permute-start.38 = (bf16[2,256,1792]{2,1,0:T(8,128)(2,1)}, bf16[2,256,1792]{2,1,0:T(8,128)(2,1)}, u32[]{:S(2)}, u32[]{:S(2)}) collective-permute-start(bf16[2,256,1792]{2,1,0:T(8,128)(2,1)} %shard_map.138.refs_2_.refs_7_), channel_id=1, source_target_pairs={{0,24},{1,25},{2,26},{3,27},{4,28},{5,29},{6,30},{7,31},{8,0},{9,1... | collective-permute-start | bytes 5505032 | tf_op jit(solution)/shard_map/ppermute | solution.py:45
  75.8 24.2 %collective-permute-start.48 = (bf16[2,128,1792]{2,1,0:T(8,128)(2,1)S(1)}, bf16[2,128,1792]{2,1,0:T(8,128)(2,1)S(1)}, u32[]{:S(2)}, u32[]{:S(2)}) collective-permute-start(bf16[2,128,1792]{2,1,0:T(8,128)(2,1)S(1)} %get-tuple-element.254.refs_13_), channel_id=1, source_target_pairs={{0,3},{1,2},{2,1},{3,0},{4,7},{5,6},{6,5},{7,4},{8,11},{9,10},{10,... | collective-permute-start | bytes 2752520 | tf_op jit(solution)/shard_map/ppermute | solution.py:45
  79.5 20.9 %collective-permute-start.43 = (bf16[2,128,1792]{2,1,0:T(8,128)(2,1)S(1)}, bf16[2,128,1792]{2,1,0:T(8,128)(2,1)S(1)}, u32[]{:S(2)}, u32[]{:S(2)}) collective-permute-start(bf16[2,128,1792]{2,1,0:T(8,128)(2,1)S(1)} %get-tuple-element.251.refs_12_), channel_id=1, source_target_pairs={{0,8},{1,9},{2,10},{3,11},{4,12},{5,13},{6,14},{7,15},{8,16},{9,17... | collective-permute-start | bytes 2752520 | tf_op jit(solution)/shard_map/ppermute | solution.py:45
  80.0 20.8 %collective-permute-start.47 = (bf16[2,128,1792]{2,1,0:T(8,128)(2,1)S(1)}, bf16[2,128,1792]{2,1,0:T(8,128)(2,1)S(1)}, u32[]{:S(2)}, u32[]{:S(2)}) collective-permute-start(bf16[2,128,1792]{2,1,0:T(8,128)(2,1)S(1)} %get-tuple-element.253), channel_id=1, source_target_pairs={{0,4},{1,5},{2,6},{3,7},{4,0},{5,1},{6,2},{7,3},{8,12},{9,13},{10,... | collective-permute-start | bytes 2752520 | tf_op jit(solution)/shard_map/ppermute | solution.py:45
  80.9 20.0 %collective-permute-start.44 = (bf16[2,128,1792]{2,1,0:T(8,128)(2,1)S(1)}, bf16[2,128,1792]{2,1,0:T(8,128)(2,1)S(1)}, u32[]{:S(2)}, u32[]{:S(2)}) collective-permute-start(bf16[2,128,1792]{2,1,0:T(8,128)(2,1)S(1)} %get-tuple-element.252), channel_id=1, source_target_pairs={{0,24},{1,25},{2,26},{3,27},{4,28},{5,29},{6,30},{7,31},{8,0},{9,1... | collective-permute-start | bytes 2752520 | tf_op jit(solution)/shard_map/ppermute | solution.py:45
  105.5 13.5 %collective-permute-start.17 = (bf16[2,448,256]{2,1,0:T(8,128)(2,1)S(1)}, bf16[2,448,256]{2,1,0:T(8,128)(2,1)S(1)}, u32[]{:S(2)}, u32[]{:S(2)}) collective-permute-start(bf16[2,448,256]{2,1,0:T(8,128)(2,1)S(1)} %get-tuple-element.145), channel_id=1, source_target_pairs={{0,1},{1,0},{2,3},{3,2},{4,5},{5,4},{6,7},{7,6},{8,9},{9,8},{10,11... | collective-permute-start | bytes 1376264 | tf_op jit(solution)/shard_map/cond/branch_1_fun/ppermute | solution.py:45
  110.7 15.7 %collective-permute-start.16 = (bf16[2,448,256]{2,1,0:T(8,128)(2,1)S(1)}, bf16[2,448,256]{2,1,0:T(8,128)(2,1)S(1)}, u32[]{:S(2)}, u32[]{:S(2)}) collective-permute-start(bf16[2,448,256]{2,1,0:T(8,128)(2,1)S(1)} %get-tuple-element.137.refs_0_), channel_id=1, source_target_pairs={{0,1},{1,0},{2,3},{3,2},{4,5},{5,4},{6,7},{7,6},{8,9},{9,8},{10,11... | collective-permute-start | bytes 1376264 | tf_op jit(solution)/shard_map/cond/branch_1_fun/ppermute | solution.py:45
  121.5 11.0 %collective-permute-start.19 = (bf16[2,448,256]{2,1,0:T(8,128)(2,1)S(1)}, bf16[2,448,256]{2,1,0:T(8,128)(2,1)S(1)}, u32[]{:S(2)}, u32[]{:S(2)}) collective-permute-start(bf16[2,448,256]{2,1,0:T(8,128)(2,1)S(1)} %get-tuple-element.153.refs_0_.refs_9_), channel_id=1, source_target_pairs={{0,32},{32,64},{64,96},{96,0},{1,33},{33,65},{65,97},{97,1},{2,34}... | collective-permute-start | bytes 1376264 | tf_op jit(solution)/shard_map/cond/branch_1_fun/ppermute | solution.py:744
  121.5 13.4 %collective-permute-start.18 = (bf16[2,448,256]{2,1,0:T(8,128)(2,1)S(1)}, bf16[2,448,256]{2,1,0:T(8,128)(2,1)S(1)}, u32[]{:S(2)}, u32[]{:S(2)}) collective-permute-start(bf16[2,448,256]{2,1,0:T(8,128)(2,1)S(1)} %get-tuple-element.156), channel_id=1, source_target_pairs={{0,1},{1,0},{2,3},{3,2},{4,5},{5,4},{6,7},{7,6},{8,9},{9,8},{10,11... | collective-permute-start | bytes 1376264 | tf_op jit(solution)/shard_map/cond/branch_1_fun/ppermute | solution.py:45
  128.9 15.9 %collective-permute-start.20 = (bf16[2,448,256]{2,1,0:T(8,128)(2,1)S(1)}, bf16[2,448,256]{2,1,0:T(8,128)(2,1)S(1)}, u32[]{:S(2)}, u32[]{:S(2)}) collective-permute-start(bf16[2,448,256]{2,1,0:T(8,128)(2,1)S(1)} %get-tuple-element.165), channel_id=1, source_target_pairs={{0,1},{1,0},{2,3},{3,2},{4,5},{5,4},{6,7},{7,6},{8,9},{9,8},{10,11... | collective-permute-start | bytes 1376264 | tf_op jit(solution)/shard_map/cond/branch_1_fun/ppermute | solution.py:45
  129.5 15.3 %collective-permute-start.21 = (bf16[2,448,256]{2,1,0:T(8,128)(2,1)S(1)}, bf16[2,448,256]{2,1,0:T(8,128)(2,1)S(1)}, u32[]{:S(2)}, u32[]{:S(2)}) collective-permute-start(bf16[2,448,256]{2,1,0:T(8,128)(2,1)S(1)} %get-tuple-element.155.refs_3_.refs_9_), channel_id=1, source_target_pairs={{0,32},{32,64},{64,96},{96,0},{1,33},{33,65},{65,97},{97,1},{2,34}... | collective-permute-start | bytes 1376264 | tf_op jit(solution)/shard_map/cond/branch_1_fun/ppermute | solution.py:744
  137.6 17.0 %collective-permute-start.24 = (bf16[2,448,256]{2,1,0:T(8,128)(2,1)S(1)}, bf16[2,448,256]{2,1,0:T(8,128)(2,1)S(1)}, u32[]{:S(2)}, u32[]{:S(2)}) collective-permute-start(bf16[2,448,256]{2,1,0:T(8,128)(2,1)S(1)} %get-tuple-element.175), channel_id=1, source_target_pairs={{0,1},{1,0},{2,3},{3,2},{4,5},{5,4},{6,7},{7,6},{8,9},{9,8},{10,11... | collective-permute-start | bytes 1376264 | tf_op jit(solution)/shard_map/cond/branch_1_fun/ppermute | solution.py:45
  139.0 15.6 %collective-permute-start.25 = (bf16[2,448,256]{2,1,0:T(8,128)(2,1)S(1)}, bf16[2,448,256]{2,1,0:T(8,128)(2,1)S(1)}, u32[]{:S(2)}, u32[]{:S(2)}) collective-permute-start(bf16[2,448,256]{2,1,0:T(8,128)(2,1)S(1)} %get-tuple-element.164.refs_3_.refs_0_.refs_9_), channel_id=1, source_target_pairs={{0,32},{32,64},{64,96},{96,0},{1,33},{33,65},{65,97},{97,1},{2,34}... | collective-permute-start | bytes 1376264 | tf_op jit(solution)/shard_map/cond/branch_1_fun/ppermute | solution.py:744
  147.4 17.0 %collective-permute-start.22 = (bf16[2,448,256]{2,1,0:T(8,128)(2,1)S(1)}, bf16[2,448,256]{2,1,0:T(8,128)(2,1)S(1)}, u32[]{:S(2)}, u32[]{:S(2)}) collective-permute-start(bf16[2,448,256]{2,1,0:T(8,128)(2,1)S(1)} %get-tuple-element.173), channel_id=1, source_target_pairs={{0,1},{1,0},{2,3},{3,2},{4,5},{5,4},{6,7},{7,6},{8,9},{9,8},{10,11... | collective-permute-start | bytes 1376264 | tf_op jit(solution)/shard_map/cond/branch_1_fun/ppermute | solution.py:45
  148.8 15.6 %collective-permute-start.23 = (bf16[2,448,256]{2,1,0:T(8,128)(2,1)S(1)}, bf16[2,448,256]{2,1,0:T(8,128)(2,1)S(1)}, u32[]{:S(2)}, u32[]{:S(2)}) collective-permute-start(bf16[2,448,256]{2,1,0:T(8,128)(2,1)S(1)} %get-tuple-element.174.refs_9_), channel_id=1, source_target_pairs={{0,32},{32,64},{64,96},{96,0},{1,33},{33,65},{65,97},{97,1},{2,34}... | collective-permute-start | bytes 1376264 | tf_op jit(solution)/shard_map/cond/branch_1_fun/ppermute | solution.py:744
  157.3 11.8 %collective-permute-start.28 = (bf16[2,448,256]{2,1,0:T(8,128)(2,1)S(1)}, bf16[2,448,256]{2,1,0:T(8,128)(2,1)S(1)}, u32[]{:S(2)}, u32[]{:S(2)}) collective-permute-start(bf16[2,448,256]{2,1,0:T(8,128)(2,1)S(1)} %get-tuple-element.192.refs_9_), channel_id=1, source_target_pairs={{0,32},{32,64},{64,96},{96,0},{1,33},{33,65},{65,97},{97,1},{2,34}... | collective-permute-start | bytes 1376264 | tf_op jit(solution)/shard_map/cond/branch_1_fun/ppermute | solution.py:744
  157.3 11.8 %collective-permute-start.27 = (bf16[2,448,128]{2,1,0:T(8,128)(2,1)S(1)}, bf16[2,448,128]{2,1,0:T(8,128)(2,1)S(1)}, u32[]{:S(2)}, u32[]{:S(2)}) collective-permute-start(bf16[2,448,128]{2,1,0:T(8,128)(2,1)S(1)} %get-tuple-element.191), channel_id=1, source_target_pairs={{0,1},{1,0},{2,3},{3,2},{4,5},{5,4},{6,7},{7,6},{8,9},{9,8},{10,11... | collective-permute-start | bytes 688136 | tf_op jit(solution)/shard_map/cond/branch_1_fun/ppermute | solution.py:45
  167.1 7.0 %collective-permute-start.26 = (bf16[2,448,128]{2,1,0:T(8,128)(2,1)S(1)}, bf16[2,448,128]{2,1,0:T(8,128)(2,1)S(1)}, u32[]{:S(2)}, u32[]{:S(2)}) collective-permute-start(bf16[2,448,128]{2,1,0:T(8,128)(2,1)S(1)} %get-tuple-element.190), channel_id=1, source_target_pairs={{0,1},{1,0},{2,3},{3,2},{4,5},{5,4},{6,7},{7,6},{8,9},{9,8},{10,11... | collective-permute-start | bytes 688136 | tf_op jit(solution)/shard_map/cond/branch_1_fun/ppermute | solution.py:45
  168.5 7.9 %collective-permute-start.31 = (bf16[2,448,256]{2,1,0:T(8,128)(2,1)S(1)}, bf16[2,448,256]{2,1,0:T(8,128)(2,1)S(1)}, u32[]{:S(2)}, u32[]{:S(2)}) collective-permute-start(bf16[2,448,256]{2,1,0:T(8,128)(2,1)S(1)} %get-tuple-element.207.own), channel_id=1, source_target_pairs={{0,32},{32,64},{64,96},{96,0},{1,33},{33,65},{65,97},{97,1},{2,34}... | collective-permute-start | bytes 1376264 | tf_op jit(solution)/shard_map/cond/branch_1_fun/ppermute | solution.py:744
  171.2 7.7 %collective-permute-start.30 = (bf16[2,448,128]{2,1,0:T(8,128)(2,1)S(1)}, bf16[2,448,128]{2,1,0:T(8,128)(2,1)S(1)}, u32[]{:S(2)}, u32[]{:S(2)}) collective-permute-start(bf16[2,448,128]{2,1,0:T(8,128)(2,1)S(1)} %get-tuple-element.206.own), channel_id=1, source_target_pairs={{0,32},{32,64},{64,96},{96,0},{1,33},{33,65},{65,97},{97,1},{2,34}... | collective-permute-start | bytes 688136 | tf_op jit(solution)/shard_map/cond/branch_1_fun/ppermute | solution.py:744
  (10 other events, 55.8 us)
